TPU v7x, 128 devices: a whole 4x4x4 slice. The times are simulated.
128 devices in a mesh: row: 8 (over y, core), col: 16 (over x, z).
Axes of the slice: x: 4, y: 4, z: 4, core: 2. Of those that a mesh axis runs over, the one named last changes fastest.
Arguments:
- atoms: bfloat16 [16384, 128], P(('row', 'col')), may hold values from -6 to 6
- atom_pair: bfloat16 [512, 16, 32, 128], P(('row', 'col')), may hold values from -6 to 6
- atom_token: int32 [16384], P(('row', 'col')), may hold values from 0 to 2047, as said below
- single: bfloat16 [2048, 768], P('row'), may hold values from -6 to 6
- pair: bfloat16 [2048, 2048, 128], P('row', 'col'), may hold values from -6 to 6
- atom_w: bfloat16 [128, 4, 128], replicated, may hold values from -0.5 to 0.5
- atom_pair_w: bfloat16 [16, 4], replicated, may hold values from -24 to 24
- atom_wo: bfloat16 [128, 128], replicated, may hold values from -0.5 to 0.5
- agg_w: bfloat16 [128, 768], replicated, may hold values from -0.5 to 0.5
- trans_in: bfloat16 [128, 2, 256], replicated, may hold values from -0.5 to 0.5
- trans_out: bfloat16 [256, 128], replicated, may hold values from -0.375 to 0.375
- bias_w: bfloat16 [128, 16], replicated, may hold values from -6 to 6
- token_w: bfloat16 [768, 4, 768], P(None, None, 'col'), may hold values from -0.21875 to 0.21875
- token_wo: bfloat16 [768, 768], P('col'), may hold values from -0.21875 to 0.21875
- back_w: bfloat16 [768, 128], P('col'), may hold values from -0.21875 to 0.21875
Outputs:
- single_out: bfloat16 [2048, 768], P('row', 'col')
- atoms_out: bfloat16 [16384, 128], P(('row', 'col'))
Inputs may be any that keep to these rules, and one draw needn't show every extreme that they name: `atom_token`: atoms are in token order; the 2048 atoms of block b (b from 0) belong to tokens b * 256 to (b + 1) * 256 - 1; every token has 1 to 15 atoms, and in every block some token has exactly 15.
All inputs are finite; a program needn't handle non-finite values.
Results may differ from a plain program's by a relative error of at most 0.024.
The roundings to bfloat16 on the way count: a program that leaves them out, or rounds other values in their place, can miss the bound.
Values may be sent and summed in bfloat16 or wider, within the bound.
No kernel may reach another device: no remote copies, remote signals or barrier semaphores. Data moves between devices by JAX's collectives and lax.ppermute only.
A program may use at most 64 MiB of HBM per device.

v0:
```python
import math

import jax
import jax.numpy as jnp
from jax import lax
from jax.sharding import PartitionSpec as P

HEADS = 16
HEAD = 48
CA = 128
ATOM_HEADS = 4
ATOM_HEAD = 32
QW = 32
KW = 128


epsilon = 1e-05
masked_score = -1e30


def extended_2(value, sides, width):
    for axis, dim in sides:
        size, length = (lax.axis_size(axis), value.shape[dim])
        up = [(i, (i + 1) % size) for i in range(size - 1)]
        down = [(j, i) for i, j in up]
        last = lax.slice_in_dim(value, length - width, length, axis=dim)
        initial = lax.slice_in_dim(value, 0, width, axis=dim)
        before = lax.ppermute(last, axis, up)
        after = lax.ppermute(initial, axis, down)
        value = jnp.concatenate([before, value, after], axis=dim)
    return value


def layer_norm(values):
    centred = values - jnp.mean(values, axis=-1, keepdims=True)
    spread = jnp.mean(centred * centred, axis=-1, keepdims=True)
    return centred * lax.rsqrt(spread + epsilon)


def rounded(values):
    return lax.optimization_barrier(values.astype(jnp.bfloat16))


def softmax_rows(scores):
    highest = jnp.max(scores, axis=-1, keepdims=True)
    raised = jnp.exp(scores - highest)
    return (raised / jnp.sum(raised, axis=-1, keepdims=True)).astype(jnp.bfloat16)


def pair_block(tile, trans_in, trans_out, bias_w):
    normed = layer_norm(tile.astype(jnp.float32)).astype(jnp.bfloat16)
    both = jnp.einsum("ijc,cmf->ijmf", normed, trans_in, preferred_element_type=jnp.float32)
    hidden = (jax.nn.silu(both[:, :, 0, :]) * both[:, :, 1, :]).astype(jnp.bfloat16)
    update = jnp.einsum("ijf,fc->ijc", hidden, trans_out, preferred_element_type=jnp.float32)
    renewed = rounded(tile.astype(jnp.float32) + update)
    renormed = layer_norm(renewed.astype(jnp.float32)).astype(jnp.bfloat16)
    return jnp.einsum("ijc,ch->hij", renormed, bias_w, preferred_element_type=jnp.float32).astype(
        jnp.bfloat16
    )


def body(
    atoms,
    atom_pair,
    atom_token,
    single,
    pair,
    atom_w,
    atom_pair_w,
    atom_wo,
    agg_w,
    trans_in,
    trans_out,
    bias_w,
    token_w,
    token_wo,
    back_w,
):
    atom_count = atoms.shape[0]
    windows = atom_count // QW
    rim = (KW - QW) // 2
    atom_norm = layer_norm(atoms.astype(jnp.float32)).astype(jnp.bfloat16)
    projected = jnp.einsum(
        "ac,cmd->amd", atom_norm, atom_w, preferred_element_type=jnp.float32
    ).astype(jnp.bfloat16)
    extended = extended_2(atoms, ((("row", "col"), 0),), rim)
    ext_norm = layer_norm(extended.astype(jnp.float32)).astype(jnp.bfloat16)
    key_value = jnp.einsum(
        "ac,cmd->amd", ext_norm, atom_w[:, 1:3, :], preferred_element_type=jnp.float32
    ).astype(jnp.bfloat16)
    device = lax.axis_index(("row", "col"))
    all_atoms = atom_count * lax.axis_size(("row", "col"))
    positions = device * atom_count - rim + jnp.arange(atom_count + 2 * rim)
    inside = (positions >= 0) & (positions < all_atoms)
    window_keys = jnp.stack(
        [
            lax.slice_in_dim(key_value, window * QW, window * QW + KW, axis=0)
            for window in range(windows)
        ]
    )
    window_mask = jnp.stack(
        [
            lax.slice_in_dim(inside, window * QW, window * QW + KW, axis=0)
            for window in range(windows)
        ]
    )
    queries = projected[:, 0, :].reshape(windows, QW, ATOM_HEADS, ATOM_HEAD)
    key_part = window_keys[:, :, 0, :].reshape(windows, KW, ATOM_HEADS, ATOM_HEAD)
    value_part = window_keys[:, :, 1, :].reshape(windows, KW, ATOM_HEADS, ATOM_HEAD)
    atom_bias = jnp.einsum(
        "wcij,ch->whij", atom_pair, atom_pair_w, preferred_element_type=jnp.float32
    )
    scores = (
        jnp.einsum("wiha,wjha->whij", queries, key_part, preferred_element_type=jnp.float32)
        / math.sqrt(ATOM_HEAD)
        + atom_bias
    )
    scores = jnp.where(window_mask[:, None, None, :], scores, masked_score)
    weights = softmax_rows(scores)
    attended = jnp.einsum(
        "whij,wjha->wiha", weights, value_part, preferred_element_type=jnp.float32
    ).reshape(atom_count, CA)
    gated = (jax.nn.sigmoid(projected[:, 3, :].astype(jnp.float32)) * attended).astype(jnp.bfloat16)
    atoms_mid = rounded(
        atoms.astype(jnp.float32) + jnp.dot(gated, atom_wo, preferred_element_type=jnp.float32)
    )
    query_rows = single.shape[0]
    row_start = lax.axis_index("row") * query_rows
    within = atom_token - row_start
    onehot = (jnp.arange(query_rows)[:, None] == within[None, :]).astype(jnp.bfloat16)
    features = jax.nn.relu(jnp.dot(atoms_mid, agg_w, preferred_element_type=jnp.float32)).astype(
        jnp.bfloat16
    )
    token_part = jnp.dot(onehot, features, preferred_element_type=jnp.float32)
    count_part = jnp.sum(onehot.astype(jnp.float32), axis=1)
    token_sum, token_count = (
        lax.psum(token_part.astype(jnp.bfloat16), "col").astype(jnp.float32),
        lax.psum(count_part.astype(jnp.bfloat16), "col").astype(jnp.float32),
    )
    token_in = rounded(single.astype(jnp.float32) + token_sum / token_count[:, None])
    key_cols = pair.shape[1]
    blocks = pair.reshape(query_rows // 16, 16, key_cols, pair.shape[2])
    bias_blocks = lax.map(lambda tile: pair_block(tile, trans_in, trans_out, bias_w), blocks)
    pair_bias = jnp.moveaxis(bias_blocks, 1, 0).reshape(HEADS, query_rows, key_cols)
    token_norm = layer_norm(token_in.astype(jnp.float32)).astype(jnp.bfloat16)
    token_proj = jnp.einsum(
        "td,dme->tme", token_norm, token_w, preferred_element_type=jnp.float32
    ).astype(jnp.bfloat16)
    head_cols = token_w.shape[2]
    kv_rows = lax.all_gather(token_proj[:, 1:3, :], "row", axis=0, tiled=True)
    all_tokens = kv_rows.shape[0]
    bias_rows = lax.all_to_all(pair_bias, "col", split_axis=0, concat_axis=2, tiled=True)
    heads_here = head_cols // HEAD
    query_part = token_proj[:, 0, :].reshape(query_rows, heads_here, HEAD)
    token_keys = kv_rows[:, 0, :].reshape(all_tokens, heads_here, HEAD)
    token_values = kv_rows[:, 1, :].reshape(all_tokens, heads_here, HEAD)
    token_scores = jnp.einsum(
        "ihe,jhe->hij", query_part, token_keys, preferred_element_type=jnp.float32
    ) / math.sqrt(HEAD)
    token_weights = softmax_rows(token_scores + bias_rows.astype(jnp.float32))
    token_attn = jnp.einsum(
        "hij,jhe->ihe", token_weights, token_values, preferred_element_type=jnp.float32
    ).reshape(query_rows, head_cols)
    token_gated = (jax.nn.sigmoid(token_proj[:, 3, :].astype(jnp.float32)) * token_attn).astype(
        jnp.bfloat16
    )
    own_cols = token_wo.shape[0]
    own_input = lax.dynamic_slice_in_dim(token_in, lax.axis_index("col") * own_cols, own_cols, 1)
    projection = lax.psum_scatter(
        jnp.dot(token_gated, token_wo, preferred_element_type=jnp.float32).astype(jnp.bfloat16),
        "col",
        scatter_dimension=1,
        tiled=True,
    ).astype(jnp.float32)
    single_out = (own_input.astype(jnp.float32) + projection).astype(jnp.bfloat16)
    back_sum = lax.psum(
        jnp.dot(single_out, back_w, preferred_element_type=jnp.float32).astype(jnp.bfloat16), "col"
    )
    picked = jnp.einsum("ta,tc->ac", onehot, back_sum, preferred_element_type=jnp.float32)
    atoms_out = (atoms_mid.astype(jnp.float32) + picked).astype(jnp.bfloat16)
    return (single_out, atoms_out)


def solution(mesh):
    in_specs = (
        P(("row", "col"), None),
        P(("row", "col"), None, None, None),
        P(("row", "col")),
        P("row", None),
        P("row", "col", None),
        P(),
        P(),
        P(),
        P(),
        P(),
        P(),
        P(),
        P(None, None, "col"),
        P("col", None),
        P("col", None),
    )
    out_specs = (P("row", "col"), P(("row", "col"), None))
    return jax.shard_map(body, mesh=mesh, in_specs=in_specs, out_specs=out_specs, check_vma=False)
```

profile of v0, /device:TPU:0, one launch (start us, length us, event | category | flops | bytes accessed | tf_op | source)
XLA Modules:
  0.0 401.3 jit_solution(17905141887769892309)
XLA Ops:
  8.0 1.3 collective-permute-start.1
  9.3 4.5 %collective-permute-start = (bf16[48,128]{1,0:T(8,128)(2,1)S(1)}, bf16[48,128]{1,0:T(8,128)(2,1)S(1)}, u32[]{:S(2)}, u32[]{:S(2)}) collective-permute-start(bf16[48,128]{1,0:T(8,128)(2,1)S(1)} %get-tuple-element.85), channel_id=1, source_target_pairs={{0,1},{1,2},{2,3},{3,4},{4,5},{5,6},{6,7},{7,8},{8,9},{9,10},{10,1... | collective-permute-start | bytes 36872 | tf_op jit(solution)/shard_map/ppermute | solution.py:28
  26.2 135.3 %while.10 = (s32[]{:T(128)}, bf16[16,16,16,128]{3,1,2,0:T(8,128)(2,1)S(1)}, bf16[16,16,128,128]{3,2,1,0:T(8,128)(2,1)}, bf16[128,2,256]{2,0,1:T(8,128)(2,1)S(1)}...) while((s32[]{:T(128)}, bf16[16,16,16,128]{3,1,2,0:T(8,128)(2,1)S(1)}, ...), condition=%wide.region_16.17_spmd, body=%wide.region_11.16_spmd.sunk | while | flops 420253696 | bytes 12996713 | solution.py:143
  27.5 1.7 fusion.127
  29.2 2.0 fusion.128
  31.2 1.8 fusion.129
  36.0 1.7 fusion.127
  37.7 2.0 fusion.128
  39.7 1.8 fusion.129
  44.4 1.7 fusion.127
  46.1 2.0 fusion.128
  48.1 1.8 fusion.129
  51.6 1.3 convert_reduce_fusion.7
  52.9 1.7 fusion.127
  54.6 2.0 fusion.128
  56.6 1.8 fusion.129
  60.1 1.3 convert_reduce_fusion.7
  61.4 1.7 fusion.127
  63.1 2.0 fusion.128
  65.1 1.8 fusion.129
  69.8 1.7 fusion.127
  71.5 2.0 fusion.128
  73.5 1.8 fusion.129
  77.0 1.3 convert_reduce_fusion.7
  78.3 1.7 fusion.127
  80.0 2.0 fusion.128
  82.0 1.8 fusion.129
  86.7 1.7 fusion.127
  88.4 2.0 fusion.128
  90.4 1.8 fusion.129
  93.9 1.3 convert_reduce_fusion.7
  95.2 1.7 fusion.127
  96.9 2.0 fusion.128
  98.9 1.8 fusion.129
  102.4 1.3 convert_reduce_fusion.7
  103.6 1.7 fusion.127
  105.3 2.0 fusion.128
  107.4 1.8 fusion.129
  112.1 1.7 fusion.127
  113.8 2.0 fusion.128
  115.8 1.8 fusion.129
  120.6 1.7 fusion.127
  122.3 2.0 fusion.128
  124.3 1.8 fusion.129
  129.0 1.7 fusion.127
  130.7 2.0 fusion.128
  132.7 1.8 fusion.129
  137.5 1.7 fusion.127
  139.2 2.0 fusion.128
  141.2 1.8 fusion.129
  145.9 1.7 fusion.127
  147.6 2.0 fusion.128
  149.6 1.8 fusion.129
  154.4 1.7 fusion.127
  156.1 2.0 fusion.128
  158.1 1.8 fusion.129
  161.6 1.3 copy.65
  162.8 10.9 %all-to-all-start = ((bf16[16,256,128]{2,1,0:T(8,128)(2,1)}), bf16[16,256,128]{2,1,0:T(8,128)(2,1)S(1)}, u32[]{:S(2)}, u32[]{:S(2)}) async-start(bf16[16,256,128]{2,1,0:T(8,128)(2,1)} %bitcast.34), calls=%async_computation | async-start | bytes 2097152 | tf_op jit(solution)/shard_map/all_to_all | solution.py:152
  173.9 46.1 %psum.22 = bf16[256]{0:T(256)(128)(2,1)S(1)} all-reduce(bf16[256]{0:T(256)(128)(2,1)S(1)} %fusion.65), channel_id=1, replica_groups=mesh['row'=8,'col'=16] {'col'}, use_global_device_ids=true, to_apply=%region_8.9 | all-reduce | flops 256 | bytes 1024 | tf_op jit(solution)/shard_map/psum | solution.py:138
  222.0 13.6 %all_gather.3 = bf16[2048,2,48]{0,2,1:T(8,128)(2,1)S(1)} all-gather(bf16[256,2,48]{0,2,1:T(8,128)(2,1)S(1)} %slice.98), channel_id=1, replica_groups=mesh['row'=8,'col'=16] {'row'}, dimensions={0}, use_global_device_ids=true | all-gather | bytes 442368 | tf_op jit(solution)/shard_map/all_gather | solution.py:150
  239.2 2.6 fusion.32
  241.9 67.5 %reduce-scatter.4.cloned.1.call-done = bf16[48,256]{1,0:T(8,128)(2,1)} async-done(((bf16[768,256]{1,0:T(8,128)(2,1)}), bf16[48,256]{1,0:T(8,128)(2,1)}) %reduce-scatter.4.cloned.1.call-update) | async-done | bytes 24592
  311.8 81.2 %all-reduce.5.cloned.1.call-done = bf16[256,128]{1,0:T(8,128)(2,1)} async-done(((bf16[256,128]{1,0:T(8,128)(2,1)}), bf16[256,128]{1,0:T(8,128)(2,1)}) %all-reduce.5.cloned.1.call-update) | async-done | bytes 65552 | tf_op jit(solution)/shard_map/psum | solution.py:176
  393.1 1.7 fusion.39
  (204 shorter events, 60.7 us)
Async XLA Ops:
  7.2 8.6 %copy-start = (bf16[4,16,32,128]{3,2,1,0:T(8,128)(2,1)S(1)}, bf16[4,16,32,128]{3,2,1,0:T(8,128)(2,1)}, u32[]{:S(2)}) copy-start(bf16[4,16,32,128]{3,2,1,0:T(8,128)(2,1)} %param.18) | copy-start | bytes 1572868
  7.2 15.2 %copy-start.1 = (bf16[128,128]{1,0:T(8,128)(2,1)S(1)}, bf16[128,128]{1,0:T(8,128)(2,1)}, u32[]{:S(2)}) copy-start(bf16[128,128]{1,0:T(8,128)(2,1)} %param.17) | copy-start | bytes 98308
  7.2 212.8 %all-reduce.3.cloned.1.call-start = ((), (), s32[]{:S(2)}) async-start(), calls=%async_computation.2 | async-start | bytes 786432 | tf_op jit(solution)/shard_map/psum | solution.py:137
  8.0 12.5 %collective-permute-start.1 = (bf16[48,128]{1,0:T(8,128)(2,1)S(1)}, bf16[48,128]{1,0:T(8,128)(2,1)S(1)}, u32[]{:S(2)}, u32[]{:S(2)}) collective-permute-start(bf16[48,128]{1,0:T(8,128)(2,1)S(1)} %get-tuple-element.86), channel_id=1, source_target_pairs={{1,0},{2,1},{3,2},{4,3},{5,4},{6,5},{7,6},{8,7},{9,8},{10,9},{11,1... | collective-permute-start | bytes 36872 | tf_op jit(solution)/shard_map/ppermute | solution.py:29
  9.3 11.3 %collective-permute-start = (bf16[48,128]{1,0:T(8,128)(2,1)S(1)}, bf16[48,128]{1,0:T(8,128)(2,1)S(1)}, u32[]{:S(2)}, u32[]{:S(2)}) collective-permute-start(bf16[48,128]{1,0:T(8,128)(2,1)S(1)} %get-tuple-element.85), channel_id=1, source_target_pairs={{0,1},{1,2},{2,3},{3,4},{4,5},{5,6},{6,7},{7,8},{8,9},{9,10},{10,1... | collective-permute-start | bytes 36872 | tf_op jit(solution)/shard_map/ppermute | solution.py:28
  18.5 155.2 %copy-start.5 = (s32[128]{0:T(128)}, s32[128]{0:T(128)S(1)}, u32[]{:S(2)}) copy-start(s32[128]{0:T(128)S(1)} %broadcast_subtract_fusion) | copy-start | bytes 1540
  22.8 2.1 copy-start.8
  22.8 2.2 copy-start.3
  23.1 3.1 copy-start.7
  23.1 3.1 copy-start.9
  161.6 58.4 %copy-start.2 = (bf16[256,768]{1,0:T(8,128)(2,1)S(1)}, bf16[256,768]{1,0:T(8,128)(2,1)}, u32[]{:S(2)}) copy-start(bf16[256,768]{1,0:T(8,128)(2,1)} %param.20) | copy-start | bytes 1179652
  162.8 58.8 %copy-start.6 = (bf16[768,4,48]{0,2,1:T(8,128)(2,1)S(1)}, bf16[768,4,48]{0,2,1:T(8,128)(2,1)}, u32[]{:S(2)}) copy-start(bf16[768,4,48]{0,2,1:T(8,128)(2,1)} %param.29) | copy-start | bytes 884740
  162.8 72.8 %all-to-all-start = ((bf16[16,256,128]{2,1,0:T(8,128)(2,1)}), bf16[16,256,128]{2,1,0:T(8,128)(2,1)S(1)}, u32[]{:S(2)}, u32[]{:S(2)}) async-start(bf16[16,256,128]{2,1,0:T(8,128)(2,1)} %bitcast.34), calls=%async_computation | async-start | bytes 2097152 | tf_op jit(solution)/shard_map/all_to_all | solution.py:152
  173.7 135.7 %reduce-scatter.4.cloned.1.call-start = ((), (), s32[]{:S(2)}) async-start(), calls=%async_computation.4 | async-start | bytes 417792
  239.2 71.1 %copy-start.4 = (bf16[48,128]{1,0:T(8,128)(2,1)S(1)}, bf16[48,128]{1,0:T(8,128)(2,1)}, u32[]{:S(2)}) copy-start(bf16[48,128]{1,0:T(8,128)(2,1)} %param.31) | copy-start | bytes 36868
  241.8 151.2 %all-reduce.5.cloned.1.call-start = ((), (), s32[]{:S(2)}) async-start(), calls=%async_computation.3 | async-start | bytes 131072 | tf_op jit(solution)/shard_map/psum | solution.py:176
Sparse Core Ops, SparseCore 0:
  26.3 90.0 all-reduce.2
  242.0 67.3 reduce-scatter.3
  312.9 80.1 all-reduce.4
where the time goes:
time: 405 us; the launch traced here: 401 us
  waiting for transfers between devices  149 us (37%)
  matrix products  84.7 us (21%)
  other arithmetic  68.4 us (17%)
  blocking collectives  59.7 us (15%)
  starting transfers between devices  16.8 us (4%)
  between operations  14.2 us (4%)
  local copies, waits for them, and re-layouts  7.55 us (2%)
    psum x1, waiting for transfers between devices, body(): lax.psum(jnp.dot(single_out, back_w, preferred_element_type=jnp.float32)....  81.2 us
    unnamed x4, waiting for transfers between devices  67.5 us
    psum x1, blocking collectives, body(): lax.psum(count_part.astype(jnp.bfloat16), 'col').astype(jnp.float32)  46.1 us
    reduce_sum x35, other arithmetic, layer_norm(): spread = jnp.mean(centred * centred, axis=-1, keepdims=True)  39 us
    dot_general x16, matrix products, pair_block(): jnp.einsum('ijc,cmf->ijmf', normed, trans_in, preferred_element_type=jnp....  32.1 us
    dot_general x16, matrix products, pair_block(): jnp.einsum('ijf,fc->ijc', hidden, trans_out, preferred_element_type=jnp.f...  29.3 us
    reduce_sum x35, other arithmetic, layer_norm(): centred = values - jnp.mean(values, axis=-1, keepdims=True)  25.4 us
    all_gather x1, blocking collectives, body(): kv_rows = lax.all_gather(token_proj[:, 1:3, :], 'row', axis=0, tiled=True)  13.6 us
  transfers between devices with their start and end apart: 6, of which 2 were waited for; matrix products, arithmetic and copies ran while one was open for 36% of the time, Pallas kernels for 0%

commit v1 on v0

v1 whole, which is shorter than its diff:
```python
import functools
import math

import jax
import jax.numpy as jnp
from jax import lax
from jax.experimental import pallas as pl
from jax.experimental.pallas import tpu as pltpu
from jax.sharding import PartitionSpec as P

HEADS = 16
HEAD = 48
CA = 128
CZ = 128
ATOM_HEADS = 4
ATOM_HEAD = 32
QW = 32
KW = 128
RIM = (KW - QW) // 2
PAIR_ROWS = 32
FIRST_ROWS = 64
MIB = 2**20

epsilon = 1e-05
masked_score = -1e30
bf16 = jnp.bfloat16
f32 = jnp.float32


def dot(a, b):
    return jnp.dot(a, b, preferred_element_type=f32)


def dot_t(a, b):
    return lax.dot_general(a, b, (((1,), (1,)), ((), ())), preferred_element_type=f32)


def layer_norm(values):
    centred = values - jnp.mean(values, axis=-1, keepdims=True)
    spread = jnp.mean(centred * centred, axis=-1, keepdims=True)
    return centred * lax.rsqrt(spread + epsilon)


def whole(array):
    return pl.BlockSpec(array.shape, lambda *_: (0,) * array.ndim)


def params(mib=48):
    return pltpu.CompilerParams(vmem_limit_bytes=mib * MIB)


def cost(flops, moved):
    return pl.CostEstimate(flops=flops, bytes_accessed=moved, transcendentals=0)


def atom_kernel(
    place_ref, pair_w_ref, before_ref, own_ref, after_ref, atom_pair_ref, token_ref, w_ref, wo_ref,
    mid_ref, send_ref,
):
    device, row, last = place_ref[0], place_ref[1], place_ref[2]
    atoms = own_ref[...].astype(f32)
    count = atoms.shape[0]
    extended = jnp.concatenate([before_ref[...].astype(f32), atoms, after_ref[...].astype(f32)], axis=0)
    norm = layer_norm(extended).astype(bf16)
    projected = dot(norm, w_ref[...]).astype(bf16)
    lanes = lax.broadcasted_iota(jnp.int32, (1, CA), 1) // ATOM_HEAD
    keys = lax.broadcasted_iota(jnp.int32, (1, KW), 1)
    parts = []
    for window in range(count // QW):
        start = window * QW
        query = projected[RIM + start : RIM + start + QW, :CA]
        query = jnp.concatenate(
            [jnp.where(lanes == head, query, jnp.zeros_like(query)) for head in range(ATOM_HEADS)], axis=0
        )
        key = projected[start : start + KW, CA : 2 * CA]
        value = projected[start : start + KW, 2 * CA : 3 * CA]
        planes = [atom_pair_ref[window, c].astype(f32) for c in range(atom_pair_ref.shape[1])]
        bias = []
        for head in range(ATOM_HEADS):
            total = planes[0] * pair_w_ref[0, head]
            for c in range(1, len(planes)):
                total = total + planes[c] * pair_w_ref[c, head]
            bias.append(total)
        scores = dot_t(query, key) / math.sqrt(ATOM_HEAD) + jnp.concatenate(bias, axis=0)
        position = device * count - RIM + start + keys
        scores = jnp.where((position >= 0) & (position < last), scores, masked_score)
        raised = jnp.exp(scores - jnp.max(scores, axis=-1, keepdims=True))
        weights = (raised / jnp.sum(raised, axis=-1, keepdims=True)).astype(bf16)
        mixed = dot(weights, value)
        out = jnp.zeros((QW, CA), f32)
        for head in range(ATOM_HEADS):
            out = out + jnp.where(lanes == head, mixed[head * QW : (head + 1) * QW], 0.0)
        parts.append(out)
    attended = jnp.concatenate(parts, axis=0)
    gate = projected[RIM : RIM + count, 3 * CA :].astype(f32)
    gated = (jax.nn.sigmoid(gate) * attended).astype(bf16)
    mid = (atoms + dot(gated, wo_ref[...])).astype(bf16)
    mid_ref[...] = mid
    local = (token_ref[...] - row).astype(f32).astype(bf16)
    tail = jnp.broadcast_to(local, (16, count))
    for target in range(send_ref.shape[0]):
        send_ref[target, :count, :] = mid
        send_ref[target, count:, :] = tail


def pair_body(pair_ref, centre_ref, win_ref, wout_ref, wb_ref, out_ref, hold_ref):
    rows = pair_ref.shape[0]
    tile = pair_ref[...].reshape(rows * pair_ref.shape[1], CZ)
    centred = dot_t(centre_ref[...], tile)
    spread = jnp.sum(centred * centred, axis=0, keepdims=True) * (1.0 / CZ)
    normed = (centred * lax.rsqrt(spread + epsilon)).astype(bf16)
    both = dot(win_ref[...], normed)
    half = both.shape[0] // 2
    gate, up = both[:half], both[half:]
    hidden = ((gate * jnp.tanh(gate) + gate) * up).astype(bf16)
    renewed = centred + dot(wout_ref[...], hidden)
    spread = jnp.sum(renewed * renewed, axis=0, keepdims=True) * (1.0 / CZ)
    bias = dot(wb_ref[...], renewed.astype(bf16)) * lax.rsqrt(spread + epsilon)
    width = pair_ref.shape[1]
    for i in range(rows):
        hold_ref[:, i, :] = bias[:, i * width : (i + 1) * width]
    out_ref[...] = hold_ref[...].astype(bf16)


def pair_first(*refs):
    pair_body(*refs)


def pair_rest(_, *refs):
    pair_body(*refs)


def pair_call(pair, weights, start, stop, partial_out):
    steps = (stop - start) // PAIR_ROWS
    skip = start // PAIR_ROWS
    rows, cols, _ = pair.shape
    in_specs = [pl.BlockSpec((PAIR_ROWS, cols, CZ), lambda i: (i + skip, 0, 0))] + [whole(w) for w in weights]
    operands = (pair, *weights)
    aliases = {}
    kernel = pair_first
    if partial_out is not None:
        in_specs = [pl.BlockSpec(memory_space=pl.ANY)] + in_specs
        operands = (partial_out, *operands)
        aliases = {0: 0}
        kernel = pair_rest
    positions = (stop - start) * cols
    return pl.pallas_call(
        kernel,
        grid=(steps,),
        in_specs=in_specs,
        out_specs=pl.BlockSpec((HEADS, PAIR_ROWS, cols), lambda i: (0, i + skip, 0)),
        out_shape=jax.ShapeDtypeStruct((HEADS, rows, cols), bf16),
        scratch_shapes=[pltpu.VMEM((HEADS, PAIR_ROWS, cols), f32)],
        input_output_aliases=aliases,
        compiler_params=params(56),
        cost_estimate=cost(positions * 620_000, positions * 288),
        name="pair_bias",
    )(*operands)


def token_kernel(got_ref, single_ref, agg_ref, wq_ref, wt_ref, in_ref, query_ref, gate_ref, send_ref):
    sources, count = got_ref.shape[0], got_ref.shape[2]
    tokens = single_ref.shape[0]
    mids = jnp.concatenate([got_ref[s, :count, :] for s in range(sources)], axis=0)
    features = jnp.maximum(dot(mids, agg_ref[...]), 0.0).astype(bf16)
    token = lax.broadcasted_iota(jnp.int32, (tokens, count), 0).astype(f32)
    onehot = jnp.concatenate(
        [
            jnp.where(token == got_ref[s, count : count + 16, :].astype(f32)[:1], 1.0, 0.0)
            for s in range(sources)
        ],
        axis=1,
    )
    token_count = jnp.sum(onehot, axis=1, keepdims=True)
    token_sum = dot(onehot.astype(bf16), features)
    token_in = (single_ref[...].astype(f32) + token_sum / token_count).astype(bf16)
    in_ref[...] = token_in
    norm = layer_norm(token_in.astype(f32)).astype(bf16)
    query_ref[...] = dot(norm, wq_ref[...]).astype(bf16)
    rest = dot_t(wt_ref[...], norm).astype(bf16)
    gate_ref[...] = rest[2 * HEAD :]
    for target in range(send_ref.shape[0]):
        send_ref[target] = rest[: 2 * HEAD]


def attention_kernel(query_ref, gate_ref, kv_ref, bias_ref, send_ref):
    rows = kv_ref.shape[0]
    per = bias_ref.shape[0] // rows
    scores = jnp.concatenate(
        [
            dot(query_ref[...], kv_ref[r, :HEAD, :]) / math.sqrt(HEAD)
            + jnp.concatenate([bias_ref[r * per + k].astype(f32) for k in range(per)], axis=1)
            for r in range(rows)
        ],
        axis=1,
    )
    raised = jnp.exp(scores - jnp.max(scores, axis=-1, keepdims=True))
    weights = (raised / jnp.sum(raised, axis=-1, keepdims=True)).astype(bf16)
    values = jnp.concatenate([kv_ref[r, HEAD:, :] for r in range(rows)], axis=1)
    attended = dot_t(values, weights)
    gated = (jax.nn.sigmoid(gate_ref[...].astype(f32)) * attended).astype(bf16)
    for target in range(send_ref.shape[0]):
        send_ref[target] = gated


def final_kernel(place_ref, got_ref, in_ref, weights_ref, mid_ref, token_ref, single_ref, atoms_ref):
    heads, head, tokens = got_ref.shape
    width = in_ref.shape[1]
    gated = got_ref[...].reshape(heads * head, tokens).T
    single = (in_ref[...].astype(f32) + dot(gated, weights_ref[:, :width])).astype(bf16)
    mine = single_ref.shape[1]
    column = lax.broadcasted_iota(jnp.int32, (width, mine), 0)
    wanted = lax.broadcasted_iota(jnp.int32, (width, mine), 1) + place_ref[3] * mine
    select = jnp.where(column == wanted, 1.0, 0.0).astype(bf16)
    single_ref[...] = dot(single, select).astype(bf16)
    back = dot(single, weights_ref[:, width:]).astype(bf16)
    count = mid_ref.shape[0]
    token = lax.broadcasted_iota(jnp.int32, (tokens, count), 0)
    onehot = jnp.where(token == token_ref[...] - place_ref[1], 1.0, 0.0)
    picked = dot(onehot.T.astype(bf16), back)
    atoms_ref[...] = (mid_ref[...].astype(f32) + picked).astype(bf16)


def body(
    atoms,
    atom_pair,
    atom_token,
    single,
    pair,
    atom_w,
    atom_pair_w,
    atom_wo,
    agg_w,
    trans_in,
    trans_out,
    bias_w,
    token_w,
    token_wo,
    back_w,
):
    row_size, col_size = lax.axis_size("row"), lax.axis_size("col")
    count = atoms.shape[0]
    query_rows, width = single.shape
    both = ("row", "col")
    devices = row_size * col_size
    up = [(i, i + 1) for i in range(devices - 1)]
    down = [(j, i) for i, j in up]
    before = lax.ppermute(atoms[count - RIM :], both, up)
    after = lax.ppermute(atoms[:RIM], both, down)
    out_weights = lax.all_gather(jnp.concatenate([token_wo, back_w], axis=1), "col", axis=0, tiled=True)

    device = lax.axis_index(both)
    place = jnp.stack(
        [
            device,
            lax.axis_index("row") * query_rows,
            jnp.asarray(count * devices, device.dtype),
            lax.axis_index("col"),
        ]
    ).astype(jnp.int32)
    smem = pl.BlockSpec(memory_space=pltpu.SMEM)
    token_row = atom_token.reshape(1, count)

    centre = (jnp.eye(CZ, dtype=f32) - 1.0 / CZ).astype(bf16)
    half = jnp.asarray(0.5, bf16)
    win = jnp.concatenate([trans_in[:, 0, :] * half, trans_in[:, 1, :]], axis=1).T
    wout = dot_t(centre, trans_out).astype(bf16)
    pair_weights = (centre, win, wout, bias_w.T)
    bias = pair_call(pair, pair_weights, 0, FIRST_ROWS, None)

    atom_weights = atom_w.reshape(CA, 4 * CA)
    vmem = pl.BlockSpec(memory_space=pltpu.VMEM)
    mid, mid_send = pl.pallas_call(
        atom_kernel,
        in_specs=[smem, smem] + [vmem] * 7,
        out_specs=[vmem, vmem],
        out_shape=[
            jax.ShapeDtypeStruct((count, CA), bf16),
            jax.ShapeDtypeStruct((col_size, count + 16, CA), bf16),
        ],
        compiler_params=params(),
        cost_estimate=cost(4_000_000_000, 2_000_000),
        name="atom_stage",
    )(place, atom_pair_w.astype(f32), before, atoms, after, atom_pair, token_row, atom_weights, atom_wo)
    mids = lax.all_to_all(mid_send, "col", split_axis=0, concat_axis=0, tiled=True)

    bias = pair_call(pair, pair_weights, FIRST_ROWS, query_rows, bias)
    bias_rows = lax.all_to_all(bias, "col", split_axis=0, concat_axis=0, tiled=True)

    turned = jnp.transpose(token_w[:, 1:, :], (1, 2, 0)).reshape(3 * HEAD, width)
    token_in, query, gate, kv_send = pl.pallas_call(
        token_kernel,
        in_specs=[vmem] * 5,
        out_specs=[vmem] * 4,
        out_shape=[
            jax.ShapeDtypeStruct((query_rows, width), bf16),
            jax.ShapeDtypeStruct((query_rows, HEAD), bf16),
            jax.ShapeDtypeStruct((HEAD, query_rows), bf16),
            jax.ShapeDtypeStruct((row_size, 2 * HEAD, query_rows), bf16),
        ],
        compiler_params=params(),
        cost_estimate=cost(4_000_000_000, 2_000_000),
        name="token_stage",
    )(mids, single, agg_w, token_w[:, 0, :], turned)
    kv = lax.all_to_all(kv_send, "row", split_axis=0, concat_axis=0, tiled=True)

    gated_send = pl.pallas_call(
        attention_kernel,
        in_specs=[vmem] * 4,
        out_specs=vmem,
        out_shape=jax.ShapeDtypeStruct((col_size, HEAD, query_rows), bf16),
        compiler_params=params(),
        cost_estimate=cost(3_000_000_000, 2_000_000),
        name="token_attention",
    )(query, gate, kv, bias_rows)
    gated = lax.all_to_all(gated_send, "col", split_axis=0, concat_axis=0, tiled=True)

    return pl.pallas_call(
        final_kernel,
        in_specs=[smem] + [vmem] * 5,
        out_specs=[vmem, vmem],
        out_shape=[
            jax.ShapeDtypeStruct((query_rows, width // col_size), bf16),
            jax.ShapeDtypeStruct((count, CA), bf16),
        ],
        compiler_params=params(),
        cost_estimate=cost(3_000_000_000, 2_000_000),
        name="token_out",
    )(place, gated, token_in, out_weights, mid, token_row)


def solution(mesh):
    in_specs = (
        P(("row", "col"), None),
        P(("row", "col"), None, None, None),
        P(("row", "col")),
        P("row", None),
        P("row", "col", None),
        P(),
        P(),
        P(),
        P(),
        P(),
        P(),
        P(),
        P(None, None, "col"),
        P("col", None),
        P("col", None),
    )
    out_specs = (P("row", "col"), P(("row", "col"), None))
    return jax.shard_map(body, mesh=mesh, in_specs=in_specs, out_specs=out_specs, check_vma=False)
```

time: 405 us -> 120 us (0.30)
  waiting for transfers between devices: 149 us -> 5.78 us
  matrix products: 84.7 us -> 0.78 us
  other arithmetic: 68.4 us -> 2.93 us
  Pallas kernels: 0 us -> 31 us
  blocking collectives: 59.7 us -> 34.4 us
    dot_general x59 -> x1, matrix products: 84.3 us -> 0.78 us  [dot_t(): lax.dot_general(a, b, (((1,), (1,)), ((), ())), preferred_element_type=f32)]
    psum x2 -> x0, waiting for transfers between devices: 81.2 us -> none  [the longest x1 81.2 us: body(): lax.psum(jnp.dot(single_out, back_w, preferred_element_type=jnp.float32)....]
    unnamed x4 -> x1, waiting for transfers between devices: 67.5 us -> 0.02 us
    reduce_sum x72 -> x0, other arithmetic: 65.5 us -> none  [the longest x35 39 us: layer_norm(): spread = jnp.mean(centred * centred, axis=-1, keepdims=True)]
    psum x1 -> x0, blocking collectives: 46.1 us -> none  [body(): lax.psum(count_part.astype(jnp.bfloat16), 'col').astype(jnp.float32)]
    all_to_all x0 -> x2, blocking collectives: none -> 34.4 us  [the longest x1 21.7 us: body(): lax.all_to_all(bias, 'col', split_axis=0, concat_axis=0, tiled=True)]
    pallas_call x0 -> x6, Pallas kernels: none -> 31 us  [the longest x2 21 us: pair_call(): pl.pallas_call(kernel, grid=(steps,), in_specs=in_specs, out_specs=pl.Blo...]
    all_gather x1 -> x0, blocking collectives: 13.6 us -> none  [body(): kv_rows = lax.all_gather(token_proj[:, 1:3, :], 'row', axis=0, tiled=True)]
  transfers between devices with their start and end apart: 6 -> 5, of which waited for: 2 -> 1; matrix products, arithmetic and copies ran while one was open for 36% -> 7% of each run, Pallas kernels for 0% -> 24%
where the time goes in v1:
time: 120 us; the launch traced here: 119 us
  blocking collectives  34.4 us (29%)
  Pallas kernels  31 us (26%)
  starting transfers between devices  18.3 us (15%)
  between operations  14.2 us (12%)
  local copies, waits for them, and re-layouts  11.2 us (9%)
  waiting for transfers between devices  5.78 us (5%)
  other arithmetic  2.93 us (2%)
    all_to_all x1, blocking collectives, body(): lax.all_to_all(bias, 'col', split_axis=0, concat_axis=0, tiled=True)  21.7 us
    pallas_call x2, Pallas kernels, pair_call(): pl.pallas_call(kernel, grid=(steps,), in_specs=in_specs, out_specs=pl.Blo...  21 us
    all_to_all x1, blocking collectives, body(): lax.all_to_all(gated_send, 'col', split_axis=0, concat_axis=0, tiled=True)  12.8 us
    all_to_all x1, starting transfers between devices, body(): lax.all_to_all(mid_send, 'col', split_axis=0, concat_axis=0, tiled=True)  8.61 us
    unnamed x22, local copies, waits for them, and re-layouts  5.93 us
    all_to_all x1, waiting for transfers between devices, body(): lax.all_to_all(mid_send, 'col', split_axis=0, concat_axis=0, tiled=True)  5.75 us
    all_to_all x1, starting transfers between devices, body(): kv = lax.all_to_all(kv_send, 'row', split_axis=0, concat_axis=0, tiled=True)  4.47 us
    ppermute x1, starting transfers between devices, body(): before = lax.ppermute(atoms[count - RIM:], both, up)  3.89 us
  transfers between devices with their start and end apart: 5, of which 1 were waited for; matrix products, arithmetic and copies ran while one was open for 7% of the time, Pallas kernels for 24%

profile of v1, /device:TPU:0, one launch (start us, length us, event | category | flops | bytes accessed | tf_op | source)
XLA Modules:
  0.0 118.6 jit_solution(6693852466361952907)
XLA Ops:
  7.2 0.0 copy-start
  7.2 0.0 all-gather.2.cloned.1.call-start
  7.2 0.7 fusion.2
  8.0 3.9 %collective-permute-start = (bf16[48,128]{1,0:T(8,128)(2,1)S(1)}, bf16[48,128]{1,0:T(8,128)(2,1)S(1)}, u32[]{:S(2)}, u32[]{:S(2)}) collective-permute-start(bf16[48,128]{1,0:T(8,128)(2,1)S(1)} %get-tuple-element.21), channel_id=1, source_target_pairs={{0,1},{1,2},{2,3},{3,4},{4,5},{5,6},{6,7},{7,8},{8,9},{9,10},{10,1... | collective-permute-start | bytes 36872 | tf_op jit(solution)/shard_map/ppermute | solution.py:248
  11.9 1.3 %collective-permute-start.1 = (bf16[48,128]{1,0:T(8,128)(2,1)S(1)}, bf16[48,128]{1,0:T(8,128)(2,1)S(1)}, u32[]{:S(2)}, u32[]{:S(2)}) collective-permute-start(bf16[48,128]{1,0:T(8,128)(2,1)S(1)} %get-tuple-element.20), channel_id=1, source_target_pairs={{1,0},{2,1},{3,2},{4,3},{5,4},{6,5},{7,6},{8,7},{9,8},{10,9},{11,1... | collective-permute-start | bytes 36872 | tf_op jit(solution)/shard_map/ppermute | solution.py:249
  13.2 1.5 %pad_maximum_fusion = bf16[48,896]{1,0:T(8,128)(2,1)} fusion(bf16[48,128]{1,0:T(8,128)(2,1)} %param.29, bf16[48,768]{1,0:T(8,128)(2,1)} %param.28), kind=kLoop, calls=%fused_computation.3 | loop fusion | flops 172032 | bytes 172032 | tf_op jit(solution)/shard_map/concatenate | solution.py:250
  14.7 0.0 all-gather.2.cloned.1.call-update
  14.7 1.2 %fusion.1 = (bf16[128,1,256]{2,1,0:T(2,128)(2,1)S(1)}, bf16[128,1,256]{2,1,0:T(2,128)(2,1)S(1)}) fusion(bf16[128,2,256]{2,1,0:T(2,128)(2,1)} %param.24), kind=kLoop, calls=%fused_computation.9 | loop fusion | bytes 262144 | tf_op jit(solution)/shard_map/slice | solution.py:266
  15.9 0.1 copy.29
  16.1 0.1 copy.30
  16.2 0.0 copy-done
  16.2 0.8 convolution_convert_fusion.refs_3_
  17.0 0.7 maximum_bitcast_fusion.refs_2_
  17.7 0.1 pad_add_fusion.place_ref
  17.8 0.9 slice.20
  18.7 0.9 slice.21
  19.6 0.9 copy.33
  20.6 0.8 copy.23.pair_w_ref
  21.3 0.2 copy.28
  21.5 0.0 collective-permute-done.before_ref
  21.5 0.0 collective-permute-done.1.after_ref
  21.5 0.0 copy-start.1
  21.5 0.7 copy-done.1
  22.3 0.0 copy-start.3
  22.3 1.0 copy-done.3
  23.3 0.0 copy-start.6
  23.3 0.8 copy-done.6
  24.1 0.0 copy-start.7
  24.1 0.7 copy-done.7
  24.7 3.1 %atom_stage.1 = (bf16[128,128]{1,0:T(8,128)(2,1)S(1)}, bf16[16,144,128]{2,1,0:T(8,128)(2,1)}) custom-call(s32[4]{0:T(128)S(1)} %pad_add_fusion.place_ref, f32[16,4]{1,0:T(8,128)S(1)} %copy.23.pair_w_ref, bf16[48,128]{1,0:T(8,128)(2,1)S(1)} %collective-permute-done.before_ref, bf16[128,128]{1,0:T(8,128)(2,1)S(1)} %copy-done.1, ...), custom_call_target="tpu_custom_call" | custom-call | flops 4000000000 | bytes 2000000 | tf_op jit(solution)/shard_map/atom_stage/pallas_call | solution.py:273
  27.9 8.6 %all-to-all-start = ((bf16[16,144,128]{2,1,0:T(8,128)(2,1)}), bf16[16,144,128]{2,1,0:T(8,128)(2,1)S(1)}, u32[]{:S(2)}, u32[]{:S(2)}) async-start(bf16[16,144,128]{2,1,0:T(8,128)(2,1)} %get-tuple-element.8), calls=%async_computation | async-start | bytes 1179648 | tf_op jit(solution)/shard_map/all_to_all | solution.py:285
  36.5 0.6 add_convert_fusion.refs_1_
  37.1 0.0 copy-start.4
  37.1 0.0 copy-start.5
  37.1 6.3 %pair_bias.2._ = bf16[16,256,128]{2,1,0:T(8,128)(2,1)} custom-call(bf16[256,128,128]{2,1,0:T(8,128)(2,1)} %refs_0_.3, bf16[128,128]{1,0:T(8,128)(2,1)} %add_convert_fusion.refs_1_, bf16[512,128]{1,0:T(8,128)(2,1)} %maximum_bitcast_fusion.refs_2_, bf16[128,256]{1,0:T(8,128)(2,1)} %convolution_convert_fusion.refs_3_, bf16[16,128]{1,0:T(8,128)(2,1)} %bitcast.26), custom_call_target="tpu_custom_call" | custom-call | flops 5079040000 | bytes 2359296 | tf_op jit(solution)/shard_map/pair_bias/pallas_call | solution.py:147
  43.4 5.8 %all-to-all-done.got_ref = bf16[16,144,128]{2,1,0:T(8,128)(2,1)S(1)} async-done(((bf16[16,144,128]{2,1,0:T(8,128)(2,1)}), bf16[16,144,128]{2,1,0:T(8,128)(2,1)S(1)}, u32[]{:S(2)}, u32[]{:S(2)}) %all-to-all-start) | async-done | bytes 589856 | tf_op jit(solution)/shard_map/all_to_all | solution.py:285
  49.1 0.0 copy-done.4
  49.1 0.0 copy-done.5
  49.1 3.1 %token_stage.1 = (bf16[256,768]{1,0:T(8,128)(2,1)S(1)}, bf16[256,48]{1,0:T(8,128)(2,1)S(1)}, bf16[48,256]{1,0:T(8,128)(2,1)S(1)}, bf16[8,96,256]{2,1,0:T(8,128)(2,1)}) custom-call(bf16[16,144,128]{2,1,0:T(8,128)(2,1)S(1)} %all-to-all-done.got_ref, bf16[256,768]{1,0:T(8,128)(2,1)S(1)} %copy-done.4, bf16[128,768]{1,0:T(8,128)(2,1)S(1)} %copy-done.5, ...), custom_call_target="tpu_custom_call" | custom-call | flops 4000000000 | bytes 2000000 | tf_op jit(solution)/shard_map/token_stage/pallas_call | solution.py:291
  52.2 4.5 %all-to-all-start.1 = ((bf16[8,96,256]{2,1,0:T(8,128)(2,1)}), bf16[8,96,256]{2,1,0:T(8,128)(2,1)S(1)}, u32[]{:S(2)}, u32[]{:S(2)}) async-start(bf16[8,96,256]{2,1,0:T(8,128)(2,1)} %get-tuple-element.11), calls=%async_computation.1 | async-start | bytes 786432 | tf_op jit(solution)/shard_map/all_to_all | solution.py:305
  56.7 14.8 %pair_bias.3 = bf16[16,256,128]{2,1,0:T(8,128)(2,1)} custom-call(bf16[16,256,128]{2,1,0:T(8,128)(2,1)} %pair_bias.2._, bf16[256,128,128]{2,1,0:T(8,128)(2,1)} %refs_0_.3, bf16[128,128]{1,0:T(8,128)(2,1)} %add_convert_fusion.refs_1_, bf16[512,128]{1,0:T(8,128)(2,1)} %maximum_bitcast_fusion.refs_2_, ...), custom_call_target="tpu_custom_call", output_to_operand_aliasing={{}: (0, {})} | custom-call | flops 15237120000 | bytes 7077888 | tf_op jit(solution)/shard_map/pair_bias/pallas_call | solution.py:147
  71.5 0.0 copy-start.8
  71.5 0.0 all-to-all-done.1.kv_ref
  71.5 21.7 %all_to_all.20.bias_ref = bf16[16,256,128]{2,1,0:T(8,128)(2,1)S(1)} all-to-all(bf16[16,256,128]{2,1,0:T(8,128)(2,1)} %pair_bias.3), channel_id=1, replica_groups=mesh['row'=8,'col'=16] {'col'}, dimensions={0} | all-to-all | bytes 2097152 | tf_op jit(solution)/shard_map/all_to_all | solution.py:288
  93.1 1.6 %token_attention.1 = bf16[16,48,256]{2,1,0:T(8,128)(2,1)S(1)} custom-call(bf16[256,48]{1,0:T(8,128)(2,1)S(1)} %get-tuple-element.9.query_ref, bf16[48,256]{1,0:T(8,128)(2,1)S(1)} %get-tuple-element.10.gate_ref, bf16[8,96,256]{2,1,0:T(8,128)(2,1)S(1)} %all-to-all-done.1.kv_ref, bf16[16,256,128]{2,1,0:T(8,128)(2,1)S(1)} %all_to_all.20.bias_ref), custom_call_target="tpu_custom_call" | custom-call | flops 3000000000 | bytes 2000000 | tf_op jit(solution)/shard_map/token_attention/pallas_call | solution.py:307
  94.8 12.8 %all_to_all.21.got_ref = bf16[16,48,256]{2,1,0:T(8,128)(2,1)S(1)} all-to-all(bf16[16,48,256]{2,1,0:T(8,128)(2,1)S(1)} %token_attention.1), channel_id=1, replica_groups=mesh['row'=8,'col'=16] {'col'}, dimensions={0} | all-to-all | bytes 786432 | tf_op jit(solution)/shard_map/all_to_all | solution.py:316
  107.6 0.0 all-gather.2.cloned.1.call-done.weights_ref
  107.6 0.0 copy-done.8
  107.6 0.0 copy-start.2
  107.6 1.3 %copy-done.2 = bf16[768,896]{1,0:T(8,128)(2,1)S(1)} copy-done((bf16[768,896]{1,0:T(8,128)(2,1)S(1)}, bf16[768,896]{1,0:T(8,128)(2,1)}, u32[]{:S(2)}) %copy-start.2) | copy-done | bytes 1376280
  108.9 2.1 %token_out.1 = (bf16[256,48]{1,0:T(8,128)(2,1)S(1)}, bf16[128,128]{1,0:T(8,128)(2,1)}) custom-call(s32[4]{0:T(128)S(1)} %pad_add_fusion.place_ref, bf16[16,48,256]{2,1,0:T(8,128)(2,1)S(1)} %all_to_all.21.got_ref, bf16[256,768]{1,0:T(8,128)(2,1)S(1)} %get-tuple-element.12.in_ref, bf16[768,896]{1,0:T(8,128)(2,1)S(1)} %copy-done.2, ...), custom_call_target="tpu_custom_call" | custom-call | flops 3000000000 | bytes 2000000 | tf_op jit(solution)/shard_map/token_out/pallas_call | solution.py:318
  111.0 0.7 copy.27
  (1 shorter events, 0.0 us)
Async XLA Ops:
  7.2 9.1 %copy-start = (bf16[256,128]{1,0:T(8,128)(2,1)S(1)}, bf16[256,128]{1,0:T(8,128)(2,1)}, u32[]{:S(2)}) copy-start(bf16[256,128]{1,0:T(8,128)(2,1)} %param.25) | copy-start | bytes 196612
  7.2 100.4 %all-gather.2.cloned.1.call-start = ((), (), s32[]{:S(2)}) async-start(), calls=%async_computation.4 | async-start | bytes 1462272 | tf_op jit(solution)/shard_map/all_gather | solution.py:250
  8.0 13.5 %collective-permute-start = (bf16[48,128]{1,0:T(8,128)(2,1)S(1)}, bf16[48,128]{1,0:T(8,128)(2,1)S(1)}, u32[]{:S(2)}, u32[]{:S(2)}) collective-permute-start(bf16[48,128]{1,0:T(8,128)(2,1)S(1)} %get-tuple-element.21), channel_id=1, source_target_pairs={{0,1},{1,2},{2,3},{3,4},{4,5},{5,6},{6,7},{7,8},{8,9},{9,10},{10,1... | collective-permute-start | bytes 36872 | tf_op jit(solution)/shard_map/ppermute | solution.py:248
  11.9 9.6 %collective-permute-start.1 = (bf16[48,128]{1,0:T(8,128)(2,1)S(1)}, bf16[48,128]{1,0:T(8,128)(2,1)S(1)}, u32[]{:S(2)}, u32[]{:S(2)}) collective-permute-start(bf16[48,128]{1,0:T(8,128)(2,1)S(1)} %get-tuple-element.20), channel_id=1, source_target_pairs={{1,0},{2,1},{3,2},{4,3},{5,4},{6,5},{7,6},{8,7},{9,8},{10,9},{11,1... | collective-permute-start | bytes 36872 | tf_op jit(solution)/shard_map/ppermute | solution.py:249
  21.5 0.8 copy-start.1
  22.3 1.0 copy-start.3
  23.3 0.8 copy-start.6
  24.1 0.7 copy-start.7
  27.9 21.3 %all-to-all-start = ((bf16[16,144,128]{2,1,0:T(8,128)(2,1)}), bf16[16,144,128]{2,1,0:T(8,128)(2,1)S(1)}, u32[]{:S(2)}, u32[]{:S(2)}) async-start(bf16[16,144,128]{2,1,0:T(8,128)(2,1)} %get-tuple-element.8), calls=%async_computation | async-start | bytes 1179648 | tf_op jit(solution)/shard_map/all_to_all | solution.py:285
  37.1 12.0 %copy-start.4 = (bf16[256,768]{1,0:T(8,128)(2,1)S(1)}, bf16[256,768]{1,0:T(8,128)(2,1)}, u32[]{:S(2)}) copy-start(bf16[256,768]{1,0:T(8,128)(2,1)} %single_ref.1) | copy-start | bytes 1179652
  37.1 12.0 %copy-start.5 = (bf16[128,768]{1,0:T(8,128)(2,1)S(1)}, bf16[128,768]{1,0:T(8,128)(2,1)}, u32[]{:S(2)}) copy-start(bf16[128,768]{1,0:T(8,128)(2,1)} %agg_ref.1) | copy-start | bytes 589828
  52.2 19.3 %all-to-all-start.1 = ((bf16[8,96,256]{2,1,0:T(8,128)(2,1)}), bf16[8,96,256]{2,1,0:T(8,128)(2,1)S(1)}, u32[]{:S(2)}, u32[]{:S(2)}) async-start(bf16[8,96,256]{2,1,0:T(8,128)(2,1)} %get-tuple-element.11), calls=%async_computation.1 | async-start | bytes 786432 | tf_op jit(solution)/shard_map/all_to_all | solution.py:305
  71.5 36.1 %copy-start.8 = (s32[128]{0:T(128)S(1)}, s32[128]{0:T(128)}, u32[]{:S(2)}) copy-start(s32[128]{0:T(128)} %param.17) | copy-start | bytes 1540
  107.6 1.3 %copy-start.2 = (bf16[768,896]{1,0:T(8,128)(2,1)S(1)}, bf16[768,896]{1,0:T(8,128)(2,1)}, u32[]{:S(2)}) copy-start(bf16[768,896]{1,0:T(8,128)(2,1)} %all-gather.2.cloned.1.call-done.weights_ref) | copy-start | bytes 4128772
Sparse Core Ops, SparseCore 0:
  14.8 46.7 all-gather.1

commit v2 on v1

v2 whole, which is shorter than its diff:
```python
import functools
import math

import jax
import jax.numpy as jnp
from jax import lax
from jax.experimental import pallas as pl
from jax.experimental.pallas import tpu as pltpu
from jax.sharding import PartitionSpec as P

HEADS = 16
HEAD = 48
CA = 128
CZ = 128
ATOM_HEADS = 4
ATOM_HEAD = 32
QW = 32
KW = 128
RIM = (KW - QW) // 2
PAIR_ROWS = 32
FIRST_ROWS = 64
MIB = 2**20
DONE = jax.ShapeDtypeStruct((8, 128), jnp.float32)

epsilon = 1e-05
masked_score = -1e30
bf16 = jnp.bfloat16
f32 = jnp.float32


def dot(a, b):
    return jnp.dot(a, b, preferred_element_type=f32)


def dot_t(a, b):
    return lax.dot_general(a, b, (((1,), (1,)), ((), ())), preferred_element_type=f32)


def layer_norm(values):
    centred = values - jnp.mean(values, axis=-1, keepdims=True)
    spread = jnp.mean(centred * centred, axis=-1, keepdims=True)
    return centred * lax.rsqrt(spread + epsilon)


def params(mib=24):
    return pltpu.CompilerParams(vmem_limit_bytes=mib * MIB)


def cost(flops, moved):
    return pl.CostEstimate(flops=flops, bytes_accessed=moved, transcendentals=0)


def atom_kernel(
    _, place_ref, before_ref, own_ref, after_ref, atom_pair_ref, pair_w_ref, token_ref, w_ref, wo_ref, out_w_ref,
    back_w_ref, mid_ref, send_ref, done_ref,
):
    done_ref[...] = jnp.zeros_like(done_ref)
    device, row, last = place_ref[0], place_ref[1], place_ref[2]
    atoms = own_ref[...].astype(f32)
    count = atoms.shape[0]
    extended = jnp.concatenate(
        [before_ref[count - RIM :, :].astype(f32), atoms, after_ref[:RIM, :].astype(f32)], axis=0
    )
    norm = layer_norm(extended).astype(bf16)
    wide = w_ref[...].astype(f32)
    query_all, key_all, value_all, gate_all = [dot(norm, wide[:, m, :].astype(bf16)).astype(bf16) for m in range(4)]
    lanes = lax.broadcasted_iota(jnp.int32, (1, CA), 1) // ATOM_HEAD
    keys = lax.broadcasted_iota(jnp.int32, (1, KW), 1)
    mix = pair_w_ref[...].astype(f32)
    parts = []
    for window in range(count // QW):
        start = window * QW
        query = query_all[RIM + start : RIM + start + QW]
        query = jnp.concatenate(
            [jnp.where(lanes == head, query, jnp.zeros_like(query)) for head in range(ATOM_HEADS)], axis=0
        )
        key = key_all[start : start + KW]
        value = value_all[start : start + KW]
        planes = [atom_pair_ref[window, c].astype(f32) for c in range(atom_pair_ref.shape[1])]
        bias = []
        for head in range(ATOM_HEADS):
            total = planes[0] * mix[head : head + 1, 0:1]
            for c in range(1, len(planes)):
                total = total + planes[c] * mix[head : head + 1, c : c + 1]
            bias.append(total)
        scores = dot_t(query, key) / math.sqrt(ATOM_HEAD) + jnp.concatenate(bias, axis=0)
        position = device * count - RIM + start + keys
        scores = jnp.where((position >= 0) & (position < last), scores, masked_score)
        raised = jnp.exp(scores - jnp.max(scores, axis=-1, keepdims=True))
        weights = (raised / jnp.sum(raised, axis=-1, keepdims=True)).astype(bf16)
        mixed = dot(weights, value)
        out = jnp.zeros((QW, CA), f32)
        for head in range(ATOM_HEADS):
            out = out + jnp.where(lanes == head, mixed[head * QW : (head + 1) * QW], 0.0)
        parts.append(out)
    attended = jnp.concatenate(parts, axis=0)
    gate = gate_all[RIM : RIM + count].astype(f32)
    gated = (jax.nn.sigmoid(gate) * attended).astype(bf16)
    mid = (atoms + dot(gated, wo_ref[...])).astype(bf16)
    mid_ref[...] = mid
    local = (token_ref[...] - row).astype(f32).astype(bf16)
    tail = jnp.broadcast_to(local, (16, count))
    back_w = back_w_ref[...]
    rows, width = out_w_ref.shape
    targets = send_ref.shape[0]
    mine = width // targets
    out_w = out_w_ref[...].astype(f32)
    blank = jnp.zeros((rows, CA - mine), bf16)
    for target in range(targets):
        send_ref[target, :count, :] = mid
        send_ref[target, count : count + 16, :] = tail
        send_ref[target, count + 16 : count + 16 + rows, :] = back_w
        part = out_w[:, target * mine : (target + 1) * mine].astype(bf16)
        send_ref[target, count + 16 + rows :, :] = jnp.concatenate([part, blank], axis=1)


def pair_body(pair_ref, win_ref, wout_ref, wb_ref, out_ref, hold_ref):
    rows = pair_ref.shape[0]
    tile = pair_ref[...].reshape(rows * pair_ref.shape[1], CZ)
    centred = dot_t(centre(), tile)
    spread = jnp.sum(centred * centred, axis=0, keepdims=True) * (1.0 / CZ)
    normed = (centred * lax.rsqrt(spread + epsilon)).astype(bf16)
    both = dot(win_ref[...], normed)
    half = both.shape[0] // 2
    gate, up = both[:half], both[half:]
    hidden = ((gate * jnp.tanh(gate) + gate) * up).astype(bf16)
    renewed = centred + dot(wout_ref[...], hidden)
    spread = jnp.sum(renewed * renewed, axis=0, keepdims=True) * (1.0 / CZ)
    bias = dot(wb_ref[...], renewed.astype(bf16)) * lax.rsqrt(spread + epsilon)
    width = pair_ref.shape[1]
    for i in range(rows):
        hold_ref[:, i, :] = bias[:, i * width : (i + 1) * width]
    out_ref[...] = hold_ref[...].astype(bf16)


def centre():
    row = lax.broadcasted_iota(jnp.int32, (CZ, CZ), 0)
    column = lax.broadcasted_iota(jnp.int32, (CZ, CZ), 1)
    return (jnp.where(row == column, 1.0, 0.0) - 1.0 / CZ).astype(bf16)


def pair_first(pair_ref, trans_in_ref, trans_out_ref, wb_ref, out_ref, done_ref, win_ref, wout_ref, hold_ref):
    @pl.when(pl.program_id(0) == 0)
    def _():
        wide = trans_in_ref[...].astype(f32)
        units = wide.shape[2]
        win_ref[:units, :] = (wide[:, 0, :].T * 0.5).astype(bf16)
        win_ref[units:, :] = wide[:, 1, :].T.astype(bf16)
        wout_ref[...] = dot_t(centre(), trans_out_ref[...]).astype(bf16)

    pair_body(pair_ref, win_ref, wout_ref, wb_ref, out_ref, hold_ref)
    done_ref[...] = jnp.zeros_like(done_ref)


def pair_rest(_, __, pair_ref, win_ref, wout_ref, wb_ref, out_ref, done_ref, hold_ref):
    pair_body(pair_ref, win_ref, wout_ref, wb_ref, out_ref, hold_ref)
    done_ref[...] = jnp.zeros_like(done_ref)


def pair_call(kernel, pair, weights, start, stop, before, out_weights):
    steps = (stop - start) // PAIR_ROWS
    vmem = pl.BlockSpec(memory_space=pltpu.VMEM)
    skip = start // PAIR_ROWS
    rows, cols, _ = pair.shape
    in_specs = [pl.BlockSpec(memory_space=pl.ANY), vmem] if before else []
    in_specs += [pl.BlockSpec((PAIR_ROWS, cols, CZ), lambda i: (i + skip, 0, 0))] + [vmem] * len(weights)
    positions = (stop - start) * cols
    return pl.pallas_call(
        kernel,
        grid=(steps,),
        in_specs=in_specs,
        out_specs=[pl.BlockSpec((HEADS, PAIR_ROWS, cols), lambda i: (0, i + skip, 0))]
        + [vmem] * (1 + len(out_weights)),
        out_shape=[jax.ShapeDtypeStruct((HEADS, rows, cols), bf16), DONE, *out_weights],
        scratch_shapes=[pltpu.VMEM((HEADS, PAIR_ROWS, cols), f32)],
        input_output_aliases={0: 0} if before else {},
        compiler_params=params(56),
        cost_estimate=cost(positions * 620_000, positions * 288),
        name="pair_bias",
    )(*before, pair, *weights)


def token_kernel(
    _, got_ref, single_ref, agg_ref, w_ref, out_w_ref, in_ref, held_ref, send_ref
):
    sources, count = got_ref.shape[0], got_ref.shape[2]
    tokens = single_ref.shape[0]
    mids = jnp.concatenate([got_ref[s, :count, :] for s in range(sources)], axis=0)
    features = jnp.maximum(dot(mids, agg_ref[...]), 0.0).astype(bf16)
    token = lax.broadcasted_iota(jnp.int32, (tokens, count), 0).astype(f32)
    onehot = jnp.concatenate(
        [
            jnp.where(token == got_ref[s, count : count + 16, :].astype(f32)[:1], 1.0, 0.0)
            for s in range(sources)
        ],
        axis=1,
    )
    token_count = jnp.sum(onehot, axis=1, keepdims=True)
    token_sum = dot(onehot.astype(bf16), features)
    token_in = (single_ref[...].astype(f32) + token_sum / token_count).astype(bf16)
    in_ref[...] = token_in
    norm = layer_norm(token_in.astype(f32)).astype(bf16)
    turned = dot_t(w_ref[...], norm).astype(bf16)
    held_ref[:, :tokens] = turned[:HEAD]
    held_ref[:, tokens : 2 * tokens] = turned[3 * HEAD :]
    send_ref[...] = turned[HEAD : 3 * HEAD]
    rows = out_w_ref.shape[0]
    back_w = jnp.concatenate(
        [got_ref[s, count + 16 : count + 16 + rows, :] for s in range(sources)], axis=0
    )
    held_ref[:, 2 * tokens :] = dot(out_w_ref[...], back_w).astype(bf16)


def attention_kernel(place_ref, held_ref, bias_ref, *refs):
    *kv_refs, send_ref, done_ref = refs
    done_ref[...] = jnp.zeros_like(done_ref)
    rows = len(kv_refs)
    tokens = kv_refs[0].shape[1]
    query = held_ref[:, :tokens].astype(f32).T.astype(bf16)
    per = bias_ref.shape[0] // rows
    scores = []
    for step, kv_ref in enumerate(kv_refs):
        source = lax.rem(place_ref[4] + rows - step, rows) * per
        bias = jnp.concatenate([bias_ref[source + k].astype(f32) for k in range(per)], axis=1)
        scores.append(dot(query, kv_ref[:HEAD, :]) / math.sqrt(HEAD) + bias)
    scores = jnp.concatenate(scores, axis=1)
    raised = jnp.exp(scores - jnp.max(scores, axis=-1, keepdims=True))
    weights = (raised / jnp.sum(raised, axis=-1, keepdims=True)).astype(bf16)
    values = jnp.concatenate([kv_ref[HEAD:, :] for kv_ref in kv_refs], axis=1)
    attended = dot_t(values, weights)
    gate = held_ref[:, tokens : 2 * tokens].astype(f32)
    gated = (jax.nn.sigmoid(gate) * attended).astype(bf16)
    back = held_ref[:, 2 * tokens :]
    for target in range(send_ref.shape[0]):
        send_ref[target, :, :tokens] = gated
        send_ref[target, :, tokens:] = back


def ready_kernel(_, place_ref, got_ref, in_ref, token_ref, out_w_ref, own_ref, back_ref, onehot_ref):
    sources, count = got_ref.shape[0], got_ref.shape[2]
    tokens, width = in_ref.shape
    mine = width // sources
    token_in = in_ref[...]
    start = count + 16
    back_w = jnp.concatenate([got_ref[s, start : start + mine, :] for s in range(sources)], axis=0)
    out_w = jnp.concatenate([got_ref[s, start + mine :, :] for s in range(sources)], axis=0)
    out_w_ref[...] = out_w.astype(f32).T[:mine].astype(bf16)
    back_ref[...] = dot_t(back_w.astype(f32).T.astype(bf16), token_in)
    wanted = lax.broadcasted_iota(jnp.int32, (mine, width), 0) + place_ref[3] * mine
    column = lax.broadcasted_iota(jnp.int32, (mine, width), 1)
    own_ref[...] = dot_t(jnp.where(column == wanted, 1.0, 0.0).astype(bf16), token_in)
    token = lax.broadcasted_iota(jnp.int32, (tokens, count), 0)
    onehot = jnp.where(token == token_ref[...] - place_ref[1], 1.0, 0.0)
    onehot_ref[...] = onehot.T.astype(bf16)


def final_kernel(got_ref, out_w_ref, own_ref, back_ref, onehot_ref, mid_ref, single_ref, atoms_ref):
    heads, head, _ = got_ref.shape
    tokens = own_ref.shape[1]
    gated = got_ref[:, :, :tokens].reshape(heads * head, tokens)
    mixed = got_ref[:, :, tokens:].reshape(heads * head, CA)
    single_ref[...] = (own_ref[...] + dot(out_w_ref[...], gated)).astype(bf16)
    back = (back_ref[...] + dot(mixed.astype(f32).T.astype(bf16), gated)).astype(bf16)
    picked = dot_t(onehot_ref[...], back)
    atoms_ref[...] = (mid_ref[...].astype(f32) + picked).astype(bf16)


def shape(*sizes, dtype=bf16):
    return jax.ShapeDtypeStruct(sizes, dtype)


def single_step(kernel, name, in_specs, out_shape, flops, moved, operands):
    return pl.pallas_call(
        kernel,
        in_specs=in_specs,
        out_specs=[pl.BlockSpec(memory_space=pltpu.VMEM)] * len(out_shape),
        out_shape=out_shape,
        compiler_params=params(),
        cost_estimate=cost(flops, moved),
        name=name,
    )(*operands)


def gathered(copies, axis):
    return lax.all_to_all(copies, axis, split_axis=0, concat_axis=0, tiled=True)


def body(
    atoms,
    atom_pair,
    atom_token,
    single,
    pair,
    atom_w,
    atom_pair_w,
    atom_wo,
    agg_w,
    trans_in,
    trans_out,
    bias_w,
    token_w,
    token_wo,
    back_w,
):
    row_size, col_size = lax.axis_size("row"), lax.axis_size("col")
    count = atoms.shape[0]
    query_rows, width = single.shape
    head_rows = token_wo.shape[0]
    both = ("row", "col")
    devices = row_size * col_size
    up = [(i, i + 1) for i in range(devices - 1)]
    down = [(j, i) for i, j in up]
    before = lax.ppermute(atoms, both, up)
    after = lax.ppermute(atoms, both, down)

    device = lax.axis_index(both)
    place = jnp.stack(
        [
            device,
            lax.axis_index("row") * query_rows,
            jnp.asarray(count * devices, device.dtype),
            lax.axis_index("col"),
            lax.axis_index("row"),
        ]
    ).astype(jnp.int32)
    smem = pl.BlockSpec(memory_space=pltpu.SMEM)
    vmem = pl.BlockSpec(memory_space=pltpu.VMEM)
    token_row = atom_token.reshape(1, count)

    units = trans_in.shape[2]
    bias, done, win, wout = pair_call(
        pair_first, pair, (trans_in, trans_out, bias_w.T), 0, FIRST_ROWS, (),
        (shape(2 * units, CZ), shape(CZ, units)),
    )
    mid, mid_send, done = single_step(
        atom_kernel,
        "atom_stage",
        [vmem, smem] + [vmem] * 10,
        [shape(count, CA), shape(col_size, count + 16 + 2 * head_rows, CA), DONE],
        4_000_000_000,
        2_000_000,
        (
            done, place, before, atoms, after, atom_pair, atom_pair_w.T, token_row, atom_w, atom_wo, token_wo, back_w,
        ),
    )
    mids = gathered(mid_send, "col")
    bias, done = pair_call(pair_rest, pair, (win, wout, bias_w.T), FIRST_ROWS, query_rows, (bias, done), ())
    bias_rows = gathered(bias, "col")

    turned = jnp.transpose(token_w, (1, 2, 0)).reshape(4 * HEAD, width)
    token_in, held, kv_send = single_step(
        token_kernel,
        "token_stage",
        [vmem] * 6,
        [
            shape(query_rows, width),
            shape(HEAD, 2 * query_rows + CA),
            shape(2 * HEAD, query_rows),
        ],
        4_000_000_000,
        2_000_000,
        (done, mids, single, agg_w, turned, token_wo),
    )
    kv = [kv_send] + [
        lax.ppermute(kv_send, "row", [(i, (i + step) % row_size) for i in range(row_size)])
        for step in range(1, row_size)
    ]
    gated_send, done = single_step(
        attention_kernel,
        "token_attention",
        [smem] + [vmem] * (2 + row_size),
        [shape(col_size, HEAD, query_rows + CA), DONE],
        3_000_000_000,
        2_000_000,
        (place, held, bias_rows, *kv),
    )
    gated = gathered(gated_send, "col")
    out_w, own, back, onehot = single_step(
        ready_kernel,
        "out_ready",
        [vmem, smem] + [vmem] * 3,
        [
            shape(width // col_size, width),
            shape(width // col_size, query_rows, dtype=f32),
            shape(CA, query_rows, dtype=f32),
            shape(count, query_rows),
        ],
        2_000_000_000,
        2_000_000,
        (done, place, mids, token_in, token_row),
    )
    single_out, atoms_out = single_step(
        final_kernel,
        "token_out",
        [vmem] * 6,
        [shape(width // col_size, query_rows), shape(count, CA)],
        2_000_000_000,
        2_000_000,
        (gated, out_w, own, back, onehot, mid),
    )
    return single_out.T, atoms_out


def solution(mesh):
    in_specs = (
        P(("row", "col"), None),
        P(("row", "col"), None, None, None),
        P(("row", "col")),
        P("row", None),
        P("row", "col", None),
        P(),
        P(),
        P(),
        P(),
        P(),
        P(),
        P(),
        P(None, None, "col"),
        P("col", None),
        P("col", None),
    )
    out_specs = (P("row", "col"), P(("row", "col"), None))
    return jax.shard_map(body, mesh=mesh, in_specs=in_specs, out_specs=out_specs, check_vma=False)
```

time: 120 us -> 87.4 us (0.73)
  blocking collectives: 34.4 us -> 0 us
  waiting for transfers between devices: 5.78 us -> 20.1 us
  starting transfers between devices: 18.3 us -> 32.1 us
  between operations: 14.2 us -> 0.89 us
  local copies, waits for them, and re-layouts: 11.2 us -> 1.5 us
  other arithmetic: 2.93 us -> 0 us
  Pallas kernels: 31 us -> 32.3 us
    all_to_all x2 -> x0, blocking collectives: 34.4 us -> none  [the longest x1 21.7 us: body(): lax.all_to_all(bias, 'col', split_axis=0, concat_axis=0, tiled=True)]
    all_to_all x2 -> x3, waiting for transfers between devices: 5.76 us -> 14.9 us  [gathered(): return lax.all_to_all(copies, axis, split_axis=0, concat_axis=0, tiled=True)]
    ppermute x2 -> x9, starting transfers between devices: 5.19 us -> 13 us  [the longest x7 7.84 us: body(): lax.ppermute(kv_send, 'row', [(i, (i + step) % row_size) for i in range(r...]
    all_to_all x2 -> x3, starting transfers between devices: 13.1 us -> 19.1 us  [gathered(): return lax.all_to_all(copies, axis, split_axis=0, concat_axis=0, tiled=True)]
    ppermute x2 -> x9, waiting for transfers between devices: 0.01 us -> 5.2 us  [the longest x7 5.2 us: body(): lax.ppermute(kv_send, 'row', [(i, (i + step) % row_size) for i in range(r...]
    unnamed x22 -> x28, local copies, waits for them, and re-layouts: 5.93 us -> 1.42 us
    slice x4 -> x0, local copies, waits for them, and re-layouts: 3.78 us -> none  [the longest x1 1.21 us: body(): trans_in[:, 0, :] * half]
    concatenate x1 -> x0, other arithmetic: 1.54 us -> none  [body(): jnp.concatenate([token_wo, back_w], axis=1)]
  transfers between devices with their start and end apart: 5 -> 12, of which waited for: 1 -> 7; matrix products, arithmetic and copies ran while one was open for 7% -> 0% of each run, Pallas kernels for 24% -> 29%
where the time goes in v2:
time: 87.4 us; the launch traced here: 86.9 us
  Pallas kernels  32.3 us (37%)
  starting transfers between devices  32.1 us (37%)
  waiting for transfers between devices  20.1 us (23%)
  local copies, waits for them, and re-layouts  1.5 us (2%)
  between operations  0.89 us (1%)
    pallas_call x2, Pallas kernels, pair_call(): pl.pallas_call(kernel, grid=(steps,), in_specs=in_specs, out_specs=[pl.Bl...  21.4 us
    all_to_all x3, starting transfers between devices, gathered(): return lax.all_to_all(copies, axis, split_axis=0, concat_axis=0, tiled=True)  19.1 us
    all_to_all x3, waiting for transfers between devices, gathered(): return lax.all_to_all(copies, axis, split_axis=0, concat_axis=0, tiled=True)  14.9 us
    pallas_call x5, Pallas kernels, single_step(): pl.pallas_call(kernel, in_specs=in_specs, out_specs=[pl.BlockSpec(memory_...  10.8 us
    ppermute x7, starting transfers between devices, body(): lax.ppermute(kv_send, 'row', [(i, (i + step) % row_size) for i in range(r...  7.84 us
    ppermute x7, waiting for transfers between devices, body(): lax.ppermute(kv_send, 'row', [(i, (i + step) % row_size) for i in range(r...  5.2 us
    ppermute x1, starting transfers between devices, body(): before = lax.ppermute(atoms, both, up)  3.91 us
  transfers between devices with their start and end apart: 12, of which 7 were waited for; matrix products, arithmetic and copies ran while one was open for 0% of the time, Pallas kernels for 29%

profile of v2, /device:TPU:0, one launch (start us, length us, event | category | flops | bytes accessed | tf_op | source)
XLA Modules:
  0.0 86.9 jit_solution(15760317005836815238)
XLA Ops:
  0.6 3.9 %collective-permute-start = (bf16[128,128]{1,0:T(8,128)(2,1)}, bf16[128,128]{1,0:T(8,128)(2,1)S(1)}, u32[]{:S(2)}, u32[]{:S(2)}) collective-permute-start(bf16[128,128]{1,0:T(8,128)(2,1)} %own_ref.1), channel_id=1, source_target_pairs={{0,1},{1,2},{2,3},{3,4},{4,5},{5,6},{6,7},{7,8},{8,9},{9,10},{10,1... | collective-permute-start | bytes 98312 | tf_op jit(solution)/shard_map/ppermute | solution.py:313
  4.5 1.3 %collective-permute-start.1 = (bf16[128,128]{1,0:T(8,128)(2,1)}, bf16[128,128]{1,0:T(8,128)(2,1)S(1)}, u32[]{:S(2)}, u32[]{:S(2)}) collective-permute-start(bf16[128,128]{1,0:T(8,128)(2,1)} %own_ref.1), channel_id=1, source_target_pairs={{1,0},{2,1},{3,2},{4,3},{5,4},{6,5},{7,6},{8,7},{9,8},{10,9},{11,1... | collective-permute-start | bytes 98312 | tf_op jit(solution)/shard_map/ppermute | solution.py:314
  5.8 0.0 copy-start
  5.9 0.0 copy-start.4
  5.9 0.0 copy-start.5
  5.9 0.0 copy-start.6
  5.9 0.0 copy-start.7
  5.9 0.0 copy-start.8
  5.9 0.0 copy-start.9
  5.9 0.0 copy-start.10
  5.9 6.6 %pair_bias.2 = (bf16[16,256,128]{2,1,0:T(8,128)(2,1)}, f32[8,128]{1,0:T(8,128)}, bf16[512,128]{1,0:T(8,128)(2,1)}, bf16[128,256]{1,0:T(8,128)(2,1)}) custom-call(bf16[256,128,128]{2,1,0:T(8,128)(2,1)} %pair_ref.3, bf16[128,2,256]{2,1,0:T(2,128)(2,1)} %trans_in_ref.1, bf16[256,128]{1,0:T(8,128)(2,1)} %trans_out_ref.1, bf16[16,128]{1,0:T(8,128)(2,1)} %bitcast.15), custom_call_target="tpu_custom_call" | custom-call | flops 5079040000 | bytes 2359296 | tf_op jit(solution)/shard_map/pair_bias/pallas_call | solution.py:168
  12.5 0.1 stack.19.place_ref
  12.6 0.0 collective-permute-done.before_ref
  12.6 0.0 collective-permute-done.1.after_ref
  12.6 0.0 copy-done
  12.6 0.0 copy-done.4
  12.6 0.0 copy-done.5
  12.6 0.0 copy-done.6
  12.6 0.0 copy-done.7
  12.6 0.0 copy-done.8
  12.6 0.0 copy-done.9
  12.6 0.0 copy-done.10
  12.6 0.0 copy-start.11
  12.7 0.7 copy-done.11
  13.3 3.4 %atom_stage.1 = (bf16[128,128]{1,0:T(8,128)(2,1)S(1)}, bf16[16,240,128]{2,1,0:T(8,128)(2,1)}, f32[8,128]{1,0:T(8,128)S(1)}) custom-call(f32[8,128]{1,0:T(8,128)S(1)} %copy-done.11, s32[5]{0:T(128)S(1)} %stack.19.place_ref, bf16[128,128]{1,0:T(8,128)(2,1)S(1)} %collective-permute-done.before_ref, bf16[128,128]{1,0:T(8,128)(2,1)S(1)} %copy-done.6, ...), custom_call_target="tpu_custom_call" | custom-call | flops 4000000000 | bytes 2000000 | tf_op jit(solution)/shard_map/atom_stage/pallas_call | solution.py:273
  16.7 0.0 copy-start.13
  16.7 8.6 %all-to-all-start = ((bf16[16,240,128]{2,1,0:T(8,128)(2,1)}), bf16[16,240,128]{2,1,0:T(8,128)(2,1)S(1)}, u32[]{:S(2)}, u32[]{:S(2)}) async-start(bf16[16,240,128]{2,1,0:T(8,128)(2,1)} %get-tuple-element.28), calls=%async_computation | async-start | bytes 1966080 | tf_op jit(solution)/shard_map/all_to_all | solution.py:285
  25.3 0.0 copy-done.13
  25.3 0.0 copy-start.1
  25.3 0.0 copy-start.2
  25.4 0.0 copy-start.3
  25.4 14.9 %pair_bias.3 = (bf16[16,256,128]{2,1,0:T(8,128)(2,1)}, f32[8,128]{1,0:T(8,128)}) custom-call(bf16[16,256,128]{2,1,0:T(8,128)(2,1)} %get-tuple-element.22._, f32[8,128]{1,0:T(8,128)} %copy-done.13, bf16[256,128,128]{2,1,0:T(8,128)(2,1)} %pair_ref.3, bf16[512,128]{1,0:T(8,128)(2,1)} %get-tuple-element.25.win_ref, ...), custom_call_target="tpu_custom_call", output_to_operand_aliasing={{0}: (0, {})} | custom-call | flops 15237120000 | bytes 7077888 | tf_op jit(solution)/shard_map/pair_bias/pallas_call | solution.py:168
  40.3 2.5 %all-to-all-done.got_ref = bf16[16,240,128]{2,1,0:T(8,128)(2,1)S(1)} async-done(((bf16[16,240,128]{2,1,0:T(8,128)(2,1)}), bf16[16,240,128]{2,1,0:T(8,128)(2,1)S(1)}, u32[]{:S(2)}, u32[]{:S(2)}) %all-to-all-start) | async-done | bytes 983072 | tf_op jit(solution)/shard_map/all_to_all | solution.py:285
  42.8 4.7 %all-to-all-start.1 = ((bf16[16,256,128]{2,1,0:T(8,128)(2,1)}), bf16[16,256,128]{2,1,0:T(8,128)(2,1)S(1)}, u32[]{:S(2)}, u32[]{:S(2)}) async-start(bf16[16,256,128]{2,1,0:T(8,128)(2,1)} %get-tuple-element.30), calls=%async_computation.1 | async-start | bytes 2097152 | tf_op jit(solution)/shard_map/all_to_all | solution.py:285
  47.5 0.0 copy-done.1
  47.5 0.0 copy-done.2
  47.5 0.0 copy-done.3
  47.5 0.0 copy-start.12
  47.5 0.7 copy-done.12
  48.2 2.4 %token_stage.1 = (bf16[256,768]{1,0:T(8,128)(2,1)S(1)}, bf16[48,640]{1,0:T(8,128)(2,1)S(1)}, bf16[96,256]{1,0:T(8,128)(2,1)S(1)}) custom-call(f32[8,128]{1,0:T(8,128)S(1)} %copy-done.12, bf16[16,240,128]{2,1,0:T(8,128)(2,1)S(1)} %all-to-all-done.got_ref, bf16[256,768]{1,0:T(8,128)(2,1)S(1)} %copy-done.1, bf16[128,768]{1,0:T(8,128)(2,1)S(1)} %copy-done.3, ...), custom_call_target="tpu_custom_call" | custom-call | flops 4000000000 | bytes 2000000 | tf_op jit(solution)/shard_map/token_stage/pallas_call | solution.py:273
  50.6 2.1 %collective-permute-start.8 = (bf16[96,256]{1,0:T(8,128)(2,1)S(1)}, bf16[96,256]{1,0:T(8,128)(2,1)S(1)}, u32[]{:S(2)}, u32[]{:S(2)}) collective-permute-start(bf16[96,256]{1,0:T(8,128)(2,1)S(1)} %get-tuple-element.31.refs_0_), channel_id=1, source_target_pairs={{0,112},{16,0},{32,16},{48,32},{64,48},{80,64},{96,80},{112,96},{1... | collective-permute-start | bytes 147464 | tf_op jit(solution)/shard_map/ppermute | solution.py:365
  52.8 1.0 %collective-permute-start.7 = (bf16[96,256]{1,0:T(8,128)(2,1)S(1)}, bf16[96,256]{1,0:T(8,128)(2,1)S(1)}, u32[]{:S(2)}, u32[]{:S(2)}) collective-permute-start(bf16[96,256]{1,0:T(8,128)(2,1)S(1)} %get-tuple-element.31.refs_0_), channel_id=1, source_target_pairs={{0,96},{16,112},{32,0},{48,16},{64,32},{80,48},{96,64},{112,80},{1... | collective-permute-start | bytes 147464 | tf_op jit(solution)/shard_map/ppermute | solution.py:365
  53.8 0.4 collective-permute-start.6
  54.2 2.9 %collective-permute-start.5 = (bf16[96,256]{1,0:T(8,128)(2,1)S(1)}, bf16[96,256]{1,0:T(8,128)(2,1)S(1)}, u32[]{:S(2)}, u32[]{:S(2)}) collective-permute-start(bf16[96,256]{1,0:T(8,128)(2,1)S(1)} %get-tuple-element.31.refs_0_), channel_id=1, source_target_pairs={{0,64},{16,80},{32,96},{48,112},{64,0},{80,16},{96,32},{112,48},{1... | collective-permute-start | bytes 147464 | tf_op jit(solution)/shard_map/ppermute | solution.py:365
  57.1 0.0 collective-permute-start.4
  57.1 0.0 collective-permute-done.8.refs_7_
  57.1 0.4 collective-permute-start.3
  57.4 0.0 collective-permute-done.7.refs_6_
  57.4 1.1 %collective-permute-start.2 = (bf16[96,256]{1,0:T(8,128)(2,1)S(1)}, bf16[96,256]{1,0:T(8,128)(2,1)S(1)}, u32[]{:S(2)}, u32[]{:S(2)}) collective-permute-start(bf16[96,256]{1,0:T(8,128)(2,1)S(1)} %get-tuple-element.31.refs_0_), channel_id=1, source_target_pairs={{0,16},{16,32},{32,48},{48,64},{64,80},{80,96},{96,112},{112,0},{1... | collective-permute-start | bytes 147464 | tf_op jit(solution)/shard_map/ppermute | solution.py:365
  58.5 0.0 collective-permute-done.6.refs_5_
  58.5 1.7 %collective-permute-done.5.refs_4_ = bf16[96,256]{1,0:T(8,128)(2,1)S(1)} collective-permute-done((bf16[96,256]{1,0:T(8,128)(2,1)S(1)}, bf16[96,256]{1,0:T(8,128)(2,1)S(1)}, u32[]{:S(2)}, u32[]{:S(2)}) %collective-permute-start.5) | collective-permute-done | bytes 49184 | tf_op jit(solution)/shard_map/ppermute | solution.py:365
  60.2 2.0 %collective-permute-done.4.refs_3_ = bf16[96,256]{1,0:T(8,128)(2,1)S(1)} collective-permute-done((bf16[96,256]{1,0:T(8,128)(2,1)S(1)}, bf16[96,256]{1,0:T(8,128)(2,1)S(1)}, u32[]{:S(2)}, u32[]{:S(2)}) %collective-permute-start.4) | collective-permute-done | bytes 49184 | tf_op jit(solution)/shard_map/ppermute | solution.py:365
  62.2 1.0 %collective-permute-done.3.refs_2_ = bf16[96,256]{1,0:T(8,128)(2,1)S(1)} collective-permute-done((bf16[96,256]{1,0:T(8,128)(2,1)S(1)}, bf16[96,256]{1,0:T(8,128)(2,1)S(1)}, u32[]{:S(2)}, u32[]{:S(2)}) %collective-permute-start.3) | collective-permute-done | bytes 49184 | tf_op jit(solution)/shard_map/ppermute | solution.py:365
  63.2 0.5 collective-permute-done.2.refs_1_
  63.7 1.4 %all-to-all-done.1.bias_ref = bf16[16,256,128]{2,1,0:T(8,128)(2,1)S(1)} async-done(((bf16[16,256,128]{2,1,0:T(8,128)(2,1)}), bf16[16,256,128]{2,1,0:T(8,128)(2,1)S(1)}, u32[]{:S(2)}, u32[]{:S(2)}) %all-to-all-start.1) | async-done | bytes 1048608 | tf_op jit(solution)/shard_map/all_to_all | solution.py:285
  65.1 3.0 %token_attention.1 = (bf16[16,48,384]{2,1,0:T(8,128)(2,1)}, f32[8,128]{1,0:T(8,128)S(1)}) custom-call(s32[5]{0:T(128)S(1)} %stack.19.place_ref, bf16[48,640]{1,0:T(8,128)(2,1)S(1)} %get-tuple-element.29.held_ref, bf16[16,256,128]{2,1,0:T(8,128)(2,1)S(1)} %all-to-all-done.1.bias_ref, bf16[96,256]{1,0:T(8,128)(2,1)S(1)} %get-tuple-element.31.refs_0_, ...), custom_call_target="tpu_custom_call" | custom-call | flops 3000000000 | bytes 2000000 | tf_op jit(solution)/shard_map/token_attention/pallas_call | solution.py:273
  68.1 5.8 %all-to-all-start.2 = ((bf16[16,48,384]{2,1,0:T(8,128)(2,1)}), bf16[16,48,384]{2,1,0:T(8,128)(2,1)S(1)}, u32[]{:S(2)}, u32[]{:S(2)}) async-start(bf16[16,48,384]{2,1,0:T(8,128)(2,1)} %get-tuple-element.32), calls=%async_computation.2 | async-start | bytes 1179648 | tf_op jit(solution)/shard_map/all_to_all | solution.py:285
  73.9 0.9 %out_ready.1 = (bf16[48,768]{1,0:T(8,128)(2,1)S(1)}, f32[48,256]{1,0:T(8,128)S(1)}, f32[128,256]{1,0:T(8,128)S(1)}, bf16[128,256]{1,0:T(8,128)(2,1)S(1)}) custom-call(f32[8,128]{1,0:T(8,128)S(1)} %get-tuple-element.33._, s32[5]{0:T(128)S(1)} %stack.19.place_ref, bf16[16,240,128]{2,1,0:T(8,128)(2,1)S(1)} %all-to-all-done.got_ref, ...), custom_call_target="tpu_custom_call" | custom-call | flops 2000000000 | bytes 2000000 | tf_op jit(solution)/shard_map/out_ready/pallas_call | solution.py:273
  74.8 11.0 %all-to-all-done.2.got_ref = bf16[16,48,384]{2,1,0:T(8,128)(2,1)S(1)} async-done(((bf16[16,48,384]{2,1,0:T(8,128)(2,1)}), bf16[16,48,384]{2,1,0:T(8,128)(2,1)S(1)}, u32[]{:S(2)}, u32[]{:S(2)}) %all-to-all-start.2) | async-done | bytes 589856 | tf_op jit(solution)/shard_map/all_to_all | solution.py:285
  85.8 1.1 %token_out.1 = (bf16[48,256]{1,0:T(8,128)(2,1)}, bf16[128,128]{1,0:T(8,128)(2,1)}) custom-call(bf16[16,48,384]{2,1,0:T(8,128)(2,1)S(1)} %all-to-all-done.2.got_ref, bf16[48,768]{1,0:T(8,128)(2,1)S(1)} %get-tuple-element.35.out_w_ref, f32[48,256]{1,0:T(8,128)S(1)} %get-tuple-element.36.own_ref, f32[128,256]{1,0:T(8,128)S(1)} %get-tuple-element.37.back_ref, ...), custom_call_target="tpu_custom_call" | custom-call | flops 2000000000 | bytes 2000000 | tf_op jit(solution)/shard_map/token_out/pallas_call | solution.py:273
Async XLA Ops:
  0.6 11.9 %collective-permute-start = (bf16[128,128]{1,0:T(8,128)(2,1)}, bf16[128,128]{1,0:T(8,128)(2,1)S(1)}, u32[]{:S(2)}, u32[]{:S(2)}) collective-permute-start(bf16[128,128]{1,0:T(8,128)(2,1)} %own_ref.1), channel_id=1, source_target_pairs={{0,1},{1,2},{2,3},{3,4},{4,5},{5,6},{6,7},{7,8},{8,9},{9,10},{10,1... | collective-permute-start | bytes 98312 | tf_op jit(solution)/shard_map/ppermute | solution.py:313
  4.5 8.0 %collective-permute-start.1 = (bf16[128,128]{1,0:T(8,128)(2,1)}, bf16[128,128]{1,0:T(8,128)(2,1)S(1)}, u32[]{:S(2)}, u32[]{:S(2)}) collective-permute-start(bf16[128,128]{1,0:T(8,128)(2,1)} %own_ref.1), channel_id=1, source_target_pairs={{1,0},{2,1},{3,2},{4,3},{5,4},{6,5},{7,6},{8,7},{9,8},{10,9},{11,1... | collective-permute-start | bytes 98312 | tf_op jit(solution)/shard_map/ppermute | solution.py:314
  5.8 6.7 %copy-start = (bf16[4,16,32,128]{3,2,1,0:T(8,128)(2,1)S(1)}, bf16[4,16,32,128]{3,2,1,0:T(8,128)(2,1)}, u32[]{:S(2)}) copy-start(bf16[4,16,32,128]{3,2,1,0:T(8,128)(2,1)} %atom_pair_ref.1) | copy-start | bytes 1572868
  5.9 6.7 %copy-start.4 = (bf16[128,4,128]{2,1,0:T(4,128)(2,1)S(1)}, bf16[128,4,128]{2,1,0:T(4,128)(2,1)}, u32[]{:S(2)}) copy-start(bf16[128,4,128]{2,1,0:T(4,128)(2,1)} %w_ref.1) | copy-start | bytes 393220
  5.9 6.7 %copy-start.5 = (bf16[48,768]{1,0:T(8,128)(2,1)S(1)}, bf16[48,768]{1,0:T(8,128)(2,1)}, u32[]{:S(2)}) copy-start(bf16[48,768]{1,0:T(8,128)(2,1)} %out_w_ref.3) | copy-start | bytes 221188
  5.9 6.7 %copy-start.6 = (bf16[128,128]{1,0:T(8,128)(2,1)S(1)}, bf16[128,128]{1,0:T(8,128)(2,1)}, u32[]{:S(2)}) copy-start(bf16[128,128]{1,0:T(8,128)(2,1)} %own_ref.1) | copy-start | bytes 98308
  5.9 6.7 %copy-start.7 = (bf16[128,128]{1,0:T(8,128)(2,1)S(1)}, bf16[128,128]{1,0:T(8,128)(2,1)}, u32[]{:S(2)}) copy-start(bf16[128,128]{1,0:T(8,128)(2,1)} %wo_ref.1) | copy-start | bytes 98308
  5.9 6.7 %copy-start.8 = (bf16[48,128]{1,0:T(8,128)(2,1)S(1)}, bf16[48,128]{1,0:T(8,128)(2,1)}, u32[]{:S(2)}) copy-start(bf16[48,128]{1,0:T(8,128)(2,1)} %back_w_ref.1) | copy-start | bytes 36868
  5.9 6.7 %copy-start.9 = (bf16[16,4]{0,1:T(4,128)(2,1)S(1)}, bf16[16,4]{0,1:T(4,128)(2,1)}, u32[]{:S(2)}) copy-start(bf16[16,4]{0,1:T(4,128)(2,1)} %param.21) | copy-start | bytes 388
  5.9 6.7 %copy-start.10 = (s32[128]{0:T(128)S(1)}, s32[128]{0:T(128)}, u32[]{:S(2)}) copy-start(s32[128]{0:T(128)} %param.17) | copy-start | bytes 1540
  12.6 0.7 copy-start.11
  16.7 8.6 %copy-start.13 = (f32[8,128]{1,0:T(8,128)}, f32[8,128]{1,0:T(8,128)S(1)}, u32[]{:S(2)}) copy-start(f32[8,128]{1,0:T(8,128)S(1)} %get-tuple-element.24.__) | copy-start | bytes 12292
  16.7 26.1 %all-to-all-start = ((bf16[16,240,128]{2,1,0:T(8,128)(2,1)}), bf16[16,240,128]{2,1,0:T(8,128)(2,1)S(1)}, u32[]{:S(2)}, u32[]{:S(2)}) async-start(bf16[16,240,128]{2,1,0:T(8,128)(2,1)} %get-tuple-element.28), calls=%async_computation | async-start | bytes 1966080 | tf_op jit(solution)/shard_map/all_to_all | solution.py:285
  25.3 22.2 %copy-start.1 = (bf16[256,768]{1,0:T(8,128)(2,1)S(1)}, bf16[256,768]{1,0:T(8,128)(2,1)}, u32[]{:S(2)}) copy-start(bf16[256,768]{1,0:T(8,128)(2,1)} %single_ref.1) | copy-start | bytes 1179652
  25.3 22.2 %copy-start.2 = (bf16[768,4,48]{0,2,1:T(8,128)(2,1)S(1)}, bf16[768,4,48]{0,2,1:T(8,128)(2,1)}, u32[]{:S(2)}) copy-start(bf16[768,4,48]{0,2,1:T(8,128)(2,1)} %param.27) | copy-start | bytes 884740
  25.4 22.2 %copy-start.3 = (bf16[128,768]{1,0:T(8,128)(2,1)S(1)}, bf16[128,768]{1,0:T(8,128)(2,1)}, u32[]{:S(2)}) copy-start(bf16[128,768]{1,0:T(8,128)(2,1)} %agg_ref.1) | copy-start | bytes 589828
  42.8 22.3 %all-to-all-start.1 = ((bf16[16,256,128]{2,1,0:T(8,128)(2,1)}), bf16[16,256,128]{2,1,0:T(8,128)(2,1)S(1)}, u32[]{:S(2)}, u32[]{:S(2)}) async-start(bf16[16,256,128]{2,1,0:T(8,128)(2,1)} %get-tuple-element.30), calls=%async_computation.1 | async-start | bytes 2097152 | tf_op jit(solution)/shard_map/all_to_all | solution.py:285
  47.5 0.7 copy-start.12
  50.6 6.4 %collective-permute-start.8 = (bf16[96,256]{1,0:T(8,128)(2,1)S(1)}, bf16[96,256]{1,0:T(8,128)(2,1)S(1)}, u32[]{:S(2)}, u32[]{:S(2)}) collective-permute-start(bf16[96,256]{1,0:T(8,128)(2,1)S(1)} %get-tuple-element.31.refs_0_), channel_id=1, source_target_pairs={{0,112},{16,0},{32,16},{48,32},{64,48},{80,64},{96,80},{112,96},{1... | collective-permute-start | bytes 147464 | tf_op jit(solution)/shard_map/ppermute | solution.py:365
  52.8 4.7 %collective-permute-start.7 = (bf16[96,256]{1,0:T(8,128)(2,1)S(1)}, bf16[96,256]{1,0:T(8,128)(2,1)S(1)}, u32[]{:S(2)}, u32[]{:S(2)}) collective-permute-start(bf16[96,256]{1,0:T(8,128)(2,1)S(1)} %get-tuple-element.31.refs_0_), channel_id=1, source_target_pairs={{0,96},{16,112},{32,0},{48,16},{64,32},{80,48},{96,64},{112,80},{1... | collective-permute-start | bytes 147464 | tf_op jit(solution)/shard_map/ppermute | solution.py:365
  53.8 4.7 %collective-permute-start.6 = (bf16[96,256]{1,0:T(8,128)(2,1)S(1)}, bf16[96,256]{1,0:T(8,128)(2,1)S(1)}, u32[]{:S(2)}, u32[]{:S(2)}) collective-permute-start(bf16[96,256]{1,0:T(8,128)(2,1)S(1)} %get-tuple-element.31.refs_0_), channel_id=1, source_target_pairs={{0,80},{16,96},{32,112},{48,0},{64,16},{80,32},{96,48},{112,64},{1... | collective-permute-start | bytes 147464 | tf_op jit(solution)/shard_map/ppermute | solution.py:365
  54.2 6.0 %collective-permute-start.5 = (bf16[96,256]{1,0:T(8,128)(2,1)S(1)}, bf16[96,256]{1,0:T(8,128)(2,1)S(1)}, u32[]{:S(2)}, u32[]{:S(2)}) collective-permute-start(bf16[96,256]{1,0:T(8,128)(2,1)S(1)} %get-tuple-element.31.refs_0_), channel_id=1, source_target_pairs={{0,64},{16,80},{32,96},{48,112},{64,0},{80,16},{96,32},{112,48},{1... | collective-permute-start | bytes 147464 | tf_op jit(solution)/shard_map/ppermute | solution.py:365
  57.1 5.1 %collective-permute-start.4 = (bf16[96,256]{1,0:T(8,128)(2,1)S(1)}, bf16[96,256]{1,0:T(8,128)(2,1)S(1)}, u32[]{:S(2)}, u32[]{:S(2)}) collective-permute-start(bf16[96,256]{1,0:T(8,128)(2,1)S(1)} %get-tuple-element.31.refs_0_), channel_id=1, source_target_pairs={{0,48},{16,64},{32,80},{48,96},{64,112},{80,0},{96,16},{112,32},{1... | collective-permute-start | bytes 147464 | tf_op jit(solution)/shard_map/ppermute | solution.py:365
  57.1 6.1 %collective-permute-start.3 = (bf16[96,256]{1,0:T(8,128)(2,1)S(1)}, bf16[96,256]{1,0:T(8,128)(2,1)S(1)}, u32[]{:S(2)}, u32[]{:S(2)}) collective-permute-start(bf16[96,256]{1,0:T(8,128)(2,1)S(1)} %get-tuple-element.31.refs_0_), channel_id=1, source_target_pairs={{0,32},{16,48},{32,64},{48,80},{64,96},{80,112},{96,0},{112,16},{1... | collective-permute-start | bytes 147464 | tf_op jit(solution)/shard_map/ppermute | solution.py:365
  57.4 6.3 %collective-permute-start.2 = (bf16[96,256]{1,0:T(8,128)(2,1)S(1)}, bf16[96,256]{1,0:T(8,128)(2,1)S(1)}, u32[]{:S(2)}, u32[]{:S(2)}) collective-permute-start(bf16[96,256]{1,0:T(8,128)(2,1)S(1)} %get-tuple-element.31.refs_0_), channel_id=1, source_target_pairs={{0,16},{16,32},{32,48},{48,64},{64,80},{80,96},{96,112},{112,0},{1... | collective-permute-start | bytes 147464 | tf_op jit(solution)/shard_map/ppermute | solution.py:365
  68.1 17.7 %all-to-all-start.2 = ((bf16[16,48,384]{2,1,0:T(8,128)(2,1)}), bf16[16,48,384]{2,1,0:T(8,128)(2,1)S(1)}, u32[]{:S(2)}, u32[]{:S(2)}) async-start(bf16[16,48,384]{2,1,0:T(8,128)(2,1)} %get-tuple-element.32), calls=%async_computation.2 | async-start | bytes 1179648 | tf_op jit(solution)/shard_map/all_to_all | solution.py:285

commit v3 on v2

--- a/solution.py
+++ b/solution.py
@@ -17,8 +17,10 @@
 QW = 32
 KW = 128
 RIM = (KW - QW) // 2
+CORES = 2
 PAIR_ROWS = 32
-FIRST_ROWS = 64
+STREAMS = 1
+FIRST_ROWS = 32
 MIB = 2**20
 DONE = jax.ShapeDtypeStruct((8, 128), jnp.float32)
 
@@ -51,7 +53,7 @@
 
 
 def atom_kernel(
-    _, place_ref, before_ref, own_ref, after_ref, atom_pair_ref, pair_w_ref, token_ref, w_ref, wo_ref, out_w_ref,
+    first_ref, place_ref, before_ref, own_ref, after_ref, atom_pair_ref, pair_w_ref, token_ref, w_ref, wo_ref, out_w_ref,
     back_w_ref, mid_ref, send_ref, done_ref,
 ):
     done_ref[...] = jnp.zeros_like(done_ref)
@@ -107,16 +109,18 @@
     out_w = out_w_ref[...].astype(f32)
     blank = jnp.zeros((rows, CA - mine), bf16)
     for target in range(targets):
-        send_ref[target, :count, :] = mid
-        send_ref[target, count : count + 16, :] = tail
-        send_ref[target, count + 16 : count + 16 + rows, :] = back_w
         part = out_w[:, target * mine : (target + 1) * mine].astype(bf16)
-        send_ref[target, count + 16 + rows :, :] = jnp.concatenate([part, blank], axis=1)
-
-
-def pair_body(pair_ref, win_ref, wout_ref, wb_ref, out_ref, hold_ref):
-    rows = pair_ref.shape[0]
-    tile = pair_ref[...].reshape(rows * pair_ref.shape[1], CZ)
+        pieces = [first_ref[target], mid, tail, back_w, jnp.concatenate([part, blank], axis=1)]
+        start = 0
+        for piece in pieces:
+            send_ref[target, start : start + piece.shape[0], :] = piece
+            start += piece.shape[0]
+
+
+def pair_body(pair_refs, win_ref, wout_ref, wb_ref, out_ref, hold_ref):
+    part, width, _ = pair_refs[0].shape
+    rows = part * len(pair_refs)
+    tile = jnp.concatenate([ref[...].reshape(part * width, CZ) for ref in pair_refs], axis=0)
     centred = dot_t(centre(), tile)
     spread = jnp.sum(centred * centred, axis=0, keepdims=True) * (1.0 / CZ)
     normed = (centred * lax.rsqrt(spread + epsilon)).astype(bf16)
@@ -127,7 +131,6 @@
     renewed = centred + dot(wout_ref[...], hidden)
     spread = jnp.sum(renewed * renewed, axis=0, keepdims=True) * (1.0 / CZ)
     bias = dot(wb_ref[...], renewed.astype(bf16)) * lax.rsqrt(spread + epsilon)
-    width = pair_ref.shape[1]
     for i in range(rows):
         hold_ref[:, i, :] = bias[:, i * width : (i + 1) * width]
     out_ref[...] = hold_ref[...].astype(bf16)
@@ -139,7 +142,9 @@
     return (jnp.where(row == column, 1.0, 0.0) - 1.0 / CZ).astype(bf16)
 
 
-def pair_first(pair_ref, trans_in_ref, trans_out_ref, wb_ref, out_ref, done_ref, win_ref, wout_ref, hold_ref):
+def pair_first(*refs):
+    *pair_refs, trans_in_ref, trans_out_ref, wb_ref, out_ref, done_ref, win_ref, wout_ref, hold_ref = refs
+
     @pl.when(pl.program_id(0) == 0)
     def _():
         wide = trans_in_ref[...].astype(f32)
@@ -148,49 +153,54 @@
         win_ref[units:, :] = wide[:, 1, :].T.astype(bf16)
         wout_ref[...] = dot_t(centre(), trans_out_ref[...]).astype(bf16)
 
-    pair_body(pair_ref, win_ref, wout_ref, wb_ref, out_ref, hold_ref)
+    pair_body(pair_refs, win_ref, wout_ref, wb_ref, out_ref, hold_ref)
     done_ref[...] = jnp.zeros_like(done_ref)
 
 
-def pair_rest(_, __, pair_ref, win_ref, wout_ref, wb_ref, out_ref, done_ref, hold_ref):
-    pair_body(pair_ref, win_ref, wout_ref, wb_ref, out_ref, hold_ref)
+def pair_rest(_, *refs):
+    *pair_refs, win_ref, wout_ref, wb_ref, out_ref, done_ref, hold_ref = refs
+    pair_body(pair_refs, win_ref, wout_ref, wb_ref, out_ref, hold_ref)
     done_ref[...] = jnp.zeros_like(done_ref)
 
 
-def pair_call(kernel, pair, weights, start, stop, before, out_weights):
+def pair_call(kernel, pair, weights, start, stop, before, out_weights, mib):
     steps = (stop - start) // PAIR_ROWS
     vmem = pl.BlockSpec(memory_space=pltpu.VMEM)
     skip = start // PAIR_ROWS
-    rows, cols, _ = pair.shape
-    in_specs = [pl.BlockSpec(memory_space=pl.ANY), vmem] if before else []
-    in_specs += [pl.BlockSpec((PAIR_ROWS, cols, CZ), lambda i: (i + skip, 0, 0))] + [vmem] * len(weights)
+    cols = pair.shape[1]
+    in_specs = [vmem] * len(before)
+    part = PAIR_ROWS // STREAMS
+    in_specs += [
+        pl.BlockSpec((part, cols, CZ), lambda i, k=k: ((i + skip) * STREAMS + k, 0, 0)) for k in range(STREAMS)
+    ]
+    in_specs += [vmem] * len(weights)
     positions = (stop - start) * cols
     return pl.pallas_call(
         kernel,
         grid=(steps,),
         in_specs=in_specs,
-        out_specs=[pl.BlockSpec((HEADS, PAIR_ROWS, cols), lambda i: (0, i + skip, 0))]
+        out_specs=[pl.BlockSpec((HEADS, PAIR_ROWS, cols), lambda i: (0, i, 0))]
         + [vmem] * (1 + len(out_weights)),
-        out_shape=[jax.ShapeDtypeStruct((HEADS, rows, cols), bf16), DONE, *out_weights],
+        out_shape=[jax.ShapeDtypeStruct((HEADS, stop - start, cols), bf16), DONE, *out_weights],
         scratch_shapes=[pltpu.VMEM((HEADS, PAIR_ROWS, cols), f32)],
-        input_output_aliases={0: 0} if before else {},
-        compiler_params=params(56),
+        compiler_params=params(mib),
         cost_estimate=cost(positions * 620_000, positions * 288),
         name="pair_bias",
-    )(*before, pair, *weights)
+    )(*before, *[pair] * STREAMS, *weights)
 
 
 def token_kernel(
-    _, got_ref, single_ref, agg_ref, w_ref, out_w_ref, in_ref, held_ref, send_ref
+    _, got_ref, single_ref, agg_ref, w_ref, in_ref, held_ref, send_ref
 ):
     sources, count = got_ref.shape[0], got_ref.shape[2]
     tokens = single_ref.shape[0]
-    mids = jnp.concatenate([got_ref[s, :count, :] for s in range(sources)], axis=0)
+    first, ids = FIRST_ROWS, FIRST_ROWS + count
+    mids = jnp.concatenate([got_ref[s, first:ids, :] for s in range(sources)], axis=0)
     features = jnp.maximum(dot(mids, agg_ref[...]), 0.0).astype(bf16)
     token = lax.broadcasted_iota(jnp.int32, (tokens, count), 0).astype(f32)
     onehot = jnp.concatenate(
         [
-            jnp.where(token == got_ref[s, count : count + 16, :].astype(f32)[:1], 1.0, 0.0)
+            jnp.where(token == got_ref[s, ids : ids + 16, :].astype(f32)[:1], 1.0, 0.0)
             for s in range(sources)
         ],
         axis=1,
@@ -202,48 +212,71 @@
     norm = layer_norm(token_in.astype(f32)).astype(bf16)
     turned = dot_t(w_ref[...], norm).astype(bf16)
     held_ref[:, :tokens] = turned[:HEAD]
-    held_ref[:, tokens : 2 * tokens] = turned[3 * HEAD :]
+    held_ref[:, tokens:] = turned[3 * HEAD :]
     send_ref[...] = turned[HEAD : 3 * HEAD]
-    rows = out_w_ref.shape[0]
-    back_w = jnp.concatenate(
-        [got_ref[s, count + 16 : count + 16 + rows, :] for s in range(sources)], axis=0
-    )
-    held_ref[:, 2 * tokens :] = dot(out_w_ref[...], back_w).astype(bf16)
-
-
-def attention_kernel(place_ref, held_ref, bias_ref, *refs):
-    *kv_refs, send_ref, done_ref = refs
-    done_ref[...] = jnp.zeros_like(done_ref)
-    rows = len(kv_refs)
+
+
+def hops_of(rows):
+    hops = rows // CORES
+    return sorted(range(hops), key=lambda hop: -min(hop, hops - hop) if hop else -hops)
+
+
+def partner(row, rows, hop, cross):
+    hops = rows // CORES
+    chip, core = row // CORES, row % CORES
+    return (chip + hop + hops) % hops * CORES + (core + cross) % CORES
+
+
+def chip_kernel(own_ref, other_ref, out_ref):
+    rows = own_ref.shape[0]
+    out_ref[:rows, :] = own_ref[...]
+    out_ref[rows:, :] = other_ref[...]
+
+
+def attention_kernel(place_ref, held_ref, mixed_ref, got_ref, bias_ref, *refs):
+    *kv_refs, send_ref = refs
+    rows = len(kv_refs) * CORES
     tokens = kv_refs[0].shape[1]
     query = held_ref[:, :tokens].astype(f32).T.astype(bf16)
     per = bias_ref.shape[0] // rows
-    scores = []
-    for step, kv_ref in enumerate(kv_refs):
-        source = lax.rem(place_ref[4] + rows - step, rows) * per
-        bias = jnp.concatenate([bias_ref[source + k].astype(f32) for k in range(per)], axis=1)
-        scores.append(dot(query, kv_ref[:HEAD, :]) / math.sqrt(HEAD) + bias)
+    scores, values = [], []
+    for hop, kv_ref in zip(hops_of(rows), kv_refs):
+        for cross in range(CORES):
+            source = partner(place_ref[4], rows, -hop, cross) * per
+            bias = jnp.concatenate(
+                [
+                    jnp.concatenate([got_ref[source + k, :FIRST_ROWS, :], bias_ref[source + k]], axis=0)
+                    for k in range(per)
+                ],
+                axis=1,
+            ).astype(f32)
+            start = cross * 2 * HEAD
+            scores.append(dot(query, kv_ref[start : start + HEAD, :]) / math.sqrt(HEAD) + bias)
+            values.append(kv_ref[start + HEAD : start + 2 * HEAD, :])
     scores = jnp.concatenate(scores, axis=1)
     raised = jnp.exp(scores - jnp.max(scores, axis=-1, keepdims=True))
     weights = (raised / jnp.sum(raised, axis=-1, keepdims=True)).astype(bf16)
-    values = jnp.concatenate([kv_ref[HEAD:, :] for kv_ref in kv_refs], axis=1)
+    values = jnp.concatenate(values, axis=1)
     attended = dot_t(values, weights)
-    gate = held_ref[:, tokens : 2 * tokens].astype(f32)
+    gate = held_ref[:, tokens:].astype(f32)
     gated = (jax.nn.sigmoid(gate) * attended).astype(bf16)
-    back = held_ref[:, 2 * tokens :]
+    back = mixed_ref[...]
     for target in range(send_ref.shape[0]):
         send_ref[target, :, :tokens] = gated
         send_ref[target, :, tokens:] = back
 
 
-def ready_kernel(_, place_ref, got_ref, in_ref, token_ref, out_w_ref, own_ref, back_ref, onehot_ref):
+def ready_kernel(
+    place_ref, got_ref, in_ref, token_ref, mine_ref, out_w_ref, own_ref, back_ref, onehot_ref, mixed_ref
+):
     sources, count = got_ref.shape[0], got_ref.shape[2]
     tokens, width = in_ref.shape
     mine = width // sources
     token_in = in_ref[...]
-    start = count + 16
+    start = FIRST_ROWS + count + 16
     back_w = jnp.concatenate([got_ref[s, start : start + mine, :] for s in range(sources)], axis=0)
     out_w = jnp.concatenate([got_ref[s, start + mine :, :] for s in range(sources)], axis=0)
+    mixed_ref[...] = dot(mine_ref[...], back_w).astype(bf16)
     out_w_ref[...] = out_w.astype(f32).T[:mine].astype(bf16)
     back_ref[...] = dot_t(back_w.astype(f32).T.astype(bf16), token_in)
     wanted = lax.broadcasted_iota(jnp.int32, (mine, width), 0) + place_ref[3] * mine
@@ -328,67 +361,78 @@
     token_row = atom_token.reshape(1, count)
 
     units = trans_in.shape[2]
-    bias, done, win, wout = pair_call(
+    first_bias, _, win, wout = pair_call(
         pair_first, pair, (trans_in, trans_out, bias_w.T), 0, FIRST_ROWS, (),
-        (shape(2 * units, CZ), shape(CZ, units)),
+        (shape(2 * units, CZ), shape(CZ, units)), 56,
     )
     mid, mid_send, done = single_step(
         atom_kernel,
         "atom_stage",
         [vmem, smem] + [vmem] * 10,
-        [shape(count, CA), shape(col_size, count + 16 + 2 * head_rows, CA), DONE],
+        [shape(count, CA), shape(col_size, FIRST_ROWS + count + 16 + 2 * head_rows, CA), DONE],
         4_000_000_000,
         2_000_000,
         (
-            done, place, before, atoms, after, atom_pair, atom_pair_w.T, token_row, atom_w, atom_wo, token_wo, back_w,
+            first_bias, place, before, atoms, after, atom_pair, atom_pair_w.T, token_row, atom_w, atom_wo, token_wo, back_w,
         ),
     )
     mids = gathered(mid_send, "col")
-    bias, done = pair_call(pair_rest, pair, (win, wout, bias_w.T), FIRST_ROWS, query_rows, (bias, done), ())
+    bias, done = pair_call(pair_rest, pair, (win, wout, bias_w.T), FIRST_ROWS, query_rows, (done,), (), 52)
     bias_rows = gathered(bias, "col")
 
     turned = jnp.transpose(token_w, (1, 2, 0)).reshape(4 * HEAD, width)
     token_in, held, kv_send = single_step(
         token_kernel,
         "token_stage",
-        [vmem] * 6,
+        [vmem] * 5,
         [
             shape(query_rows, width),
-            shape(HEAD, 2 * query_rows + CA),
+            shape(HEAD, 2 * query_rows),
             shape(2 * HEAD, query_rows),
         ],
         4_000_000_000,
         2_000_000,
-        (done, mids, single, agg_w, turned, token_wo),
-    )
-    kv = [kv_send] + [
-        lax.ppermute(kv_send, "row", [(i, (i + step) % row_size) for i in range(row_size)])
-        for step in range(1, row_size)
+        (done, mids, single, agg_w, turned),
+    )
+    across = lax.ppermute(kv_send, "row", [(i, partner(i, row_size, 0, 1)) for i in range(row_size)])
+    (chip_kv,) = single_step(
+        chip_kernel,
+        "chip_keys",
+        [vmem] * 2,
+        [shape(4 * HEAD, query_rows)],
+        1_000_000,
+        200_000,
+        (kv_send, across),
+    )
+    kv = [chip_kv] + [
+        lax.ppermute(chip_kv, "row", [(i, partner(i, row_size, hop, 0)) for i in range(row_size)])
+        for hop in hops_of(row_size)[1:]
     ]
-    gated_send, done = single_step(
-        attention_kernel,
-        "token_attention",
-        [smem] + [vmem] * (2 + row_size),
-        [shape(col_size, HEAD, query_rows + CA), DONE],
-        3_000_000_000,
-        2_000_000,
-        (place, held, bias_rows, *kv),
-    )
-    gated = gathered(gated_send, "col")
-    out_w, own, back, onehot = single_step(
+    out_w, own, back, onehot, mixed = single_step(
         ready_kernel,
         "out_ready",
-        [vmem, smem] + [vmem] * 3,
+        [smem] + [vmem] * 4,
         [
             shape(width // col_size, width),
             shape(width // col_size, query_rows, dtype=f32),
             shape(CA, query_rows, dtype=f32),
             shape(count, query_rows),
+            shape(head_rows, CA),
         ],
         2_000_000_000,
         2_000_000,
-        (done, place, mids, token_in, token_row),
-    )
+        (place, mids, token_in, token_row, token_wo),
+    )
+    (gated_send,) = single_step(
+        attention_kernel,
+        "token_attention",
+        [smem] + [vmem] * (4 + len(kv)),
+        [shape(col_size, HEAD, query_rows + CA)],
+        3_000_000_000,
+        2_000_000,
+        (place, held, mixed, mids, bias_rows, *kv),
+    )
+    gated = gathered(gated_send, "col")
     single_out, atoms_out = single_step(
         final_kernel,
         "token_out",

time: 87.4 us -> 85.5 us (0.978)
  blocking collectives: 0 us -> 16.6 us
  waiting for transfers between devices: 20.1 us -> 10.9 us
  starting transfers between devices: 32.1 us -> 24 us
    all_to_all x0 -> x1, blocking collectives: none -> 16.6 us  [gathered(): return lax.all_to_all(copies, axis, split_axis=0, concat_axis=0, tiled=True)]
    all_to_all x3 -> x2, starting transfers between devices: 19.1 us -> 13.1 us  [gathered(): return lax.all_to_all(copies, axis, split_axis=0, concat_axis=0, tiled=True)]
    all_to_all x3 -> x2, waiting for transfers between devices: 14.9 us -> 9.79 us  [gathered(): return lax.all_to_all(copies, axis, split_axis=0, concat_axis=0, tiled=True)]
    ppermute x7 -> x4, waiting for transfers between devices: 5.2 us -> 0.9 us  [the longest x1 0.89 us: body(): lax.ppermute(kv_send, 'row', [(i, partner(i, row_size, 0, 1)) for i in ra...]
    ppermute x7 -> x4, starting transfers between devices: 7.84 us -> 5.77 us  [the longest x3 5.35 us: body(): lax.ppermute(chip_kv, 'row', [(i, partner(i, row_size, hop, 0)) for i in...]
    pallas_call x5 -> x6, Pallas kernels: 10.8 us -> 10.1 us  [single_step(): pl.pallas_call(kernel, in_specs=in_specs, out_specs=[pl.BlockSpec(memory_...]
  transfers between devices with their start and end apart: 12 -> 8, of which waited for: 7 -> 4; matrix products, arithmetic and copies ran while one was open for 0% -> 0% of each run, Pallas kernels for 29% -> 29%
where the time goes in v3:
time: 85.5 us; the launch traced here: 85.1 us
  Pallas kernels  31.6 us (37%)
  starting transfers between devices  24 us (28%)
  blocking collectives  16.6 us (19%)
  waiting for transfers between devices  10.9 us (13%)
  local copies, waits for them, and re-layouts  1.04 us (1%)
  between operations  0.86 us (1%)
    pallas_call x2, Pallas kernels, pair_call(): pl.pallas_call(kernel, grid=(steps,), in_specs=in_specs, out_specs=[pl.Bl...  21.5 us
    all_to_all x1, blocking collectives, gathered(): return lax.all_to_all(copies, axis, split_axis=0, concat_axis=0, tiled=True)  16.6 us
    all_to_all x2, starting transfers between devices, gathered(): return lax.all_to_all(copies, axis, split_axis=0, concat_axis=0, tiled=True)  13.1 us
    pallas_call x6, Pallas kernels, single_step(): pl.pallas_call(kernel, in_specs=in_specs, out_specs=[pl.BlockSpec(memory_...  10.1 us
    all_to_all x2, waiting for transfers between devices, gathered(): return lax.all_to_all(copies, axis, split_axis=0, concat_axis=0, tiled=True)  9.79 us
    ppermute x3, starting transfers between devices, body(): lax.ppermute(chip_kv, 'row', [(i, partner(i, row_size, hop, 0)) for i in...  5.35 us
    ppermute x1, starting transfers between devices, body(): before = lax.ppermute(atoms, both, up)  3.91 us
  transfers between devices with their start and end apart: 8, of which 4 were waited for; matrix products, arithmetic and copies ran while one was open for 0% of the time, Pallas kernels for 29%

profile of v3, /device:TPU:0, one launch (start us, length us, event | category | flops | bytes accessed | tf_op | source)
XLA Modules:
  0.0 85.1 jit_solution(10650410379490537619)
XLA Ops:
  0.6 3.9 %collective-permute-start = (bf16[128,128]{1,0:T(8,128)(2,1)}, bf16[128,128]{1,0:T(8,128)(2,1)S(1)}, u32[]{:S(2)}, u32[]{:S(2)}) collective-permute-start(bf16[128,128]{1,0:T(8,128)(2,1)} %own_ref.1), channel_id=1, source_target_pairs={{0,1},{1,2},{2,3},{3,4},{4,5},{5,6},{6,7},{7,8},{8,9},{9,10},{10,1... | collective-permute-start | bytes 98312 | tf_op jit(solution)/shard_map/ppermute | solution.py:346
  4.5 1.3 %collective-permute-start.1 = (bf16[128,128]{1,0:T(8,128)(2,1)}, bf16[128,128]{1,0:T(8,128)(2,1)S(1)}, u32[]{:S(2)}, u32[]{:S(2)}) collective-permute-start(bf16[128,128]{1,0:T(8,128)(2,1)} %own_ref.1), channel_id=1, source_target_pairs={{1,0},{2,1},{3,2},{4,3},{5,4},{6,5},{7,6},{8,7},{9,8},{10,9},{11,1... | collective-permute-start | bytes 98312 | tf_op jit(solution)/shard_map/ppermute | solution.py:347
  5.8 0.0 copy-start
  5.9 0.0 copy-start.4
  5.9 0.0 copy-start.5
  5.9 0.0 copy-start.6
  5.9 0.0 copy-start.7
  5.9 0.0 copy-start.8
  5.9 0.0 copy-start.10
  5.9 0.0 copy-start.11
  5.9 4.3 %pair_bias.2 = (bf16[16,32,128]{2,1,0:T(8,128)(2,1)}, f32[8,128]{1,0:T(8,128)}, bf16[512,128]{1,0:T(8,128)(2,1)}, bf16[128,256]{1,0:T(8,128)(2,1)}) custom-call(bf16[256,128,128]{2,1,0:T(8,128)(2,1)} %refs_0_.3, bf16[128,2,256]{2,1,0:T(2,128)(2,1)} %refs_1_.1, bf16[256,128]{1,0:T(8,128)(2,1)} %refs_2_.1, bf16[16,128]{1,0:T(8,128)(2,1)} %bitcast.12), custom_call_target="tpu_custom_call" | custom-call | flops 2539520000 | bytes 1179648 | tf_op jit(solution)/shard_map/pair_bias/pallas_call | solution.py:178
  10.2 0.1 stack.19.place_ref
  10.3 0.0 collective-permute-done.before_ref
  10.3 0.3 collective-permute-done.1.after_ref
  10.6 0.0 copy-done
  10.6 0.0 copy-done.4
  10.6 0.0 copy-done.5
  10.6 0.0 copy-done.6
  10.6 0.0 copy-done.7
  10.6 0.0 copy-done.8
  10.6 0.0 copy-done.10
  10.6 0.0 copy-done.11
  10.6 0.0 copy-start.13
  10.6 0.9 %copy-done.13 = bf16[16,32,128]{2,1,0:T(8,128)(2,1)S(1)} copy-done((bf16[16,32,128]{2,1,0:T(8,128)(2,1)S(1)}, bf16[16,32,128]{2,1,0:T(8,128)(2,1)}, u32[]{:S(2)}) %copy-start.13) | copy-done | bytes 131096
  11.5 3.4 %atom_stage.1 = (bf16[128,128]{1,0:T(8,128)(2,1)S(1)}, bf16[16,272,128]{2,1,0:T(8,128)(2,1)}, f32[8,128]{1,0:T(8,128)S(1)}) custom-call(bf16[16,32,128]{2,1,0:T(8,128)(2,1)S(1)} %copy-done.13, s32[5]{0:T(128)S(1)} %stack.19.place_ref, bf16[128,128]{1,0:T(8,128)(2,1)S(1)} %collective-permute-done.before_ref, bf16[128,128]{1,0:T(8,128)(2,1)S(1)} %copy-done.6, ...), custom_call_target="tpu_custom_call" | custom-call | flops 4000000000 | bytes 2000000 | tf_op jit(solution)/shard_map/atom_stage/pallas_call | solution.py:306
  15.0 0.0 copy-start.9
  15.0 0.0 copy-start.12
  15.0 0.0 copy-start.14
  15.0 8.6 %all-to-all-start = ((bf16[16,272,128]{2,1,0:T(8,128)(2,1)}), bf16[16,272,128]{2,1,0:T(8,128)(2,1)S(1)}, u32[]{:S(2)}, u32[]{:S(2)}) async-start(bf16[16,272,128]{2,1,0:T(8,128)(2,1)} %get-tuple-element.25), calls=%async_computation | async-start | bytes 2228224 | tf_op jit(solution)/shard_map/all_to_all | solution.py:318
  23.6 0.0 copy-done.9
  23.6 0.0 copy-done.12
  23.6 0.0 copy-done.14
  23.6 17.2 %pair_bias.3 = (bf16[16,224,128]{2,1,0:T(8,128)(2,1)}, f32[8,128]{1,0:T(8,128)S(1)}) custom-call(f32[8,128]{1,0:T(8,128)S(1)} %get-tuple-element.21._, bf16[256,128,128]{2,1,0:T(8,128)(2,1)} %refs_0_.3, bf16[512,128]{1,0:T(8,128)(2,1)S(1)} %copy-done.12, bf16[128,256]{1,0:T(8,128)(2,1)S(1)} %copy-done.14, bf16[16,128]{1,0:T(8,128)(2,1)S(1)} %bitcast.13), custom_call_target="tpu_custom_call" | custom-call | flops 17776640000 | bytes 8257536 | tf_op jit(solution)/shard_map/pair_bias/pallas_call | solution.py:178
  40.8 0.0 copy-start.1
  40.8 0.0 copy-start.2
  40.8 0.0 copy-start.3
  40.8 2.9 %all-to-all-done.got_ref = bf16[16,272,128]{2,1,0:T(8,128)(2,1)S(1)} async-done(((bf16[16,272,128]{2,1,0:T(8,128)(2,1)}), bf16[16,272,128]{2,1,0:T(8,128)(2,1)S(1)}, u32[]{:S(2)}, u32[]{:S(2)}) %all-to-all-start) | async-done | bytes 1114144 | tf_op jit(solution)/shard_map/all_to_all | solution.py:318
  43.7 4.5 %all-to-all-start.1 = ((bf16[16,224,128]{2,1,0:T(8,128)(2,1)}), bf16[16,224,128]{2,1,0:T(8,128)(2,1)S(1)}, u32[]{:S(2)}, u32[]{:S(2)}) async-start(bf16[16,224,128]{2,1,0:T(8,128)(2,1)} %get-tuple-element.29), calls=%async_computation.1 | async-start | bytes 1835008 | tf_op jit(solution)/shard_map/all_to_all | solution.py:318
  48.2 0.0 copy-done.1
  48.2 0.0 copy-done.2
  48.2 0.0 copy-done.3
  48.2 2.5 %token_stage.1 = (bf16[256,768]{1,0:T(8,128)(2,1)S(1)}, bf16[48,512]{1,0:T(8,128)(2,1)S(1)}, bf16[96,256]{1,0:T(8,128)(2,1)S(1)}) custom-call(f32[8,128]{1,0:T(8,128)S(1)} %get-tuple-element.24._, bf16[16,272,128]{2,1,0:T(8,128)(2,1)S(1)} %all-to-all-done.got_ref, bf16[256,768]{1,0:T(8,128)(2,1)S(1)} %copy-done.1, bf16[128,768]{1,0:T(8,128)(2,1)S(1)} %copy-done.3, ...), custom_call_target="tpu_custom_call" | custom-call | flops 4000000000 | bytes 2000000 | tf_op jit(solution)/shard_map/token_stage/pallas_call | solution.py:306
  50.7 0.4 collective-permute-start.2
  51.1 0.9 %collective-permute-done.2.other_ref = bf16[96,256]{1,0:T(8,128)(2,1)S(1)} collective-permute-done((bf16[96,256]{1,0:T(8,128)(2,1)S(1)}, bf16[96,256]{1,0:T(8,128)(2,1)S(1)}, u32[]{:S(2)}, u32[]{:S(2)}) %collective-permute-start.2) | collective-permute-done | bytes 49184 | tf_op jit(solution)/shard_map/ppermute | solution.py:397
  52.0 3.1 %collective-permute-start.5 = (bf16[192,256]{1,0:T(8,128)(2,1)S(1)}, bf16[192,256]{1,0:T(8,128)(2,1)S(1)}, u32[]{:S(2)}, u32[]{:S(2)}) collective-permute-start(bf16[192,256]{1,0:T(8,128)(2,1)S(1)} %chip_keys.1.refs_0_), channel_id=1, source_target_pairs={{0,96},{16,112},{32,0},{48,16},{64,32},{80,48},{96,64},{112,80},{1... | collective-permute-start | bytes 294920 | tf_op jit(solution)/shard_map/ppermute | solution.py:408
  55.1 0.0 collective-permute-start.4
  55.1 2.2 %collective-permute-start.3 = (bf16[192,256]{1,0:T(8,128)(2,1)S(1)}, bf16[192,256]{1,0:T(8,128)(2,1)S(1)}, u32[]{:S(2)}, u32[]{:S(2)}) collective-permute-start(bf16[192,256]{1,0:T(8,128)(2,1)S(1)} %chip_keys.1.refs_0_), channel_id=1, source_target_pairs={{0,64},{16,80},{32,96},{48,112},{64,0},{80,16},{96,32},{112,48},{1... | collective-permute-start | bytes 294920 | tf_op jit(solution)/shard_map/ppermute | solution.py:408
  57.3 0.9 %out_ready.1 = (bf16[48,768]{1,0:T(8,128)(2,1)S(1)}, f32[48,256]{1,0:T(8,128)S(1)}, f32[128,256]{1,0:T(8,128)S(1)}, bf16[128,256]{1,0:T(8,128)(2,1)S(1)}, bf16[48,128]{1,0:T(8,128)(2,1)S(1)}) custom-call(s32[5]{0:T(128)S(1)} %stack.19.place_ref, bf16[16,272,128]{2,1,0:T(8,128)(2,1)S(1)} %all-to-all-done.got_ref, ...), custom_call_target="tpu_custom_call" | custom-call | flops 2000000000 | bytes 2000000 | tf_op jit(solution)/shard_map/out_ready/pallas_call | solution.py:306
  58.3 6.9 %all-to-all-done.1.bias_ref = bf16[16,224,128]{2,1,0:T(8,128)(2,1)S(1)} async-done(((bf16[16,224,128]{2,1,0:T(8,128)(2,1)}), bf16[16,224,128]{2,1,0:T(8,128)(2,1)S(1)}, u32[]{:S(2)}, u32[]{:S(2)}) %all-to-all-start.1) | async-done | bytes 917536 | tf_op jit(solution)/shard_map/all_to_all | solution.py:318
  65.2 0.0 collective-permute-done.5.refs_3_
  65.2 0.0 collective-permute-done.4.refs_2_
  65.2 0.0 collective-permute-done.3.refs_1_
  65.2 2.2 %token_attention.1 = bf16[16,48,384]{2,1,0:T(8,128)(2,1)S(1)} custom-call(s32[5]{0:T(128)S(1)} %stack.19.place_ref, bf16[48,512]{1,0:T(8,128)(2,1)S(1)} %get-tuple-element.26.held_ref, bf16[48,128]{1,0:T(8,128)(2,1)S(1)} %get-tuple-element.28.mixed_ref, bf16[16,272,128]{2,1,0:T(8,128)(2,1)S(1)} %all-to-all-done.got_ref, ...), custom_call_target="tpu_custom_call" | custom-call | flops 3000000000 | bytes 2000000 | tf_op jit(solution)/shard_map/token_attention/pallas_call | solution.py:306
  67.4 16.6 %all_to_all.15.got_ref = bf16[16,48,384]{2,1,0:T(8,128)(2,1)S(1)} all-to-all(bf16[16,48,384]{2,1,0:T(8,128)(2,1)S(1)} %token_attention.1), channel_id=1, replica_groups=mesh['row'=8,'col'=16] {'col'}, dimensions={0} | all-to-all | bytes 1179648 | tf_op jit(solution)/shard_map/all_to_all | solution.py:318
  84.0 1.1 %token_out.1 = (bf16[48,256]{1,0:T(8,128)(2,1)}, bf16[128,128]{1,0:T(8,128)(2,1)}) custom-call(bf16[16,48,384]{2,1,0:T(8,128)(2,1)S(1)} %all_to_all.15.got_ref, bf16[48,768]{1,0:T(8,128)(2,1)S(1)} %get-tuple-element.31.out_w_ref, f32[48,256]{1,0:T(8,128)S(1)} %get-tuple-element.32.own_ref, f32[128,256]{1,0:T(8,128)S(1)} %get-tuple-element.33.back_ref, ...), custom_call_target="tpu_custom_call" | custom-call | flops 2000000000 | bytes 2000000 | tf_op jit(solution)/shard_map/token_out/pallas_call | solution.py:306
  (1 shorter events, 0.0 us)
Async XLA Ops:
  0.6 9.7 %collective-permute-start = (bf16[128,128]{1,0:T(8,128)(2,1)}, bf16[128,128]{1,0:T(8,128)(2,1)S(1)}, u32[]{:S(2)}, u32[]{:S(2)}) collective-permute-start(bf16[128,128]{1,0:T(8,128)(2,1)} %own_ref.1), channel_id=1, source_target_pairs={{0,1},{1,2},{2,3},{3,4},{4,5},{5,6},{6,7},{7,8},{8,9},{9,10},{10,1... | collective-permute-start | bytes 98312 | tf_op jit(solution)/shard_map/ppermute | solution.py:346
  4.5 6.0 %collective-permute-start.1 = (bf16[128,128]{1,0:T(8,128)(2,1)}, bf16[128,128]{1,0:T(8,128)(2,1)S(1)}, u32[]{:S(2)}, u32[]{:S(2)}) collective-permute-start(bf16[128,128]{1,0:T(8,128)(2,1)} %own_ref.1), channel_id=1, source_target_pairs={{1,0},{2,1},{3,2},{4,3},{5,4},{6,5},{7,6},{8,7},{9,8},{10,9},{11,1... | collective-permute-start | bytes 98312 | tf_op jit(solution)/shard_map/ppermute | solution.py:347
  5.8 4.7 %copy-start = (bf16[4,16,32,128]{3,2,1,0:T(8,128)(2,1)S(1)}, bf16[4,16,32,128]{3,2,1,0:T(8,128)(2,1)}, u32[]{:S(2)}) copy-start(bf16[4,16,32,128]{3,2,1,0:T(8,128)(2,1)} %atom_pair_ref.1) | copy-start | bytes 1572868
  5.9 4.7 %copy-start.4 = (bf16[128,4,128]{2,1,0:T(4,128)(2,1)S(1)}, bf16[128,4,128]{2,1,0:T(4,128)(2,1)}, u32[]{:S(2)}) copy-start(bf16[128,4,128]{2,1,0:T(4,128)(2,1)} %w_ref.1) | copy-start | bytes 393220
  5.9 4.7 %copy-start.5 = (bf16[48,768]{1,0:T(8,128)(2,1)S(1)}, bf16[48,768]{1,0:T(8,128)(2,1)}, u32[]{:S(2)}) copy-start(bf16[48,768]{1,0:T(8,128)(2,1)} %mine_ref.1) | copy-start | bytes 221188
  5.9 4.7 %copy-start.6 = (bf16[128,128]{1,0:T(8,128)(2,1)S(1)}, bf16[128,128]{1,0:T(8,128)(2,1)}, u32[]{:S(2)}) copy-start(bf16[128,128]{1,0:T(8,128)(2,1)} %own_ref.1) | copy-start | bytes 98308
  5.9 4.7 %copy-start.7 = (bf16[128,128]{1,0:T(8,128)(2,1)S(1)}, bf16[128,128]{1,0:T(8,128)(2,1)}, u32[]{:S(2)}) copy-start(bf16[128,128]{1,0:T(8,128)(2,1)} %wo_ref.1) | copy-start | bytes 98308
  5.9 4.7 %copy-start.8 = (bf16[48,128]{1,0:T(8,128)(2,1)S(1)}, bf16[48,128]{1,0:T(8,128)(2,1)}, u32[]{:S(2)}) copy-start(bf16[48,128]{1,0:T(8,128)(2,1)} %back_w_ref.1) | copy-start | bytes 36868
  5.9 4.7 %copy-start.10 = (bf16[16,4]{0,1:T(4,128)(2,1)S(1)}, bf16[16,4]{0,1:T(4,128)(2,1)}, u32[]{:S(2)}) copy-start(bf16[16,4]{0,1:T(4,128)(2,1)} %param.21) | copy-start | bytes 388
  5.9 4.7 %copy-start.11 = (s32[128]{0:T(128)S(1)}, s32[128]{0:T(128)}, u32[]{:S(2)}) copy-start(s32[128]{0:T(128)} %param.17) | copy-start | bytes 1540
  10.6 0.9 %copy-start.13 = (bf16[16,32,128]{2,1,0:T(8,128)(2,1)S(1)}, bf16[16,32,128]{2,1,0:T(8,128)(2,1)}, u32[]{:S(2)}) copy-start(bf16[16,32,128]{2,1,0:T(8,128)(2,1)} %get-tuple-element.20.first_ref) | copy-start | bytes 393220
  15.0 8.6 %copy-start.9 = (bf16[128,16]{0,1:T(8,128)(2,1)S(1)}, bf16[128,16]{0,1:T(8,128)(2,1)}, u32[]{:S(2)}) copy-start(bf16[128,16]{0,1:T(8,128)(2,1)} %param.26) | copy-start | bytes 12292
  15.0 8.6 %copy-start.12 = (bf16[512,128]{1,0:T(8,128)(2,1)S(1)}, bf16[512,128]{1,0:T(8,128)(2,1)}, u32[]{:S(2)}) copy-start(bf16[512,128]{1,0:T(8,128)(2,1)} %get-tuple-element.22.refs_1_) | copy-start | bytes 393220
  15.0 8.6 %copy-start.14 = (bf16[128,256]{1,0:T(8,128)(2,1)S(1)}, bf16[128,256]{1,0:T(8,128)(2,1)}, u32[]{:S(2)}) copy-start(bf16[128,256]{1,0:T(8,128)(2,1)} %get-tuple-element.23.refs_2_) | copy-start | bytes 196612
  15.0 28.7 %all-to-all-start = ((bf16[16,272,128]{2,1,0:T(8,128)(2,1)}), bf16[16,272,128]{2,1,0:T(8,128)(2,1)S(1)}, u32[]{:S(2)}, u32[]{:S(2)}) async-start(bf16[16,272,128]{2,1,0:T(8,128)(2,1)} %get-tuple-element.25), calls=%async_computation | async-start | bytes 2228224 | tf_op jit(solution)/shard_map/all_to_all | solution.py:318
  40.8 7.4 %copy-start.1 = (bf16[256,768]{1,0:T(8,128)(2,1)S(1)}, bf16[256,768]{1,0:T(8,128)(2,1)}, u32[]{:S(2)}) copy-start(bf16[256,768]{1,0:T(8,128)(2,1)} %single_ref.1) | copy-start | bytes 1179652
  40.8 7.4 %copy-start.2 = (bf16[768,4,48]{0,2,1:T(8,128)(2,1)S(1)}, bf16[768,4,48]{0,2,1:T(8,128)(2,1)}, u32[]{:S(2)}) copy-start(bf16[768,4,48]{0,2,1:T(8,128)(2,1)} %param.27) | copy-start | bytes 884740
  40.8 7.4 %copy-start.3 = (bf16[128,768]{1,0:T(8,128)(2,1)S(1)}, bf16[128,768]{1,0:T(8,128)(2,1)}, u32[]{:S(2)}) copy-start(bf16[128,768]{1,0:T(8,128)(2,1)} %agg_ref.1) | copy-start | bytes 589828
  43.7 21.5 %all-to-all-start.1 = ((bf16[16,224,128]{2,1,0:T(8,128)(2,1)}), bf16[16,224,128]{2,1,0:T(8,128)(2,1)S(1)}, u32[]{:S(2)}, u32[]{:S(2)}) async-start(bf16[16,224,128]{2,1,0:T(8,128)(2,1)} %get-tuple-element.29), calls=%async_computation.1 | async-start | bytes 1835008 | tf_op jit(solution)/shard_map/all_to_all | solution.py:318
  50.7 1.3 %collective-permute-start.2 = (bf16[96,256]{1,0:T(8,128)(2,1)S(1)}, bf16[96,256]{1,0:T(8,128)(2,1)S(1)}, u32[]{:S(2)}, u32[]{:S(2)}) collective-permute-start(bf16[96,256]{1,0:T(8,128)(2,1)S(1)} %get-tuple-element.30.own_ref), channel_id=1, source_target_pairs={{0,16},{16,0},{32,48},{48,32},{64,80},{80,64},{96,112},{112,96},{1... | collective-permute-start | bytes 147464 | tf_op jit(solution)/shard_map/ppermute | solution.py:397
  52.0 13.2 %collective-permute-start.5 = (bf16[192,256]{1,0:T(8,128)(2,1)S(1)}, bf16[192,256]{1,0:T(8,128)(2,1)S(1)}, u32[]{:S(2)}, u32[]{:S(2)}) collective-permute-start(bf16[192,256]{1,0:T(8,128)(2,1)S(1)} %chip_keys.1.refs_0_), channel_id=1, source_target_pairs={{0,96},{16,112},{32,0},{48,16},{64,32},{80,48},{96,64},{112,80},{1... | collective-permute-start | bytes 294920 | tf_op jit(solution)/shard_map/ppermute | solution.py:408
  55.1 10.1 %collective-permute-start.4 = (bf16[192,256]{1,0:T(8,128)(2,1)S(1)}, bf16[192,256]{1,0:T(8,128)(2,1)S(1)}, u32[]{:S(2)}, u32[]{:S(2)}) collective-permute-start(bf16[192,256]{1,0:T(8,128)(2,1)S(1)} %chip_keys.1.refs_0_), channel_id=1, source_target_pairs={{0,32},{16,48},{32,64},{48,80},{64,96},{80,112},{96,0},{112,16},{1... | collective-permute-start | bytes 294920 | tf_op jit(solution)/shard_map/ppermute | solution.py:408
  55.1 10.1 %collective-permute-start.3 = (bf16[192,256]{1,0:T(8,128)(2,1)S(1)}, bf16[192,256]{1,0:T(8,128)(2,1)S(1)}, u32[]{:S(2)}, u32[]{:S(2)}) collective-permute-start(bf16[192,256]{1,0:T(8,128)(2,1)S(1)} %chip_keys.1.refs_0_), channel_id=1, source_target_pairs={{0,64},{16,80},{32,96},{48,112},{64,0},{80,16},{96,32},{112,48},{1... | collective-permute-start | bytes 294920 | tf_op jit(solution)/shard_map/ppermute | solution.py:408

commit v4 on v3

--- a/solution.py
+++ b/solution.py
@@ -19,8 +19,8 @@
 RIM = (KW - QW) // 2
 CORES = 2
 PAIR_ROWS = 32
-STREAMS = 1
 FIRST_ROWS = 32
+EARLY_ROWS = 64
 MIB = 2**20
 DONE = jax.ShapeDtypeStruct((8, 128), jnp.float32)
 
@@ -48,24 +48,62 @@
     return pltpu.CompilerParams(vmem_limit_bytes=mib * MIB)
 
 
+def in_hbm(array):
+    return pltpu.with_memory_space_constraint(array, pltpu.HBM)
+
+
 def cost(flops, moved):
     return pl.CostEstimate(flops=flops, bytes_accessed=moved, transcendentals=0)
 
 
+def regrouped(size, groups):
+    row = lax.broadcasted_iota(jnp.int32, (size, size), 0)
+    column = lax.broadcasted_iota(jnp.int32, (size, size), 1)
+    length = size // groups
+    return jnp.where(column == (row % length) * groups + row // length, 1.0, 0.0).astype(bf16)
+
+
 def atom_kernel(
-    first_ref, place_ref, before_ref, own_ref, after_ref, atom_pair_ref, pair_w_ref, token_ref, w_ref, wo_ref, out_w_ref,
-    back_w_ref, mid_ref, send_ref, done_ref,
+    first_ref, place_ref, even_ref, own_ref, odd_ref, atom_pair_ref, pair_w_ref, token_ref, w_ref, wo_ref,
+    out_w_ref, back_w_ref, send_ref, mid_ref, done_ref, hold_ref, slice_ref, block_sem, hold_sem, back_sem,
 ):
     done_ref[...] = jnp.zeros_like(done_ref)
     device, row, last = place_ref[0], place_ref[1], place_ref[2]
     atoms = own_ref[...].astype(f32)
     count = atoms.shape[0]
-    extended = jnp.concatenate(
-        [before_ref[count - RIM :, :].astype(f32), atoms, after_ref[:RIM, :].astype(f32)], axis=0
-    )
+    odd = device % 2 == 1
+    before = jnp.where(odd, even_ref[count - RIM :, :].astype(f32), odd_ref[count - RIM :, :].astype(f32))
+    after = jnp.where(odd, odd_ref[:RIM, :].astype(f32), even_ref[:RIM, :].astype(f32))
+    extended = jnp.concatenate([before, atoms, after], axis=0)
     norm = layer_norm(extended).astype(bf16)
-    wide = w_ref[...].astype(f32)
-    query_all, key_all, value_all, gate_all = [dot(norm, wide[:, m, :].astype(bf16)).astype(bf16) for m in range(4)]
+    sorted_w = dot(regrouped(4 * CA, 4), w_ref[...]).astype(bf16)
+    query_all, key_all, value_all, gate_all = [
+        dot(norm, sorted_w[m * CA : (m + 1) * CA]).astype(bf16) for m in range(4)
+    ]
+    targets = send_ref.shape[0]
+    rows, width = out_w_ref.shape
+    mine = width // targets
+    half = rows // 2
+    start = FIRST_ROWS + count
+    out_w = out_w_ref[...].astype(f32)
+    local = (token_ref[...] - row).astype(f32)
+    spare = jnp.zeros((half, CA // 2 - mine), f32)
+    for target in range(targets):
+        part = out_w[:, target * mine : (target + 1) * mine]
+        packed = jnp.concatenate([part[:half], spare, part[half:], spare], axis=1)
+        slice_ref[target] = jnp.concatenate([packed, jnp.broadcast_to(local, (8, CA))], axis=0).astype(bf16)
+    early = [
+        pltpu.make_async_copy(
+            first_ref.at[:, pl.ds(0, FIRST_ROWS), :], send_ref.at[:, pl.ds(0, FIRST_ROWS), :], block_sem.at[0]
+        ),
+        pltpu.make_async_copy(slice_ref, send_ref.at[:, pl.ds(start + rows, half + 8), :], block_sem.at[1]),
+    ]
+    early += [
+        pltpu.make_async_copy(back_w_ref, send_ref.at[target, pl.ds(start, rows), :], back_sem.at[target])
+        for target in range(targets)
+    ]
+    for copy in early:
+        copy.start()
     lanes = lax.broadcasted_iota(jnp.int32, (1, CA), 1) // ATOM_HEAD
     keys = lax.broadcasted_iota(jnp.int32, (1, KW), 1)
     mix = pair_w_ref[...].astype(f32)
@@ -100,24 +138,18 @@
     gated = (jax.nn.sigmoid(gate) * attended).astype(bf16)
     mid = (atoms + dot(gated, wo_ref[...])).astype(bf16)
     mid_ref[...] = mid
-    local = (token_ref[...] - row).astype(f32).astype(bf16)
-    tail = jnp.broadcast_to(local, (16, count))
-    back_w = back_w_ref[...]
-    rows, width = out_w_ref.shape
-    targets = send_ref.shape[0]
-    mine = width // targets
-    out_w = out_w_ref[...].astype(f32)
-    blank = jnp.zeros((rows, CA - mine), bf16)
-    for target in range(targets):
-        part = out_w[:, target * mine : (target + 1) * mine].astype(bf16)
-        pieces = [first_ref[target], mid, tail, back_w, jnp.concatenate([part, blank], axis=1)]
-        start = 0
-        for piece in pieces:
-            send_ref[target, start : start + piece.shape[0], :] = piece
-            start += piece.shape[0]
-
-
-def pair_body(pair_refs, win_ref, wout_ref, wb_ref, out_ref, hold_ref):
+    hold_ref[...] = mid
+    late = [
+        pltpu.make_async_copy(hold_ref, send_ref.at[target, pl.ds(FIRST_ROWS, count), :], hold_sem.at[target])
+        for target in range(targets)
+    ]
+    for copy in late:
+        copy.start()
+    for copy in early + late:
+        copy.wait()
+
+
+def pair_body(pair_refs, win_ref, wout_ref, wb_ref, hold_ref):
     part, width, _ = pair_refs[0].shape
     rows = part * len(pair_refs)
     tile = jnp.concatenate([ref[...].reshape(part * width, CZ) for ref in pair_refs], axis=0)
@@ -133,7 +165,7 @@
     bias = dot(wb_ref[...], renewed.astype(bf16)) * lax.rsqrt(spread + epsilon)
     for i in range(rows):
         hold_ref[:, i, :] = bias[:, i * width : (i + 1) * width]
-    out_ref[...] = hold_ref[...].astype(bf16)
+    return hold_ref[...].astype(bf16)
 
 
 def centre():
@@ -143,50 +175,54 @@
 
 
 def pair_first(*refs):
-    *pair_refs, trans_in_ref, trans_out_ref, wb_ref, out_ref, done_ref, win_ref, wout_ref, hold_ref = refs
+    *pair_refs, trans_in_ref, trans_out_ref, wb_ref, out_ref, win_ref, wout_ref, hold_ref = refs
 
     @pl.when(pl.program_id(0) == 0)
     def _():
-        wide = trans_in_ref[...].astype(f32)
-        units = wide.shape[2]
-        win_ref[:units, :] = (wide[:, 0, :].T * 0.5).astype(bf16)
-        win_ref[units:, :] = wide[:, 1, :].T.astype(bf16)
+        units = win_ref.shape[0] // 2
+        parts = units // CZ
+        wide = dot(regrouped(win_ref.shape[0], 2 * parts), trans_in_ref[...])
+        for part in range(parts):
+            gate = wide[2 * part * CZ : (2 * part + 1) * CZ]
+            up = wide[(2 * part + 1) * CZ : (2 * part + 2) * CZ]
+            win_ref[part * CZ : (part + 1) * CZ, :] = (gate.T * 0.5).astype(bf16)
+            win_ref[units + part * CZ : units + (part + 1) * CZ, :] = up.T.astype(bf16)
         wout_ref[...] = dot_t(centre(), trans_out_ref[...]).astype(bf16)
 
-    pair_body(pair_refs, win_ref, wout_ref, wb_ref, out_ref, hold_ref)
+    rows = pl.ds(pl.multiple_of(pl.program_id(0) * PAIR_ROWS, PAIR_ROWS), PAIR_ROWS)
+    out_ref[:, rows, :] = pair_body(pair_refs, win_ref, wout_ref, wb_ref, hold_ref)
+
+
+def pair_rest(_, early_ref, *refs):
+    *pair_refs, win_ref, wout_ref, wb_ref, out_ref, done_ref, hold_ref = refs
     done_ref[...] = jnp.zeros_like(done_ref)
 
-
-def pair_rest(_, *refs):
-    *pair_refs, win_ref, wout_ref, wb_ref, out_ref, done_ref, hold_ref = refs
-    pair_body(pair_refs, win_ref, wout_ref, wb_ref, out_ref, hold_ref)
-    done_ref[...] = jnp.zeros_like(done_ref)
-
-
-def pair_call(kernel, pair, weights, start, stop, before, out_weights, mib):
-    steps = (stop - start) // PAIR_ROWS
+    @pl.when(pl.program_id(0) == 0)
+    def _():
+        out_ref[...] = early_ref[:, FIRST_ROWS:, :]
+
+    @pl.when(pl.program_id(0) > 0)
+    def _():
+        out_ref[...] = pair_body(pair_refs, win_ref, wout_ref, wb_ref, hold_ref)
+
+
+def pair_call(kernel, pair, before, weights, steps, block, out_specs, out_shape):
+    cols = pair.shape[1]
     vmem = pl.BlockSpec(memory_space=pltpu.VMEM)
-    skip = start // PAIR_ROWS
-    cols = pair.shape[1]
-    in_specs = [vmem] * len(before)
-    part = PAIR_ROWS // STREAMS
-    in_specs += [
-        pl.BlockSpec((part, cols, CZ), lambda i, k=k: ((i + skip) * STREAMS + k, 0, 0)) for k in range(STREAMS)
-    ]
-    in_specs += [vmem] * len(weights)
-    positions = (stop - start) * cols
+    positions = steps * PAIR_ROWS * cols
     return pl.pallas_call(
         kernel,
         grid=(steps,),
-        in_specs=in_specs,
-        out_specs=[pl.BlockSpec((HEADS, PAIR_ROWS, cols), lambda i: (0, i, 0))]
-        + [vmem] * (1 + len(out_weights)),
-        out_shape=[jax.ShapeDtypeStruct((HEADS, stop - start, cols), bf16), DONE, *out_weights],
+        in_specs=[vmem] * len(before)
+        + [pl.BlockSpec((PAIR_ROWS, cols, CZ), lambda i: (block(i), 0, 0))]
+        + [vmem] * len(weights),
+        out_specs=out_specs,
+        out_shape=out_shape,
         scratch_shapes=[pltpu.VMEM((HEADS, PAIR_ROWS, cols), f32)],
-        compiler_params=params(mib),
+        compiler_params=params(48),
         cost_estimate=cost(positions * 620_000, positions * 288),
         name="pair_bias",
-    )(*before, *[pair] * STREAMS, *weights)
+    )(*before, in_hbm(pair), *weights)
 
 
 def token_kernel(
@@ -200,7 +236,7 @@
     token = lax.broadcasted_iota(jnp.int32, (tokens, count), 0).astype(f32)
     onehot = jnp.concatenate(
         [
-            jnp.where(token == got_ref[s, ids : ids + 16, :].astype(f32)[:1], 1.0, 0.0)
+            jnp.where(token == got_ref[s, ids + HEAD + HEAD // 2 - 8 :, :].astype(f32)[8:9], 1.0, 0.0)
             for s in range(sources)
         ],
         axis=1,
@@ -216,15 +252,8 @@
     send_ref[...] = turned[HEAD : 3 * HEAD]
 
 
-def hops_of(rows):
-    hops = rows // CORES
-    return sorted(range(hops), key=lambda hop: -min(hop, hops - hop) if hop else -hops)
-
-
-def partner(row, rows, hop, cross):
-    hops = rows // CORES
-    chip, core = row // CORES, row % CORES
-    return (chip + hop + hops) % hops * CORES + (core + cross) % CORES
+def partner(row, hop, cross):
+    return (row // CORES ^ hop) * CORES + (row % CORES ^ cross)
 
 
 def chip_kernel(own_ref, other_ref, out_ref):
@@ -240,9 +269,9 @@
     query = held_ref[:, :tokens].astype(f32).T.astype(bf16)
     per = bias_ref.shape[0] // rows
     scores, values = [], []
-    for hop, kv_ref in zip(hops_of(rows), kv_refs):
+    for hop, kv_ref in enumerate(kv_refs):
         for cross in range(CORES):
-            source = partner(place_ref[4], rows, -hop, cross) * per
+            source = partner(place_ref[4], hop, cross) * per
             bias = jnp.concatenate(
                 [
                     jnp.concatenate([got_ref[source + k, :FIRST_ROWS, :], bias_ref[source + k]], axis=0)
@@ -273,11 +302,15 @@
     tokens, width = in_ref.shape
     mine = width // sources
     token_in = in_ref[...]
-    start = FIRST_ROWS + count + 16
+    start = FIRST_ROWS + count
     back_w = jnp.concatenate([got_ref[s, start : start + mine, :] for s in range(sources)], axis=0)
-    out_w = jnp.concatenate([got_ref[s, start + mine :, :] for s in range(sources)], axis=0)
+    half = mine // 2
+    packed = [got_ref[s, start + mine :, :].astype(f32)[:half] for s in range(sources)]
+    out_w = jnp.concatenate(
+        [jnp.concatenate([part, pltpu.roll(part, CA // 2, 1)], axis=0) for part in packed], axis=0
+    )
     mixed_ref[...] = dot(mine_ref[...], back_w).astype(bf16)
-    out_w_ref[...] = out_w.astype(f32).T[:mine].astype(bf16)
+    out_w_ref[...] = out_w.T[:mine].astype(bf16)
     back_ref[...] = dot_t(back_w.astype(f32).T.astype(bf16), token_in)
     wanted = lax.broadcasted_iota(jnp.int32, (mine, width), 0) + place_ref[3] * mine
     column = lax.broadcasted_iota(jnp.int32, (mine, width), 1)
@@ -341,10 +374,8 @@
     head_rows = token_wo.shape[0]
     both = ("row", "col")
     devices = row_size * col_size
-    up = [(i, i + 1) for i in range(devices - 1)]
-    down = [(j, i) for i, j in up]
-    before = lax.ppermute(atoms, both, up)
-    after = lax.ppermute(atoms, both, down)
+    pairs = [[(i, i + 1) for i in range(start, devices - 1, 2)] for start in range(2)]
+    swaps = [lax.ppermute(atoms, both, pair + [(j, i) for i, j in pair]) for pair in pairs]
 
     device = lax.axis_index(both)
     place = jnp.stack(
@@ -361,23 +392,52 @@
     token_row = atom_token.reshape(1, count)
 
     units = trans_in.shape[2]
-    first_bias, _, win, wout = pair_call(
-        pair_first, pair, (trans_in, trans_out, bias_w.T), 0, FIRST_ROWS, (),
-        (shape(2 * units, CZ), shape(CZ, units)), 56,
-    )
-    mid, mid_send, done = single_step(
+    trans_rows = trans_in.reshape(CZ, 2, units // CZ, CZ).transpose(0, 2, 1, 3).reshape(2 * units, CZ)
+    key_cols = pair.shape[1]
+    early, win, wout = pair_call(
+        pair_first,
+        pair,
+        (),
+        (in_hbm(trans_rows), in_hbm(trans_out), in_hbm(bias_w.T)),
+        EARLY_ROWS // PAIR_ROWS,
+        lambda i: i,
+        [vmem] * 3,
+        [shape(HEADS, EARLY_ROWS, key_cols), shape(2 * units, CZ), shape(CZ, units)],
+    )
+    misc = head_rows // 2 + 8
+    mid_send, mid, done = pl.pallas_call(
         atom_kernel,
-        "atom_stage",
-        [vmem, smem] + [vmem] * 10,
-        [shape(count, CA), shape(col_size, FIRST_ROWS + count + 16 + 2 * head_rows, CA), DONE],
-        4_000_000_000,
-        2_000_000,
-        (
-            first_bias, place, before, atoms, after, atom_pair, atom_pair_w.T, token_row, atom_w, atom_wo, token_wo, back_w,
-        ),
-    )
+        in_specs=[vmem, smem] + [vmem] * 10,
+        out_specs=[pl.BlockSpec(memory_space=pltpu.HBM), vmem, vmem],
+        out_shape=[
+            pltpu.HBM((col_size, FIRST_ROWS + count + head_rows + misc, CA), bf16),
+            shape(count, CA),
+            DONE,
+        ],
+        scratch_shapes=[
+            pltpu.VMEM((count, CA), bf16),
+            pltpu.VMEM((col_size, misc, CA), bf16),
+            pltpu.SemaphoreType.DMA((2,)),
+            pltpu.SemaphoreType.DMA((col_size,)),
+            pltpu.SemaphoreType.DMA((col_size,)),
+        ],
+        compiler_params=params(),
+        cost_estimate=cost(4_000_000_000, 2_000_000),
+        name="atom_stage",
+    )(early, place, swaps[0], atoms, swaps[1], atom_pair, atom_pair_w.T, token_row, atom_w.reshape(4 * CA, CA), atom_wo,
+      token_wo, back_w)
     mids = gathered(mid_send, "col")
-    bias, done = pair_call(pair_rest, pair, (win, wout, bias_w.T), FIRST_ROWS, query_rows, (done,), (), 52)
+    late_rows = query_rows - FIRST_ROWS
+    bias, done = pair_call(
+        pair_rest,
+        pair,
+        (done, early),
+        (win, wout, in_hbm(bias_w.T)),
+        late_rows // PAIR_ROWS,
+        lambda i: jnp.maximum(i, 1) + FIRST_ROWS // PAIR_ROWS,
+        [pl.BlockSpec((HEADS, PAIR_ROWS, key_cols), lambda i: (0, i, 0)), vmem],
+        [shape(HEADS, late_rows, key_cols), DONE],
+    )
     bias_rows = gathered(bias, "col")
 
     turned = jnp.transpose(token_w, (1, 2, 0)).reshape(4 * HEAD, width)
@@ -394,7 +454,7 @@
         2_000_000,
         (done, mids, single, agg_w, turned),
     )
-    across = lax.ppermute(kv_send, "row", [(i, partner(i, row_size, 0, 1)) for i in range(row_size)])
+    across = lax.ppermute(kv_send, "row", [(i, partner(i, 0, 1)) for i in range(row_size)])
     (chip_kv,) = single_step(
         chip_kernel,
         "chip_keys",
@@ -405,8 +465,8 @@
         (kv_send, across),
     )
     kv = [chip_kv] + [
-        lax.ppermute(chip_kv, "row", [(i, partner(i, row_size, hop, 0)) for i in range(row_size)])
-        for hop in hops_of(row_size)[1:]
+        lax.ppermute(chip_kv, "row", [(i, partner(i, hop, 0)) for i in range(row_size)])
+        for hop in range(1, row_size // CORES)
     ]
     out_w, own, back, onehot, mixed = single_step(
         ready_kernel,

time: 85.5 us -> 79.9 us (0.935)
  starting transfers between devices: 24 us -> 19.8 us
  blocking collectives: 16.6 us -> 14.8 us
  waiting for transfers between devices: 10.9 us -> 12.5 us
  local copies, waits for them, and re-layouts: 1.04 us -> 0.14 us
    ppermute x6, starting transfers between devices: 11 us -> 7.14 us  [the longest x3 4.17 us: body(): lax.ppermute(chip_kv, 'row', [(i, partner(i, hop, 0)) for i in range(row_...]
    pallas_call x6 -> x5, Pallas kernels: 10.1 us -> 6.68 us  [single_step(): pl.pallas_call(kernel, in_specs=in_specs, out_specs=[pl.BlockSpec(memory_...]
    pallas_call x2 -> x3, Pallas kernels: 21.5 us -> 24.7 us  [the longest x2 21 us: pair_call(): pl.pallas_call(kernel, grid=(steps,), in_specs=[vmem] * len(before) + [pl...]
    all_to_all x1, blocking collectives: 16.6 us -> 14.8 us  [gathered(): return lax.all_to_all(copies, axis, split_axis=0, concat_axis=0, tiled=True)]
    all_to_all x2, waiting for transfers between devices: 9.79 us -> 11.4 us  [gathered(): return lax.all_to_all(copies, axis, split_axis=0, concat_axis=0, tiled=True)]
    unnamed x30 -> x22, local copies, waits for them, and re-layouts: 0.95 us -> 0.05 us
  transfers between devices with their start and end apart: 8 -> 8, of which waited for: 4 -> 3; matrix products, arithmetic and copies ran while one was open for 0% -> 0% of each run, Pallas kernels for 29% -> 31%
where the time goes in v4:
time: 79.9 us; the launch traced here: 79.5 us
  Pallas kernels  31.4 us (39%)
  starting transfers between devices  19.8 us (25%)
  blocking collectives  14.8 us (19%)
  waiting for transfers between devices  12.5 us (16%)
  between operations  0.88 us (1%)
    pallas_call x2, Pallas kernels, pair_call(): pl.pallas_call(kernel, grid=(steps,), in_specs=[vmem] * len(before) + [pl...  21 us
    all_to_all x1, blocking collectives, gathered(): return lax.all_to_all(copies, axis, split_axis=0, concat_axis=0, tiled=True)  14.8 us
    all_to_all x2, starting transfers between devices, gathered(): return lax.all_to_all(copies, axis, split_axis=0, concat_axis=0, tiled=True)  12.7 us
    all_to_all x2, waiting for transfers between devices, gathered(): return lax.all_to_all(copies, axis, split_axis=0, concat_axis=0, tiled=True)  11.4 us
    pallas_call x5, Pallas kernels, single_step(): pl.pallas_call(kernel, in_specs=in_specs, out_specs=[pl.BlockSpec(memory_...  6.68 us
    ppermute x3, starting transfers between devices, body(): lax.ppermute(chip_kv, 'row', [(i, partner(i, hop, 0)) for i in range(row_...  4.17 us
    pallas_call x1, Pallas kernels, body(): pl.pallas_call(atom_kernel, in_specs=[vmem, smem] + [vmem] * 10, out_spec...  3.7 us
    ppermute x2, starting transfers between devices, body(): lax.ppermute(atoms, both, pair + [(j, i) for i, j in pair])  2.73 us
  transfers between devices with their start and end apart: 8, of which 3 were waited for; matrix products, arithmetic and copies ran while one was open for 0% of the time, Pallas kernels for 31%

profile of v4, /device:TPU:0, one launch (start us, length us, event | category | flops | bytes accessed | tf_op | source)
XLA Modules:
  0.0 79.5 jit_solution(17639010917035075124)
XLA Ops:
  0.6 2.1 %collective-permute-start = (bf16[128,128]{1,0:T(8,128)(2,1)}, bf16[128,128]{1,0:T(8,128)(2,1)S(1)}, u32[]{:S(2)}, u32[]{:S(2)}) collective-permute-start(bf16[128,128]{1,0:T(8,128)(2,1)} %own_ref.1), channel_id=1, source_target_pairs={{0,1},{2,3},{4,5},{6,7},{8,9},{10,11},{12,13},{14,15},{16,17},{18,... | collective-permute-start | bytes 98312 | tf_op jit(solution)/shard_map/ppermute | solution.py:378
  2.7 0.7 collective-permute-start.1
  3.4 0.0 copy-start
  3.4 0.0 copy-start.4
  3.4 0.0 copy-start.5
  3.4 0.0 copy-start.6
  3.4 0.0 copy-start.7
  3.4 0.0 copy-start.8
  3.4 0.0 copy-start.9
  3.4 0.0 copy-start.10
  3.5 6.0 %pair_bias.2 = (bf16[16,64,128]{2,1,0:T(8,128)(2,1)S(1)}, bf16[512,128]{1,0:T(8,128)(2,1)S(1)}, bf16[128,256]{1,0:T(8,128)(2,1)S(1)}) custom-call(bf16[256,128,128]{2,1,0:T(8,128)(2,1)} %refs_0_.3, bf16[512,128]{1,0:T(8,128)(2,1)} %bitcast.22, bf16[256,128]{1,0:T(8,128)(2,1)} %refs_2_.1, bf16[16,128]{1,0:T(8,128)(2,1)} %bitcast.23), custom_call_target="tpu_custom_call" | custom-call | flops 5079040000 | bytes 2359296 | tf_op jit(solution)/shard_map/pair_bias/pallas_call | solution.py:213
  9.5 0.1 stack.19.place_ref
  9.6 0.0 collective-permute-done.even_ref
  9.6 0.0 collective-permute-done.1.odd_ref
  9.6 0.0 copy-done
  9.6 0.0 copy-done.4
  9.6 0.0 copy-done.5
  9.6 0.0 copy-done.6
  9.6 0.0 copy-done.7
  9.6 0.0 copy-done.8
  9.7 0.0 copy-done.9
  9.7 0.0 copy-done.10
  9.7 3.7 %atom_stage.1 = (bf16[16,240,128]{2,1,0:T(8,128)(2,1)}, bf16[128,128]{1,0:T(8,128)(2,1)S(1)}, f32[8,128]{1,0:T(8,128)S(1)}) custom-call(bf16[16,64,128]{2,1,0:T(8,128)(2,1)S(1)} %get-tuple-element.20.first_ref.early_ref, s32[5]{0:T(128)S(1)} %stack.19.place_ref, bf16[128,128]{1,0:T(8,128)(2,1)S(1)} %collective-permute-done.even_ref, ...), custom_call_target="tpu_custom_call" | custom-call | flops 4000000000 | bytes 2000000 | tf_op jit(solution)/shard_map/atom_stage/pallas_call | solution.py:408
  13.4 9.0 %all-to-all-start = ((bf16[16,240,128]{2,1,0:T(8,128)(2,1)}), bf16[16,240,128]{2,1,0:T(8,128)(2,1)S(1)}, u32[]{:S(2)}, u32[]{:S(2)}) async-start(bf16[16,240,128]{2,1,0:T(8,128)(2,1)} %get-tuple-element.25), calls=%async_computation | async-start | bytes 1966080 | tf_op jit(solution)/shard_map/all_to_all | solution.py:351
  22.4 0.0 copy-start.1
  22.4 0.0 copy-start.2
  22.4 0.0 copy-start.3
  22.4 15.0 %pair_bias.3 = (bf16[16,224,128]{2,1,0:T(8,128)(2,1)}, f32[8,128]{1,0:T(8,128)S(1)}) custom-call(f32[8,128]{1,0:T(8,128)S(1)} %get-tuple-element.21._, bf16[16,64,128]{2,1,0:T(8,128)(2,1)S(1)} %get-tuple-element.20.first_ref.early_ref, bf16[256,128,128]{2,1,0:T(8,128)(2,1)} %refs_0_.3, bf16[512,128]{1,0:T(8,128)(2,1)S(1)} %get-tuple-element.22.refs_1_, ...), custom_call_target="tpu_custom_call" | custom-call | flops 17776640000 | bytes 8257536 | tf_op jit(solution)/shard_map/pair_bias/pallas_call | solution.py:213
  37.4 3.5 %all-to-all-done.got_ref = bf16[16,240,128]{2,1,0:T(8,128)(2,1)S(1)} async-done(((bf16[16,240,128]{2,1,0:T(8,128)(2,1)}), bf16[16,240,128]{2,1,0:T(8,128)(2,1)S(1)}, u32[]{:S(2)}, u32[]{:S(2)}) %all-to-all-start) | async-done | bytes 983072 | tf_op jit(solution)/shard_map/all_to_all | solution.py:351
  40.8 3.7 %all-to-all-start.1 = ((bf16[16,224,128]{2,1,0:T(8,128)(2,1)}), bf16[16,224,128]{2,1,0:T(8,128)(2,1)S(1)}, u32[]{:S(2)}, u32[]{:S(2)}) async-start(bf16[16,224,128]{2,1,0:T(8,128)(2,1)} %get-tuple-element.29), calls=%async_computation.1 | async-start | bytes 1835008 | tf_op jit(solution)/shard_map/all_to_all | solution.py:351
  44.6 0.0 copy-done.1
  44.6 0.0 copy-done.2
  44.6 0.0 copy-done.3
  44.6 2.5 %token_stage.1 = (bf16[256,768]{1,0:T(8,128)(2,1)S(1)}, bf16[48,512]{1,0:T(8,128)(2,1)S(1)}, bf16[96,256]{1,0:T(8,128)(2,1)S(1)}) custom-call(f32[8,128]{1,0:T(8,128)S(1)} %get-tuple-element.24._, bf16[16,240,128]{2,1,0:T(8,128)(2,1)S(1)} %all-to-all-done.got_ref, bf16[256,768]{1,0:T(8,128)(2,1)S(1)} %copy-done.1, bf16[128,768]{1,0:T(8,128)(2,1)S(1)} %copy-done.3, ...), custom_call_target="tpu_custom_call" | custom-call | flops 4000000000 | bytes 2000000 | tf_op jit(solution)/shard_map/token_stage/pallas_call | solution.py:339
  47.1 0.2 collective-permute-start.2
  47.3 1.1 %collective-permute-done.2.other_ref = bf16[96,256]{1,0:T(8,128)(2,1)S(1)} collective-permute-done((bf16[96,256]{1,0:T(8,128)(2,1)S(1)}, bf16[96,256]{1,0:T(8,128)(2,1)S(1)}, u32[]{:S(2)}, u32[]{:S(2)}) %collective-permute-start.2) | collective-permute-done | bytes 49184 | tf_op jit(solution)/shard_map/ppermute | solution.py:457
  48.4 3.1 %collective-permute-start.5 = (bf16[192,256]{1,0:T(8,128)(2,1)S(1)}, bf16[192,256]{1,0:T(8,128)(2,1)S(1)}, u32[]{:S(2)}, u32[]{:S(2)}) collective-permute-start(bf16[192,256]{1,0:T(8,128)(2,1)S(1)} %chip_keys.1.refs_0_), channel_id=1, source_target_pairs={{0,96},{16,112},{32,64},{48,80},{64,32},{80,48},{96,0},{112,16},{1... | collective-permute-start | bytes 294920 | tf_op jit(solution)/shard_map/ppermute | solution.py:468
  51.5 0.6 collective-permute-start.4
  52.1 0.5 collective-permute-start.3
  52.6 0.9 %out_ready.1 = (bf16[48,768]{1,0:T(8,128)(2,1)S(1)}, f32[48,256]{1,0:T(8,128)S(1)}, f32[128,256]{1,0:T(8,128)S(1)}, bf16[128,256]{1,0:T(8,128)(2,1)S(1)}, bf16[48,128]{1,0:T(8,128)(2,1)S(1)}) custom-call(s32[5]{0:T(128)S(1)} %stack.19.place_ref, bf16[16,240,128]{2,1,0:T(8,128)(2,1)S(1)} %all-to-all-done.got_ref, ...), custom_call_target="tpu_custom_call" | custom-call | flops 2000000000 | bytes 2000000 | tf_op jit(solution)/shard_map/out_ready/pallas_call | solution.py:339
  53.5 7.9 %all-to-all-done.1.bias_ref = bf16[16,224,128]{2,1,0:T(8,128)(2,1)S(1)} async-done(((bf16[16,224,128]{2,1,0:T(8,128)(2,1)}), bf16[16,224,128]{2,1,0:T(8,128)(2,1)S(1)}, u32[]{:S(2)}, u32[]{:S(2)}) %all-to-all-start.1) | async-done | bytes 917536 | tf_op jit(solution)/shard_map/all_to_all | solution.py:351
  61.4 0.0 collective-permute-done.5.refs_3_
  61.4 0.0 collective-permute-done.4.refs_2_
  61.4 0.0 collective-permute-done.3.refs_1_
  61.4 2.2 %token_attention.1 = bf16[16,48,384]{2,1,0:T(8,128)(2,1)S(1)} custom-call(s32[5]{0:T(128)S(1)} %stack.19.place_ref, bf16[48,512]{1,0:T(8,128)(2,1)S(1)} %get-tuple-element.26.held_ref, bf16[48,128]{1,0:T(8,128)(2,1)S(1)} %get-tuple-element.28.mixed_ref, bf16[16,240,128]{2,1,0:T(8,128)(2,1)S(1)} %all-to-all-done.got_ref, ...), custom_call_target="tpu_custom_call" | custom-call | flops 3000000000 | bytes 2000000 | tf_op jit(solution)/shard_map/token_attention/pallas_call | solution.py:339
  63.6 14.8 %all_to_all.15.got_ref = bf16[16,48,384]{2,1,0:T(8,128)(2,1)S(1)} all-to-all(bf16[16,48,384]{2,1,0:T(8,128)(2,1)S(1)} %token_attention.1), channel_id=1, replica_groups=mesh['row'=8,'col'=16] {'col'}, dimensions={0} | all-to-all | bytes 1179648 | tf_op jit(solution)/shard_map/all_to_all | solution.py:351
  78.4 1.1 %token_out.1 = (bf16[48,256]{1,0:T(8,128)(2,1)}, bf16[128,128]{1,0:T(8,128)(2,1)}) custom-call(bf16[16,48,384]{2,1,0:T(8,128)(2,1)S(1)} %all_to_all.15.got_ref, bf16[48,768]{1,0:T(8,128)(2,1)S(1)} %get-tuple-element.31.out_w_ref, f32[48,256]{1,0:T(8,128)S(1)} %get-tuple-element.32.own_ref, f32[128,256]{1,0:T(8,128)S(1)} %get-tuple-element.33.back_ref, ...), custom_call_target="tpu_custom_call" | custom-call | flops 2000000000 | bytes 2000000 | tf_op jit(solution)/shard_map/token_out/pallas_call | solution.py:339
  (1 shorter events, 0.0 us)
Async XLA Ops:
  0.6 9.0 %collective-permute-start = (bf16[128,128]{1,0:T(8,128)(2,1)}, bf16[128,128]{1,0:T(8,128)(2,1)S(1)}, u32[]{:S(2)}, u32[]{:S(2)}) collective-permute-start(bf16[128,128]{1,0:T(8,128)(2,1)} %own_ref.1), channel_id=1, source_target_pairs={{0,1},{2,3},{4,5},{6,7},{8,9},{10,11},{12,13},{14,15},{16,17},{18,... | collective-permute-start | bytes 98312 | tf_op jit(solution)/shard_map/ppermute | solution.py:378
  2.7 6.9 %collective-permute-start.1 = (bf16[128,128]{1,0:T(8,128)(2,1)}, bf16[128,128]{1,0:T(8,128)(2,1)S(1)}, u32[]{:S(2)}, u32[]{:S(2)}) collective-permute-start(bf16[128,128]{1,0:T(8,128)(2,1)} %own_ref.1), channel_id=1, source_target_pairs={{1,2},{3,4},{5,6},{7,8},{9,10},{11,12},{13,14},{15,16},{17,18},{19... | collective-permute-start | bytes 98312 | tf_op jit(solution)/shard_map/ppermute | solution.py:378
  3.4 6.2 %copy-start = (bf16[4,16,32,128]{3,2,1,0:T(8,128)(2,1)S(1)}, bf16[4,16,32,128]{3,2,1,0:T(8,128)(2,1)}, u32[]{:S(2)}) copy-start(bf16[4,16,32,128]{3,2,1,0:T(8,128)(2,1)} %atom_pair_ref.1) | copy-start | bytes 1572868
  3.4 6.2 %copy-start.4 = (bf16[128,4,128]{2,1,0:T(4,128)(2,1)S(1)}, bf16[128,4,128]{2,1,0:T(4,128)(2,1)}, u32[]{:S(2)}) copy-start(bf16[128,4,128]{2,1,0:T(4,128)(2,1)} %param.20) | copy-start | bytes 393220
  3.4 6.2 %copy-start.5 = (bf16[48,768]{1,0:T(8,128)(2,1)S(1)}, bf16[48,768]{1,0:T(8,128)(2,1)}, u32[]{:S(2)}) copy-start(bf16[48,768]{1,0:T(8,128)(2,1)} %mine_ref.1) | copy-start | bytes 221188
  3.4 6.2 %copy-start.6 = (bf16[128,128]{1,0:T(8,128)(2,1)S(1)}, bf16[128,128]{1,0:T(8,128)(2,1)}, u32[]{:S(2)}) copy-start(bf16[128,128]{1,0:T(8,128)(2,1)} %own_ref.1) | copy-start | bytes 98308
  3.4 6.2 %copy-start.7 = (bf16[128,128]{1,0:T(8,128)(2,1)S(1)}, bf16[128,128]{1,0:T(8,128)(2,1)}, u32[]{:S(2)}) copy-start(bf16[128,128]{1,0:T(8,128)(2,1)} %wo_ref.1) | copy-start | bytes 98308
  3.4 6.2 %copy-start.8 = (bf16[48,128]{1,0:T(8,128)(2,1)S(1)}, bf16[48,128]{1,0:T(8,128)(2,1)}, u32[]{:S(2)}) copy-start(bf16[48,128]{1,0:T(8,128)(2,1)} %back_w_ref.1) | copy-start | bytes 36868
  3.4 6.2 %copy-start.9 = (bf16[16,4]{0,1:T(4,128)(2,1)S(1)}, bf16[16,4]{0,1:T(4,128)(2,1)}, u32[]{:S(2)}) copy-start(bf16[16,4]{0,1:T(4,128)(2,1)} %param.21) | copy-start | bytes 388
  3.4 6.2 %copy-start.10 = (s32[128]{0:T(128)S(1)}, s32[128]{0:T(128)}, u32[]{:S(2)}) copy-start(s32[128]{0:T(128)} %param.17) | copy-start | bytes 1540
  13.4 27.4 %all-to-all-start = ((bf16[16,240,128]{2,1,0:T(8,128)(2,1)}), bf16[16,240,128]{2,1,0:T(8,128)(2,1)S(1)}, u32[]{:S(2)}, u32[]{:S(2)}) async-start(bf16[16,240,128]{2,1,0:T(8,128)(2,1)} %get-tuple-element.25), calls=%async_computation | async-start | bytes 1966080 | tf_op jit(solution)/shard_map/all_to_all | solution.py:351
  22.4 22.2 %copy-start.1 = (bf16[256,768]{1,0:T(8,128)(2,1)S(1)}, bf16[256,768]{1,0:T(8,128)(2,1)}, u32[]{:S(2)}) copy-start(bf16[256,768]{1,0:T(8,128)(2,1)} %single_ref.1) | copy-start | bytes 1179652
  22.4 22.2 %copy-start.2 = (bf16[768,4,48]{0,2,1:T(8,128)(2,1)S(1)}, bf16[768,4,48]{0,2,1:T(8,128)(2,1)}, u32[]{:S(2)}) copy-start(bf16[768,4,48]{0,2,1:T(8,128)(2,1)} %param.27) | copy-start | bytes 884740
  22.4 22.2 %copy-start.3 = (bf16[128,768]{1,0:T(8,128)(2,1)S(1)}, bf16[128,768]{1,0:T(8,128)(2,1)}, u32[]{:S(2)}) copy-start(bf16[128,768]{1,0:T(8,128)(2,1)} %agg_ref.1) | copy-start | bytes 589828
  40.8 20.5 %all-to-all-start.1 = ((bf16[16,224,128]{2,1,0:T(8,128)(2,1)}), bf16[16,224,128]{2,1,0:T(8,128)(2,1)S(1)}, u32[]{:S(2)}, u32[]{:S(2)}) async-start(bf16[16,224,128]{2,1,0:T(8,128)(2,1)} %get-tuple-element.29), calls=%async_computation.1 | async-start | bytes 1835008 | tf_op jit(solution)/shard_map/all_to_all | solution.py:351
  47.1 1.3 %collective-permute-start.2 = (bf16[96,256]{1,0:T(8,128)(2,1)S(1)}, bf16[96,256]{1,0:T(8,128)(2,1)S(1)}, u32[]{:S(2)}, u32[]{:S(2)}) collective-permute-start(bf16[96,256]{1,0:T(8,128)(2,1)S(1)} %get-tuple-element.30.own_ref), channel_id=1, source_target_pairs={{0,16},{16,0},{32,48},{48,32},{64,80},{80,64},{96,112},{112,96},{1... | collective-permute-start | bytes 147464 | tf_op jit(solution)/shard_map/ppermute | solution.py:457
  48.4 13.0 %collective-permute-start.5 = (bf16[192,256]{1,0:T(8,128)(2,1)S(1)}, bf16[192,256]{1,0:T(8,128)(2,1)S(1)}, u32[]{:S(2)}, u32[]{:S(2)}) collective-permute-start(bf16[192,256]{1,0:T(8,128)(2,1)S(1)} %chip_keys.1.refs_0_), channel_id=1, source_target_pairs={{0,96},{16,112},{32,64},{48,80},{64,32},{80,48},{96,0},{112,16},{1... | collective-permute-start | bytes 294920 | tf_op jit(solution)/shard_map/ppermute | solution.py:468
  51.5 9.9 %collective-permute-start.4 = (bf16[192,256]{1,0:T(8,128)(2,1)S(1)}, bf16[192,256]{1,0:T(8,128)(2,1)S(1)}, u32[]{:S(2)}, u32[]{:S(2)}) collective-permute-start(bf16[192,256]{1,0:T(8,128)(2,1)S(1)} %chip_keys.1.refs_0_), channel_id=1, source_target_pairs={{0,64},{16,80},{32,96},{48,112},{64,0},{80,16},{96,32},{112,48},{1... | collective-permute-start | bytes 294920 | tf_op jit(solution)/shard_map/ppermute | solution.py:468
  52.1 9.3 %collective-permute-start.3 = (bf16[192,256]{1,0:T(8,128)(2,1)S(1)}, bf16[192,256]{1,0:T(8,128)(2,1)S(1)}, u32[]{:S(2)}, u32[]{:S(2)}) collective-permute-start(bf16[192,256]{1,0:T(8,128)(2,1)S(1)} %chip_keys.1.refs_0_), channel_id=1, source_target_pairs={{0,32},{16,48},{32,0},{48,16},{64,96},{80,112},{96,64},{112,80},{1... | collective-permute-start | bytes 294920 | tf_op jit(solution)/shard_map/ppermute | solution.py:468

commit v5 on v4

--- a/solution.py
+++ b/solution.py
@@ -18,6 +18,7 @@
 KW = 128
 RIM = (KW - QW) // 2
 CORES = 2
+COPIES = 4
 PAIR_ROWS = 32
 FIRST_ROWS = 32
 EARLY_ROWS = 64
@@ -56,16 +57,21 @@
     return pl.CostEstimate(flops=flops, bytes_accessed=moved, transcendentals=0)
 
 
-def regrouped(size, groups):
-    row = lax.broadcasted_iota(jnp.int32, (size, size), 0)
-    column = lax.broadcasted_iota(jnp.int32, (size, size), 1)
-    length = size // groups
-    return jnp.where(column == (row % length) * groups + row // length, 1.0, 0.0).astype(bf16)
+def regrouped(rows, groups):
+    row = lax.broadcasted_iota(jnp.int32, (CZ, CZ), 0)
+    column = lax.broadcasted_iota(jnp.int32, (CZ, CZ), 1)
+    length = CZ // groups
+    order = jnp.where(column == (row % length) * groups + row // length, 1.0, 0.0).astype(bf16)
+    blocks = [dot(order, rows[start : start + CZ]) for start in range(0, rows.shape[0], CZ)]
+    return [
+        jnp.concatenate([block[group * length : (group + 1) * length] for block in blocks], axis=0)
+        for group in range(groups)
+    ]
 
 
 def atom_kernel(
     first_ref, place_ref, even_ref, own_ref, odd_ref, atom_pair_ref, pair_w_ref, token_ref, w_ref, wo_ref,
-    out_w_ref, back_w_ref, send_ref, mid_ref, done_ref, hold_ref, slice_ref, block_sem, hold_sem, back_sem,
+    out_w_ref, back_w_ref, send_ref, mid_ref, done_ref, hold_ref, slice_ref, block_sem, hold_sem,
 ):
     done_ref[...] = jnp.zeros_like(done_ref)
     device, row, last = place_ref[0], place_ref[1], place_ref[2]
@@ -76,31 +82,28 @@
     after = jnp.where(odd, odd_ref[:RIM, :].astype(f32), even_ref[:RIM, :].astype(f32))
     extended = jnp.concatenate([before, atoms, after], axis=0)
     norm = layer_norm(extended).astype(bf16)
-    sorted_w = dot(regrouped(4 * CA, 4), w_ref[...]).astype(bf16)
     query_all, key_all, value_all, gate_all = [
-        dot(norm, sorted_w[m * CA : (m + 1) * CA]).astype(bf16) for m in range(4)
+        dot(norm, part.astype(bf16)).astype(bf16) for part in regrouped(w_ref[...], 4)
     ]
     targets = send_ref.shape[0]
     rows, width = out_w_ref.shape
     mine = width // targets
     half = rows // 2
     start = FIRST_ROWS + count
+    back_w = back_w_ref[...]
     out_w = out_w_ref[...].astype(f32)
     local = (token_ref[...] - row).astype(f32)
     spare = jnp.zeros((half, CA // 2 - mine), f32)
     for target in range(targets):
         part = out_w[:, target * mine : (target + 1) * mine]
         packed = jnp.concatenate([part[:half], spare, part[half:], spare], axis=1)
-        slice_ref[target] = jnp.concatenate([packed, jnp.broadcast_to(local, (8, CA))], axis=0).astype(bf16)
+        slice_ref[target, :rows] = back_w
+        slice_ref[target, rows:] = jnp.concatenate([packed, jnp.broadcast_to(local, (8, CA))], axis=0).astype(bf16)
     early = [
         pltpu.make_async_copy(
             first_ref.at[:, pl.ds(0, FIRST_ROWS), :], send_ref.at[:, pl.ds(0, FIRST_ROWS), :], block_sem.at[0]
         ),
-        pltpu.make_async_copy(slice_ref, send_ref.at[:, pl.ds(start + rows, half + 8), :], block_sem.at[1]),
-    ]
-    early += [
-        pltpu.make_async_copy(back_w_ref, send_ref.at[target, pl.ds(start, rows), :], back_sem.at[target])
-        for target in range(targets)
+        pltpu.make_async_copy(slice_ref, send_ref.at[:, pl.ds(start, rows + half + 8), :], block_sem.at[1]),
     ]
     for copy in early:
         copy.start()
@@ -138,10 +141,16 @@
     gated = (jax.nn.sigmoid(gate) * attended).astype(bf16)
     mid = (atoms + dot(gated, wo_ref[...])).astype(bf16)
     mid_ref[...] = mid
-    hold_ref[...] = mid
+    for target in range(targets):
+        hold_ref[target] = mid
+    step = targets // COPIES
     late = [
-        pltpu.make_async_copy(hold_ref, send_ref.at[target, pl.ds(FIRST_ROWS, count), :], hold_sem.at[target])
-        for target in range(targets)
+        pltpu.make_async_copy(
+            hold_ref.at[pl.ds(part * step, step)],
+            send_ref.at[pl.ds(part * step, step), pl.ds(FIRST_ROWS, count), :],
+            hold_sem.at[part],
+        )
+        for part in range(COPIES)
     ]
     for copy in late:
         copy.start()
@@ -181,10 +190,9 @@
     def _():
         units = win_ref.shape[0] // 2
         parts = units // CZ
-        wide = dot(regrouped(win_ref.shape[0], 2 * parts), trans_in_ref[...])
+        groups = regrouped(trans_in_ref[...], 2 * parts)
         for part in range(parts):
-            gate = wide[2 * part * CZ : (2 * part + 1) * CZ]
-            up = wide[(2 * part + 1) * CZ : (2 * part + 2) * CZ]
+            gate, up = groups[2 * part : 2 * part + 2]
             win_ref[part * CZ : (part + 1) * CZ, :] = (gate.T * 0.5).astype(bf16)
             win_ref[units + part * CZ : units + (part + 1) * CZ, :] = up.T.astype(bf16)
         wout_ref[...] = dot_t(centre(), trans_out_ref[...]).astype(bf16)
@@ -283,10 +291,11 @@
             scores.append(dot(query, kv_ref[start : start + HEAD, :]) / math.sqrt(HEAD) + bias)
             values.append(kv_ref[start + HEAD : start + 2 * HEAD, :])
     scores = jnp.concatenate(scores, axis=1)
-    raised = jnp.exp(scores - jnp.max(scores, axis=-1, keepdims=True))
-    weights = (raised / jnp.sum(raised, axis=-1, keepdims=True)).astype(bf16)
+    raised = jnp.exp(scores - jnp.max(scores, axis=-1, keepdims=True)).astype(bf16)
     values = jnp.concatenate(values, axis=1)
-    attended = dot_t(values, weights)
+    ones = jnp.ones((16, values.shape[1]), bf16)
+    mixed = dot_t(jnp.concatenate([values, ones], axis=0), raised)
+    attended = mixed[:HEAD] / mixed[HEAD : HEAD + 1]
     gate = held_ref[:, tokens:].astype(f32)
     gated = (jax.nn.sigmoid(gate) * attended).astype(bf16)
     back = mixed_ref[...]
@@ -415,11 +424,10 @@
             DONE,
         ],
         scratch_shapes=[
-            pltpu.VMEM((count, CA), bf16),
-            pltpu.VMEM((col_size, misc, CA), bf16),
+            pltpu.VMEM((col_size, count, CA), bf16),
+            pltpu.VMEM((col_size, head_rows + misc, CA), bf16),
             pltpu.SemaphoreType.DMA((2,)),
-            pltpu.SemaphoreType.DMA((col_size,)),
-            pltpu.SemaphoreType.DMA((col_size,)),
+            pltpu.SemaphoreType.DMA((COPIES,)),
         ],
         compiler_params=params(),
         cost_estimate=cost(4_000_000_000, 2_000_000),

time: 79.9 us -> 79.1 us (0.990)
  Pallas kernels: 31.4 us -> 30.6 us
where the time goes in v5:
time: 79.1 us; the launch traced here: 78.8 us
  Pallas kernels  30.6 us (39%)
  starting transfers between devices  19.8 us (25%)
  blocking collectives  14.8 us (19%)
  waiting for transfers between devices  12.5 us (16%)
  between operations  0.88 us (1%)
    pallas_call x2, Pallas kernels, pair_call(): pl.pallas_call(kernel, grid=(steps,), in_specs=[vmem] * len(before) + [pl...  20.8 us
    all_to_all x1, blocking collectives, gathered(): return lax.all_to_all(copies, axis, split_axis=0, concat_axis=0, tiled=True)  14.8 us
    all_to_all x2, starting transfers between devices, gathered(): return lax.all_to_all(copies, axis, split_axis=0, concat_axis=0, tiled=True)  12.7 us
    all_to_all x2, waiting for transfers between devices, gathered(): return lax.all_to_all(copies, axis, split_axis=0, concat_axis=0, tiled=True)  11.4 us
    pallas_call x5, Pallas kernels, single_step(): pl.pallas_call(kernel, in_specs=in_specs, out_specs=[pl.BlockSpec(memory_...  6.44 us
    ppermute x3, starting transfers between devices, body(): lax.ppermute(chip_kv, 'row', [(i, partner(i, hop, 0)) for i in range(row_...  4.17 us
    pallas_call x1, Pallas kernels, body(): pl.pallas_call(atom_kernel, in_specs=[vmem, smem] + [vmem] * 10, out_spec...  3.37 us
    ppermute x2, starting transfers between devices, body(): lax.ppermute(atoms, both, pair + [(j, i) for i, j in pair])  2.73 us
  transfers between devices with their start and end apart: 8, of which 3 were waited for; matrix products, arithmetic and copies ran while one was open for 0% of the time, Pallas kernels for 31%

profile of v5, /device:TPU:0, one launch (start us, length us, event | category | flops | bytes accessed | tf_op | source)
XLA Modules:
  0.0 78.8 jit_solution(18257354990618807337)
XLA Ops:
  0.6 2.1 %collective-permute-start = (bf16[128,128]{1,0:T(8,128)(2,1)}, bf16[128,128]{1,0:T(8,128)(2,1)S(1)}, u32[]{:S(2)}, u32[]{:S(2)}) collective-permute-start(bf16[128,128]{1,0:T(8,128)(2,1)} %own_ref.1), channel_id=1, source_target_pairs={{0,1},{2,3},{4,5},{6,7},{8,9},{10,11},{12,13},{14,15},{16,17},{18,... | collective-permute-start | bytes 98312 | tf_op jit(solution)/shard_map/ppermute | solution.py:387
  2.7 0.7 collective-permute-start.1
  3.4 0.0 copy-start
  3.4 0.0 copy-start.4
  3.4 0.0 copy-start.5
  3.4 0.0 copy-start.6
  3.4 0.0 copy-start.7
  3.4 0.0 copy-start.8
  3.4 0.0 copy-start.9
  3.4 0.0 copy-start.10
  3.5 5.9 %pair_bias.2 = (bf16[16,64,128]{2,1,0:T(8,128)(2,1)S(1)}, bf16[512,128]{1,0:T(8,128)(2,1)S(1)}, bf16[128,256]{1,0:T(8,128)(2,1)S(1)}) custom-call(bf16[256,128,128]{2,1,0:T(8,128)(2,1)} %refs_0_.3, bf16[512,128]{1,0:T(8,128)(2,1)} %bitcast.22, bf16[256,128]{1,0:T(8,128)(2,1)} %refs_2_.1, bf16[16,128]{1,0:T(8,128)(2,1)} %bitcast.23), custom_call_target="tpu_custom_call" | custom-call | flops 5079040000 | bytes 2359296 | tf_op jit(solution)/shard_map/pair_bias/pallas_call | solution.py:221
  9.3 0.1 stack.19.place_ref
  9.4 0.0 collective-permute-done.even_ref
  9.4 0.0 collective-permute-done.1.odd_ref
  9.4 0.0 copy-done
  9.4 0.0 copy-done.4
  9.5 0.0 copy-done.5
  9.5 0.0 copy-done.6
  9.5 0.0 copy-done.7
  9.5 0.0 copy-done.8
  9.5 0.0 copy-done.9
  9.5 0.0 copy-done.10
  9.5 3.4 %atom_stage.1 = (bf16[16,240,128]{2,1,0:T(8,128)(2,1)}, bf16[128,128]{1,0:T(8,128)(2,1)S(1)}, f32[8,128]{1,0:T(8,128)S(1)}) custom-call(bf16[16,64,128]{2,1,0:T(8,128)(2,1)S(1)} %get-tuple-element.20.first_ref.early_ref, s32[5]{0:T(128)S(1)} %stack.19.place_ref, bf16[128,128]{1,0:T(8,128)(2,1)S(1)} %collective-permute-done.even_ref, ...), custom_call_target="tpu_custom_call" | custom-call | flops 4000000000 | bytes 2000000 | tf_op jit(solution)/shard_map/atom_stage/pallas_call | solution.py:417
  12.9 9.0 %all-to-all-start = ((bf16[16,240,128]{2,1,0:T(8,128)(2,1)}), bf16[16,240,128]{2,1,0:T(8,128)(2,1)S(1)}, u32[]{:S(2)}, u32[]{:S(2)}) async-start(bf16[16,240,128]{2,1,0:T(8,128)(2,1)} %get-tuple-element.25), calls=%async_computation | async-start | bytes 1966080 | tf_op jit(solution)/shard_map/all_to_all | solution.py:360
  21.9 0.0 copy-start.1
  21.9 0.0 copy-start.2
  21.9 0.0 copy-start.3
  21.9 15.0 %pair_bias.3 = (bf16[16,224,128]{2,1,0:T(8,128)(2,1)}, f32[8,128]{1,0:T(8,128)S(1)}) custom-call(f32[8,128]{1,0:T(8,128)S(1)} %get-tuple-element.21._, bf16[16,64,128]{2,1,0:T(8,128)(2,1)S(1)} %get-tuple-element.20.first_ref.early_ref, bf16[256,128,128]{2,1,0:T(8,128)(2,1)} %refs_0_.3, bf16[512,128]{1,0:T(8,128)(2,1)S(1)} %get-tuple-element.22.refs_1_, ...), custom_call_target="tpu_custom_call" | custom-call | flops 17776640000 | bytes 8257536 | tf_op jit(solution)/shard_map/pair_bias/pallas_call | solution.py:221
  36.9 3.5 %all-to-all-done.got_ref = bf16[16,240,128]{2,1,0:T(8,128)(2,1)S(1)} async-done(((bf16[16,240,128]{2,1,0:T(8,128)(2,1)}), bf16[16,240,128]{2,1,0:T(8,128)(2,1)S(1)}, u32[]{:S(2)}, u32[]{:S(2)}) %all-to-all-start) | async-done | bytes 983072 | tf_op jit(solution)/shard_map/all_to_all | solution.py:360
  40.3 3.7 %all-to-all-start.1 = ((bf16[16,224,128]{2,1,0:T(8,128)(2,1)}), bf16[16,224,128]{2,1,0:T(8,128)(2,1)S(1)}, u32[]{:S(2)}, u32[]{:S(2)}) async-start(bf16[16,224,128]{2,1,0:T(8,128)(2,1)} %get-tuple-element.29), calls=%async_computation.1 | async-start | bytes 1835008 | tf_op jit(solution)/shard_map/all_to_all | solution.py:360
  44.1 0.0 copy-done.1
  44.1 0.0 copy-done.2
  44.1 0.0 copy-done.3
  44.1 2.5 %token_stage.1 = (bf16[256,768]{1,0:T(8,128)(2,1)S(1)}, bf16[48,512]{1,0:T(8,128)(2,1)S(1)}, bf16[96,256]{1,0:T(8,128)(2,1)S(1)}) custom-call(f32[8,128]{1,0:T(8,128)S(1)} %get-tuple-element.24._, bf16[16,240,128]{2,1,0:T(8,128)(2,1)S(1)} %all-to-all-done.got_ref, bf16[256,768]{1,0:T(8,128)(2,1)S(1)} %copy-done.1, bf16[128,768]{1,0:T(8,128)(2,1)S(1)} %copy-done.3, ...), custom_call_target="tpu_custom_call" | custom-call | flops 4000000000 | bytes 2000000 | tf_op jit(solution)/shard_map/token_stage/pallas_call | solution.py:348
  46.6 0.2 collective-permute-start.2
  46.8 1.1 %collective-permute-done.2.other_ref = bf16[96,256]{1,0:T(8,128)(2,1)S(1)} collective-permute-done((bf16[96,256]{1,0:T(8,128)(2,1)S(1)}, bf16[96,256]{1,0:T(8,128)(2,1)S(1)}, u32[]{:S(2)}, u32[]{:S(2)}) %collective-permute-start.2) | collective-permute-done | bytes 49184 | tf_op jit(solution)/shard_map/ppermute | solution.py:465
  47.9 3.1 %collective-permute-start.5 = (bf16[192,256]{1,0:T(8,128)(2,1)S(1)}, bf16[192,256]{1,0:T(8,128)(2,1)S(1)}, u32[]{:S(2)}, u32[]{:S(2)}) collective-permute-start(bf16[192,256]{1,0:T(8,128)(2,1)S(1)} %chip_keys.1.refs_0_), channel_id=1, source_target_pairs={{0,96},{16,112},{32,64},{48,80},{64,32},{80,48},{96,0},{112,16},{1... | collective-permute-start | bytes 294920 | tf_op jit(solution)/shard_map/ppermute | solution.py:476
  51.0 0.6 collective-permute-start.4
  51.6 0.4 collective-permute-start.3
  52.1 0.9 %out_ready.1 = (bf16[48,768]{1,0:T(8,128)(2,1)S(1)}, f32[48,256]{1,0:T(8,128)S(1)}, f32[128,256]{1,0:T(8,128)S(1)}, bf16[128,256]{1,0:T(8,128)(2,1)S(1)}, bf16[48,128]{1,0:T(8,128)(2,1)S(1)}) custom-call(s32[5]{0:T(128)S(1)} %stack.19.place_ref, bf16[16,240,128]{2,1,0:T(8,128)(2,1)S(1)} %all-to-all-done.got_ref, ...), custom_call_target="tpu_custom_call" | custom-call | flops 2000000000 | bytes 2000000 | tf_op jit(solution)/shard_map/out_ready/pallas_call | solution.py:348
  53.0 7.9 %all-to-all-done.1.bias_ref = bf16[16,224,128]{2,1,0:T(8,128)(2,1)S(1)} async-done(((bf16[16,224,128]{2,1,0:T(8,128)(2,1)}), bf16[16,224,128]{2,1,0:T(8,128)(2,1)S(1)}, u32[]{:S(2)}, u32[]{:S(2)}) %all-to-all-start.1) | async-done | bytes 917536 | tf_op jit(solution)/shard_map/all_to_all | solution.py:360
  60.9 0.0 collective-permute-done.5.refs_3_
  60.9 0.0 collective-permute-done.4.refs_2_
  60.9 0.0 collective-permute-done.3.refs_1_
  60.9 2.0 %token_attention.1 = bf16[16,48,384]{2,1,0:T(8,128)(2,1)S(1)} custom-call(s32[5]{0:T(128)S(1)} %stack.19.place_ref, bf16[48,512]{1,0:T(8,128)(2,1)S(1)} %get-tuple-element.26.held_ref, bf16[48,128]{1,0:T(8,128)(2,1)S(1)} %get-tuple-element.28.mixed_ref, bf16[16,240,128]{2,1,0:T(8,128)(2,1)S(1)} %all-to-all-done.got_ref, ...), custom_call_target="tpu_custom_call" | custom-call | flops 3000000000 | bytes 2000000 | tf_op jit(solution)/shard_map/token_attention/pallas_call | solution.py:348
  62.9 14.8 %all_to_all.15.got_ref = bf16[16,48,384]{2,1,0:T(8,128)(2,1)S(1)} all-to-all(bf16[16,48,384]{2,1,0:T(8,128)(2,1)S(1)} %token_attention.1), channel_id=1, replica_groups=mesh['row'=8,'col'=16] {'col'}, dimensions={0} | all-to-all | bytes 1179648 | tf_op jit(solution)/shard_map/all_to_all | solution.py:360
  77.7 1.1 %token_out.1 = (bf16[48,256]{1,0:T(8,128)(2,1)}, bf16[128,128]{1,0:T(8,128)(2,1)}) custom-call(bf16[16,48,384]{2,1,0:T(8,128)(2,1)S(1)} %all_to_all.15.got_ref, bf16[48,768]{1,0:T(8,128)(2,1)S(1)} %get-tuple-element.31.out_w_ref, f32[48,256]{1,0:T(8,128)S(1)} %get-tuple-element.32.own_ref, f32[128,256]{1,0:T(8,128)S(1)} %get-tuple-element.33.back_ref, ...), custom_call_target="tpu_custom_call" | custom-call | flops 2000000000 | bytes 2000000 | tf_op jit(solution)/shard_map/token_out/pallas_call | solution.py:348
  (1 shorter events, 0.0 us)
Async XLA Ops:
  0.6 8.8 %collective-permute-start = (bf16[128,128]{1,0:T(8,128)(2,1)}, bf16[128,128]{1,0:T(8,128)(2,1)S(1)}, u32[]{:S(2)}, u32[]{:S(2)}) collective-permute-start(bf16[128,128]{1,0:T(8,128)(2,1)} %own_ref.1), channel_id=1, source_target_pairs={{0,1},{2,3},{4,5},{6,7},{8,9},{10,11},{12,13},{14,15},{16,17},{18,... | collective-permute-start | bytes 98312 | tf_op jit(solution)/shard_map/ppermute | solution.py:387
  2.7 6.7 %collective-permute-start.1 = (bf16[128,128]{1,0:T(8,128)(2,1)}, bf16[128,128]{1,0:T(8,128)(2,1)S(1)}, u32[]{:S(2)}, u32[]{:S(2)}) collective-permute-start(bf16[128,128]{1,0:T(8,128)(2,1)} %own_ref.1), channel_id=1, source_target_pairs={{1,2},{3,4},{5,6},{7,8},{9,10},{11,12},{13,14},{15,16},{17,18},{19... | collective-permute-start | bytes 98312 | tf_op jit(solution)/shard_map/ppermute | solution.py:387
  3.4 6.1 %copy-start = (bf16[4,16,32,128]{3,2,1,0:T(8,128)(2,1)S(1)}, bf16[4,16,32,128]{3,2,1,0:T(8,128)(2,1)}, u32[]{:S(2)}) copy-start(bf16[4,16,32,128]{3,2,1,0:T(8,128)(2,1)} %atom_pair_ref.1) | copy-start | bytes 1572868
  3.4 6.1 %copy-start.4 = (bf16[128,4,128]{2,1,0:T(4,128)(2,1)S(1)}, bf16[128,4,128]{2,1,0:T(4,128)(2,1)}, u32[]{:S(2)}) copy-start(bf16[128,4,128]{2,1,0:T(4,128)(2,1)} %param.20) | copy-start | bytes 393220
  3.4 6.1 %copy-start.5 = (bf16[48,768]{1,0:T(8,128)(2,1)S(1)}, bf16[48,768]{1,0:T(8,128)(2,1)}, u32[]{:S(2)}) copy-start(bf16[48,768]{1,0:T(8,128)(2,1)} %mine_ref.1) | copy-start | bytes 221188
  3.4 6.1 %copy-start.6 = (bf16[128,128]{1,0:T(8,128)(2,1)S(1)}, bf16[128,128]{1,0:T(8,128)(2,1)}, u32[]{:S(2)}) copy-start(bf16[128,128]{1,0:T(8,128)(2,1)} %own_ref.1) | copy-start | bytes 98308
  3.4 6.1 %copy-start.7 = (bf16[128,128]{1,0:T(8,128)(2,1)S(1)}, bf16[128,128]{1,0:T(8,128)(2,1)}, u32[]{:S(2)}) copy-start(bf16[128,128]{1,0:T(8,128)(2,1)} %wo_ref.1) | copy-start | bytes 98308
  3.4 6.1 %copy-start.8 = (bf16[48,128]{1,0:T(8,128)(2,1)S(1)}, bf16[48,128]{1,0:T(8,128)(2,1)}, u32[]{:S(2)}) copy-start(bf16[48,128]{1,0:T(8,128)(2,1)} %back_w_ref.1) | copy-start | bytes 36868
  3.4 6.1 %copy-start.9 = (bf16[16,4]{0,1:T(4,128)(2,1)S(1)}, bf16[16,4]{0,1:T(4,128)(2,1)}, u32[]{:S(2)}) copy-start(bf16[16,4]{0,1:T(4,128)(2,1)} %param.21) | copy-start | bytes 388
  3.4 6.1 %copy-start.10 = (s32[128]{0:T(128)S(1)}, s32[128]{0:T(128)}, u32[]{:S(2)}) copy-start(s32[128]{0:T(128)} %param.17) | copy-start | bytes 1540
  12.9 27.4 %all-to-all-start = ((bf16[16,240,128]{2,1,0:T(8,128)(2,1)}), bf16[16,240,128]{2,1,0:T(8,128)(2,1)S(1)}, u32[]{:S(2)}, u32[]{:S(2)}) async-start(bf16[16,240,128]{2,1,0:T(8,128)(2,1)} %get-tuple-element.25), calls=%async_computation | async-start | bytes 1966080 | tf_op jit(solution)/shard_map/all_to_all | solution.py:360
  21.9 22.2 %copy-start.1 = (bf16[256,768]{1,0:T(8,128)(2,1)S(1)}, bf16[256,768]{1,0:T(8,128)(2,1)}, u32[]{:S(2)}) copy-start(bf16[256,768]{1,0:T(8,128)(2,1)} %single_ref.1) | copy-start | bytes 1179652
  21.9 22.2 %copy-start.2 = (bf16[768,4,48]{0,2,1:T(8,128)(2,1)S(1)}, bf16[768,4,48]{0,2,1:T(8,128)(2,1)}, u32[]{:S(2)}) copy-start(bf16[768,4,48]{0,2,1:T(8,128)(2,1)} %param.27) | copy-start | bytes 884740
  21.9 22.2 %copy-start.3 = (bf16[128,768]{1,0:T(8,128)(2,1)S(1)}, bf16[128,768]{1,0:T(8,128)(2,1)}, u32[]{:S(2)}) copy-start(bf16[128,768]{1,0:T(8,128)(2,1)} %agg_ref.1) | copy-start | bytes 589828
  40.3 20.5 %all-to-all-start.1 = ((bf16[16,224,128]{2,1,0:T(8,128)(2,1)}), bf16[16,224,128]{2,1,0:T(8,128)(2,1)S(1)}, u32[]{:S(2)}, u32[]{:S(2)}) async-start(bf16[16,224,128]{2,1,0:T(8,128)(2,1)} %get-tuple-element.29), calls=%async_computation.1 | async-start | bytes 1835008 | tf_op jit(solution)/shard_map/all_to_all | solution.py:360
  46.6 1.3 %collective-permute-start.2 = (bf16[96,256]{1,0:T(8,128)(2,1)S(1)}, bf16[96,256]{1,0:T(8,128)(2,1)S(1)}, u32[]{:S(2)}, u32[]{:S(2)}) collective-permute-start(bf16[96,256]{1,0:T(8,128)(2,1)S(1)} %get-tuple-element.30.own_ref), channel_id=1, source_target_pairs={{0,16},{16,0},{32,48},{48,32},{64,80},{80,64},{96,112},{112,96},{1... | collective-permute-start | bytes 147464 | tf_op jit(solution)/shard_map/ppermute | solution.py:465
  47.9 13.0 %collective-permute-start.5 = (bf16[192,256]{1,0:T(8,128)(2,1)S(1)}, bf16[192,256]{1,0:T(8,128)(2,1)S(1)}, u32[]{:S(2)}, u32[]{:S(2)}) collective-permute-start(bf16[192,256]{1,0:T(8,128)(2,1)S(1)} %chip_keys.1.refs_0_), channel_id=1, source_target_pairs={{0,96},{16,112},{32,64},{48,80},{64,32},{80,48},{96,0},{112,16},{1... | collective-permute-start | bytes 294920 | tf_op jit(solution)/shard_map/ppermute | solution.py:476
  51.0 9.9 %collective-permute-start.4 = (bf16[192,256]{1,0:T(8,128)(2,1)S(1)}, bf16[192,256]{1,0:T(8,128)(2,1)S(1)}, u32[]{:S(2)}, u32[]{:S(2)}) collective-permute-start(bf16[192,256]{1,0:T(8,128)(2,1)S(1)} %chip_keys.1.refs_0_), channel_id=1, source_target_pairs={{0,64},{16,80},{32,96},{48,112},{64,0},{80,16},{96,32},{112,48},{1... | collective-permute-start | bytes 294920 | tf_op jit(solution)/shard_map/ppermute | solution.py:476
  51.6 9.3 %collective-permute-start.3 = (bf16[192,256]{1,0:T(8,128)(2,1)S(1)}, bf16[192,256]{1,0:T(8,128)(2,1)S(1)}, u32[]{:S(2)}, u32[]{:S(2)}) collective-permute-start(bf16[192,256]{1,0:T(8,128)(2,1)S(1)} %chip_keys.1.refs_0_), channel_id=1, source_target_pairs={{0,32},{16,48},{32,0},{48,16},{64,96},{80,112},{96,64},{112,80},{1... | collective-permute-start | bytes 294920 | tf_op jit(solution)/shard_map/ppermute | solution.py:476

commit v6 on v5

--- a/solution.py
+++ b/solution.py
@@ -129,9 +129,8 @@
         scores = dot_t(query, key) / math.sqrt(ATOM_HEAD) + jnp.concatenate(bias, axis=0)
         position = device * count - RIM + start + keys
         scores = jnp.where((position >= 0) & (position < last), scores, masked_score)
-        raised = jnp.exp(scores - jnp.max(scores, axis=-1, keepdims=True))
-        weights = (raised / jnp.sum(raised, axis=-1, keepdims=True)).astype(bf16)
-        mixed = dot(weights, value)
+        raised = jnp.exp(scores - jnp.max(scores, axis=-1, keepdims=True)).astype(bf16)
+        mixed = dot(raised, value) / dot(raised, jnp.ones_like(value))
         out = jnp.zeros((QW, CA), f32)
         for head in range(ATOM_HEADS):
             out = out + jnp.where(lanes == head, mixed[head * QW : (head + 1) * QW], 0.0)

time: 79.1 us -> 78.4 us (level)
  no operation moved by 1% of the time
where the time goes in v6:
time: 78.4 us; the launch traced here: 78.1 us
  Pallas kernels  29.9 us (38%)
  starting transfers between devices  19.8 us (25%)
  blocking collectives  14.8 us (19%)
  waiting for transfers between devices  12.5 us (16%)
  between operations  0.88 us (1%)
    pallas_call x2, Pallas kernels, pair_call(): pl.pallas_call(kernel, grid=(steps,), in_specs=[vmem] * len(before) + [pl...  20.8 us
    all_to_all x1, blocking collectives, gathered(): return lax.all_to_all(copies, axis, split_axis=0, concat_axis=0, tiled=True)  14.8 us
    all_to_all x2, starting transfers between devices, gathered(): return lax.all_to_all(copies, axis, split_axis=0, concat_axis=0, tiled=True)  12.7 us
    all_to_all x2, waiting for transfers between devices, gathered(): return lax.all_to_all(copies, axis, split_axis=0, concat_axis=0, tiled=True)  11.4 us
    pallas_call x5, Pallas kernels, single_step(): pl.pallas_call(kernel, in_specs=in_specs, out_specs=[pl.BlockSpec(memory_...  6.43 us
    ppermute x3, starting transfers between devices, body(): lax.ppermute(chip_kv, 'row', [(i, partner(i, hop, 0)) for i in range(row_...  4.17 us
    ppermute x2, starting transfers between devices, body(): lax.ppermute(atoms, both, pair + [(j, i) for i, j in pair])  2.73 us
    pallas_call x1, Pallas kernels, body(): pl.pallas_call(atom_kernel, in_specs=[vmem, smem] + [vmem] * 10, out_spec...  2.66 us
  transfers between devices with their start and end apart: 8, of which 3 were waited for; matrix products, arithmetic and copies ran while one was open for 0% of the time, Pallas kernels for 31%

profile of v6, /device:TPU:0, one launch (start us, length us, event | category | flops | bytes accessed | tf_op | source)
XLA Modules:
  0.0 78.1 jit_solution(17604500400103695558)
XLA Ops:
  0.6 2.1 %collective-permute-start = (bf16[128,128]{1,0:T(8,128)(2,1)}, bf16[128,128]{1,0:T(8,128)(2,1)S(1)}, u32[]{:S(2)}, u32[]{:S(2)}) collective-permute-start(bf16[128,128]{1,0:T(8,128)(2,1)} %own_ref.1), channel_id=1, source_target_pairs={{0,1},{2,3},{4,5},{6,7},{8,9},{10,11},{12,13},{14,15},{16,17},{18,... | collective-permute-start | bytes 98312 | tf_op jit(solution)/shard_map/ppermute | solution.py:386
  2.7 0.7 collective-permute-start.1
  3.4 0.0 copy-start
  3.4 0.0 copy-start.4
  3.4 0.0 copy-start.5
  3.4 0.0 copy-start.6
  3.4 0.0 copy-start.7
  3.4 0.0 copy-start.8
  3.4 0.0 copy-start.9
  3.4 0.0 copy-start.10
  3.5 5.9 %pair_bias.2 = (bf16[16,64,128]{2,1,0:T(8,128)(2,1)S(1)}, bf16[512,128]{1,0:T(8,128)(2,1)S(1)}, bf16[128,256]{1,0:T(8,128)(2,1)S(1)}) custom-call(bf16[256,128,128]{2,1,0:T(8,128)(2,1)} %refs_0_.3, bf16[512,128]{1,0:T(8,128)(2,1)} %bitcast.22, bf16[256,128]{1,0:T(8,128)(2,1)} %refs_2_.1, bf16[16,128]{1,0:T(8,128)(2,1)} %bitcast.23), custom_call_target="tpu_custom_call" | custom-call | flops 5079040000 | bytes 2359296 | tf_op jit(solution)/shard_map/pair_bias/pallas_call | solution.py:220
  9.3 0.1 stack.19.place_ref
  9.4 0.0 collective-permute-done.even_ref
  9.4 0.0 collective-permute-done.1.odd_ref
  9.4 0.0 copy-done
  9.4 0.0 copy-done.4
  9.5 0.0 copy-done.5
  9.5 0.0 copy-done.6
  9.5 0.0 copy-done.7
  9.5 0.0 copy-done.8
  9.5 0.0 copy-done.9
  9.5 0.0 copy-done.10
  9.5 2.7 %atom_stage.1 = (bf16[16,240,128]{2,1,0:T(8,128)(2,1)}, bf16[128,128]{1,0:T(8,128)(2,1)S(1)}, f32[8,128]{1,0:T(8,128)S(1)}) custom-call(bf16[16,64,128]{2,1,0:T(8,128)(2,1)S(1)} %get-tuple-element.20.first_ref.early_ref, s32[5]{0:T(128)S(1)} %stack.19.place_ref, bf16[128,128]{1,0:T(8,128)(2,1)S(1)} %collective-permute-done.even_ref, ...), custom_call_target="tpu_custom_call" | custom-call | flops 4000000000 | bytes 2000000 | tf_op jit(solution)/shard_map/atom_stage/pallas_call | solution.py:416
  12.2 9.0 %all-to-all-start = ((bf16[16,240,128]{2,1,0:T(8,128)(2,1)}), bf16[16,240,128]{2,1,0:T(8,128)(2,1)S(1)}, u32[]{:S(2)}, u32[]{:S(2)}) async-start(bf16[16,240,128]{2,1,0:T(8,128)(2,1)} %get-tuple-element.25), calls=%async_computation | async-start | bytes 1966080 | tf_op jit(solution)/shard_map/all_to_all | solution.py:359
  21.2 0.0 copy-start.1
  21.2 0.0 copy-start.2
  21.2 0.0 copy-start.3
  21.2 14.9 %pair_bias.3 = (bf16[16,224,128]{2,1,0:T(8,128)(2,1)}, f32[8,128]{1,0:T(8,128)S(1)}) custom-call(f32[8,128]{1,0:T(8,128)S(1)} %get-tuple-element.21._, bf16[16,64,128]{2,1,0:T(8,128)(2,1)S(1)} %get-tuple-element.20.first_ref.early_ref, bf16[256,128,128]{2,1,0:T(8,128)(2,1)} %refs_0_.3, bf16[512,128]{1,0:T(8,128)(2,1)S(1)} %get-tuple-element.22.refs_1_, ...), custom_call_target="tpu_custom_call" | custom-call | flops 17776640000 | bytes 8257536 | tf_op jit(solution)/shard_map/pair_bias/pallas_call | solution.py:220
  36.1 3.5 %all-to-all-done.got_ref = bf16[16,240,128]{2,1,0:T(8,128)(2,1)S(1)} async-done(((bf16[16,240,128]{2,1,0:T(8,128)(2,1)}), bf16[16,240,128]{2,1,0:T(8,128)(2,1)S(1)}, u32[]{:S(2)}, u32[]{:S(2)}) %all-to-all-start) | async-done | bytes 983072 | tf_op jit(solution)/shard_map/all_to_all | solution.py:359
  39.6 3.7 %all-to-all-start.1 = ((bf16[16,224,128]{2,1,0:T(8,128)(2,1)}), bf16[16,224,128]{2,1,0:T(8,128)(2,1)S(1)}, u32[]{:S(2)}, u32[]{:S(2)}) async-start(bf16[16,224,128]{2,1,0:T(8,128)(2,1)} %get-tuple-element.29), calls=%async_computation.1 | async-start | bytes 1835008 | tf_op jit(solution)/shard_map/all_to_all | solution.py:359
  43.4 0.0 copy-done.1
  43.4 0.0 copy-done.2
  43.4 0.0 copy-done.3
  43.4 2.4 %token_stage.1 = (bf16[256,768]{1,0:T(8,128)(2,1)S(1)}, bf16[48,512]{1,0:T(8,128)(2,1)S(1)}, bf16[96,256]{1,0:T(8,128)(2,1)S(1)}) custom-call(f32[8,128]{1,0:T(8,128)S(1)} %get-tuple-element.24._, bf16[16,240,128]{2,1,0:T(8,128)(2,1)S(1)} %all-to-all-done.got_ref, bf16[256,768]{1,0:T(8,128)(2,1)S(1)} %copy-done.1, bf16[128,768]{1,0:T(8,128)(2,1)S(1)} %copy-done.3, ...), custom_call_target="tpu_custom_call" | custom-call | flops 4000000000 | bytes 2000000 | tf_op jit(solution)/shard_map/token_stage/pallas_call | solution.py:347
  45.9 0.2 collective-permute-start.2
  46.1 1.1 %collective-permute-done.2.other_ref = bf16[96,256]{1,0:T(8,128)(2,1)S(1)} collective-permute-done((bf16[96,256]{1,0:T(8,128)(2,1)S(1)}, bf16[96,256]{1,0:T(8,128)(2,1)S(1)}, u32[]{:S(2)}, u32[]{:S(2)}) %collective-permute-start.2) | collective-permute-done | bytes 49184 | tf_op jit(solution)/shard_map/ppermute | solution.py:464
  47.2 3.1 %collective-permute-start.5 = (bf16[192,256]{1,0:T(8,128)(2,1)S(1)}, bf16[192,256]{1,0:T(8,128)(2,1)S(1)}, u32[]{:S(2)}, u32[]{:S(2)}) collective-permute-start(bf16[192,256]{1,0:T(8,128)(2,1)S(1)} %chip_keys.1.refs_0_), channel_id=1, source_target_pairs={{0,96},{16,112},{32,64},{48,80},{64,32},{80,48},{96,0},{112,16},{1... | collective-permute-start | bytes 294920 | tf_op jit(solution)/shard_map/ppermute | solution.py:475
  50.3 0.6 collective-permute-start.4
  50.9 0.4 collective-permute-start.3
  51.4 0.9 %out_ready.1 = (bf16[48,768]{1,0:T(8,128)(2,1)S(1)}, f32[48,256]{1,0:T(8,128)S(1)}, f32[128,256]{1,0:T(8,128)S(1)}, bf16[128,256]{1,0:T(8,128)(2,1)S(1)}, bf16[48,128]{1,0:T(8,128)(2,1)S(1)}) custom-call(s32[5]{0:T(128)S(1)} %stack.19.place_ref, bf16[16,240,128]{2,1,0:T(8,128)(2,1)S(1)} %all-to-all-done.got_ref, ...), custom_call_target="tpu_custom_call" | custom-call | flops 2000000000 | bytes 2000000 | tf_op jit(solution)/shard_map/out_ready/pallas_call | solution.py:347
  52.3 7.9 %all-to-all-done.1.bias_ref = bf16[16,224,128]{2,1,0:T(8,128)(2,1)S(1)} async-done(((bf16[16,224,128]{2,1,0:T(8,128)(2,1)}), bf16[16,224,128]{2,1,0:T(8,128)(2,1)S(1)}, u32[]{:S(2)}, u32[]{:S(2)}) %all-to-all-start.1) | async-done | bytes 917536 | tf_op jit(solution)/shard_map/all_to_all | solution.py:359
  60.2 0.0 collective-permute-done.5.refs_3_
  60.2 0.0 collective-permute-done.4.refs_2_
  60.2 0.0 collective-permute-done.3.refs_1_
  60.2 2.0 %token_attention.1 = bf16[16,48,384]{2,1,0:T(8,128)(2,1)S(1)} custom-call(s32[5]{0:T(128)S(1)} %stack.19.place_ref, bf16[48,512]{1,0:T(8,128)(2,1)S(1)} %get-tuple-element.26.held_ref, bf16[48,128]{1,0:T(8,128)(2,1)S(1)} %get-tuple-element.28.mixed_ref, bf16[16,240,128]{2,1,0:T(8,128)(2,1)S(1)} %all-to-all-done.got_ref, ...), custom_call_target="tpu_custom_call" | custom-call | flops 3000000000 | bytes 2000000 | tf_op jit(solution)/shard_map/token_attention/pallas_call | solution.py:347
  62.2 14.8 %all_to_all.15.got_ref = bf16[16,48,384]{2,1,0:T(8,128)(2,1)S(1)} all-to-all(bf16[16,48,384]{2,1,0:T(8,128)(2,1)S(1)} %token_attention.1), channel_id=1, replica_groups=mesh['row'=8,'col'=16] {'col'}, dimensions={0} | all-to-all | bytes 1179648 | tf_op jit(solution)/shard_map/all_to_all | solution.py:359
  77.0 1.1 %token_out.1 = (bf16[48,256]{1,0:T(8,128)(2,1)}, bf16[128,128]{1,0:T(8,128)(2,1)}) custom-call(bf16[16,48,384]{2,1,0:T(8,128)(2,1)S(1)} %all_to_all.15.got_ref, bf16[48,768]{1,0:T(8,128)(2,1)S(1)} %get-tuple-element.31.out_w_ref, f32[48,256]{1,0:T(8,128)S(1)} %get-tuple-element.32.own_ref, f32[128,256]{1,0:T(8,128)S(1)} %get-tuple-element.33.back_ref, ...), custom_call_target="tpu_custom_call" | custom-call | flops 2000000000 | bytes 2000000 | tf_op jit(solution)/shard_map/token_out/pallas_call | solution.py:347
  (1 shorter events, 0.0 us)
Async XLA Ops:
  0.6 8.8 %collective-permute-start = (bf16[128,128]{1,0:T(8,128)(2,1)}, bf16[128,128]{1,0:T(8,128)(2,1)S(1)}, u32[]{:S(2)}, u32[]{:S(2)}) collective-permute-start(bf16[128,128]{1,0:T(8,128)(2,1)} %own_ref.1), channel_id=1, source_target_pairs={{0,1},{2,3},{4,5},{6,7},{8,9},{10,11},{12,13},{14,15},{16,17},{18,... | collective-permute-start | bytes 98312 | tf_op jit(solution)/shard_map/ppermute | solution.py:386
  2.7 6.7 %collective-permute-start.1 = (bf16[128,128]{1,0:T(8,128)(2,1)}, bf16[128,128]{1,0:T(8,128)(2,1)S(1)}, u32[]{:S(2)}, u32[]{:S(2)}) collective-permute-start(bf16[128,128]{1,0:T(8,128)(2,1)} %own_ref.1), channel_id=1, source_target_pairs={{1,2},{3,4},{5,6},{7,8},{9,10},{11,12},{13,14},{15,16},{17,18},{19... | collective-permute-start | bytes 98312 | tf_op jit(solution)/shard_map/ppermute | solution.py:386
  3.4 6.1 %copy-start = (bf16[4,16,32,128]{3,2,1,0:T(8,128)(2,1)S(1)}, bf16[4,16,32,128]{3,2,1,0:T(8,128)(2,1)}, u32[]{:S(2)}) copy-start(bf16[4,16,32,128]{3,2,1,0:T(8,128)(2,1)} %atom_pair_ref.1) | copy-start | bytes 1572868
  3.4 6.1 %copy-start.4 = (bf16[128,4,128]{2,1,0:T(4,128)(2,1)S(1)}, bf16[128,4,128]{2,1,0:T(4,128)(2,1)}, u32[]{:S(2)}) copy-start(bf16[128,4,128]{2,1,0:T(4,128)(2,1)} %param.20) | copy-start | bytes 393220
  3.4 6.1 %copy-start.5 = (bf16[48,768]{1,0:T(8,128)(2,1)S(1)}, bf16[48,768]{1,0:T(8,128)(2,1)}, u32[]{:S(2)}) copy-start(bf16[48,768]{1,0:T(8,128)(2,1)} %mine_ref.1) | copy-start | bytes 221188
  3.4 6.1 %copy-start.6 = (bf16[128,128]{1,0:T(8,128)(2,1)S(1)}, bf16[128,128]{1,0:T(8,128)(2,1)}, u32[]{:S(2)}) copy-start(bf16[128,128]{1,0:T(8,128)(2,1)} %own_ref.1) | copy-start | bytes 98308
  3.4 6.1 %copy-start.7 = (bf16[128,128]{1,0:T(8,128)(2,1)S(1)}, bf16[128,128]{1,0:T(8,128)(2,1)}, u32[]{:S(2)}) copy-start(bf16[128,128]{1,0:T(8,128)(2,1)} %wo_ref.1) | copy-start | bytes 98308
  3.4 6.1 %copy-start.8 = (bf16[48,128]{1,0:T(8,128)(2,1)S(1)}, bf16[48,128]{1,0:T(8,128)(2,1)}, u32[]{:S(2)}) copy-start(bf16[48,128]{1,0:T(8,128)(2,1)} %back_w_ref.1) | copy-start | bytes 36868
  3.4 6.1 %copy-start.9 = (bf16[16,4]{0,1:T(4,128)(2,1)S(1)}, bf16[16,4]{0,1:T(4,128)(2,1)}, u32[]{:S(2)}) copy-start(bf16[16,4]{0,1:T(4,128)(2,1)} %param.21) | copy-start | bytes 388
  3.4 6.1 %copy-start.10 = (s32[128]{0:T(128)S(1)}, s32[128]{0:T(128)}, u32[]{:S(2)}) copy-start(s32[128]{0:T(128)} %param.17) | copy-start | bytes 1540
  12.2 27.5 %all-to-all-start = ((bf16[16,240,128]{2,1,0:T(8,128)(2,1)}), bf16[16,240,128]{2,1,0:T(8,128)(2,1)S(1)}, u32[]{:S(2)}, u32[]{:S(2)}) async-start(bf16[16,240,128]{2,1,0:T(8,128)(2,1)} %get-tuple-element.25), calls=%async_computation | async-start | bytes 1966080 | tf_op jit(solution)/shard_map/all_to_all | solution.py:359
  21.2 22.2 %copy-start.1 = (bf16[256,768]{1,0:T(8,128)(2,1)S(1)}, bf16[256,768]{1,0:T(8,128)(2,1)}, u32[]{:S(2)}) copy-start(bf16[256,768]{1,0:T(8,128)(2,1)} %single_ref.1) | copy-start | bytes 1179652
  21.2 22.2 %copy-start.2 = (bf16[768,4,48]{0,2,1:T(8,128)(2,1)S(1)}, bf16[768,4,48]{0,2,1:T(8,128)(2,1)}, u32[]{:S(2)}) copy-start(bf16[768,4,48]{0,2,1:T(8,128)(2,1)} %param.27) | copy-start | bytes 884740
  21.2 22.2 %copy-start.3 = (bf16[128,768]{1,0:T(8,128)(2,1)S(1)}, bf16[128,768]{1,0:T(8,128)(2,1)}, u32[]{:S(2)}) copy-start(bf16[128,768]{1,0:T(8,128)(2,1)} %agg_ref.1) | copy-start | bytes 589828
  39.6 20.5 %all-to-all-start.1 = ((bf16[16,224,128]{2,1,0:T(8,128)(2,1)}), bf16[16,224,128]{2,1,0:T(8,128)(2,1)S(1)}, u32[]{:S(2)}, u32[]{:S(2)}) async-start(bf16[16,224,128]{2,1,0:T(8,128)(2,1)} %get-tuple-element.29), calls=%async_computation.1 | async-start | bytes 1835008 | tf_op jit(solution)/shard_map/all_to_all | solution.py:359
  45.9 1.3 %collective-permute-start.2 = (bf16[96,256]{1,0:T(8,128)(2,1)S(1)}, bf16[96,256]{1,0:T(8,128)(2,1)S(1)}, u32[]{:S(2)}, u32[]{:S(2)}) collective-permute-start(bf16[96,256]{1,0:T(8,128)(2,1)S(1)} %get-tuple-element.30.own_ref), channel_id=1, source_target_pairs={{0,16},{16,0},{32,48},{48,32},{64,80},{80,64},{96,112},{112,96},{1... | collective-permute-start | bytes 147464 | tf_op jit(solution)/shard_map/ppermute | solution.py:464
  47.2 13.0 %collective-permute-start.5 = (bf16[192,256]{1,0:T(8,128)(2,1)S(1)}, bf16[192,256]{1,0:T(8,128)(2,1)S(1)}, u32[]{:S(2)}, u32[]{:S(2)}) collective-permute-start(bf16[192,256]{1,0:T(8,128)(2,1)S(1)} %chip_keys.1.refs_0_), channel_id=1, source_target_pairs={{0,96},{16,112},{32,64},{48,80},{64,32},{80,48},{96,0},{112,16},{1... | collective-permute-start | bytes 294920 | tf_op jit(solution)/shard_map/ppermute | solution.py:475
  50.3 9.9 %collective-permute-start.4 = (bf16[192,256]{1,0:T(8,128)(2,1)S(1)}, bf16[192,256]{1,0:T(8,128)(2,1)S(1)}, u32[]{:S(2)}, u32[]{:S(2)}) collective-permute-start(bf16[192,256]{1,0:T(8,128)(2,1)S(1)} %chip_keys.1.refs_0_), channel_id=1, source_target_pairs={{0,64},{16,80},{32,96},{48,112},{64,0},{80,16},{96,32},{112,48},{1... | collective-permute-start | bytes 294920 | tf_op jit(solution)/shard_map/ppermute | solution.py:475
  50.9 9.3 %collective-permute-start.3 = (bf16[192,256]{1,0:T(8,128)(2,1)S(1)}, bf16[192,256]{1,0:T(8,128)(2,1)S(1)}, u32[]{:S(2)}, u32[]{:S(2)}) collective-permute-start(bf16[192,256]{1,0:T(8,128)(2,1)S(1)} %chip_keys.1.refs_0_), channel_id=1, source_target_pairs={{0,32},{16,48},{32,0},{48,16},{64,96},{80,112},{96,64},{112,80},{1... | collective-permute-start | bytes 294920 | tf_op jit(solution)/shard_map/ppermute | solution.py:475

commit v7 on v6

--- a/solution.py
+++ b/solution.py
@@ -333,8 +333,10 @@
     tokens = own_ref.shape[1]
     gated = got_ref[:, :, :tokens].reshape(heads * head, tokens)
     mixed = got_ref[:, :, tokens:].reshape(heads * head, CA)
-    single_ref[...] = (own_ref[...] + dot(out_w_ref[...], gated)).astype(bf16)
-    back = (back_ref[...] + dot(mixed.astype(f32).T.astype(bf16), gated)).astype(bf16)
+    mine = own_ref.shape[0]
+    product = dot(jnp.concatenate([out_w_ref[...], mixed.astype(f32).T.astype(bf16)], axis=0), gated)
+    single_ref[...] = (own_ref[...] + product[:mine]).astype(bf16)
+    back = (back_ref[...] + product[mine:]).astype(bf16)
     picked = dot_t(onehot_ref[...], back)
     atoms_ref[...] = (mid_ref[...].astype(f32) + picked).astype(bf16)
 

time: 78.4 us -> 78.4 us (level)
  no operation moved by 1% of the time
where the time goes in v7:
time: 78.4 us; the launch traced here: 78 us
  Pallas kernels  29.9 us (38%)
  starting transfers between devices  19.8 us (25%)
  blocking collectives  14.8 us (19%)
  waiting for transfers between devices  12.5 us (16%)
  between operations  0.88 us (1%)
    pallas_call x2, Pallas kernels, pair_call(): pl.pallas_call(kernel, grid=(steps,), in_specs=[vmem] * len(before) + [pl...  20.8 us
    all_to_all x1, blocking collectives, gathered(): return lax.all_to_all(copies, axis, split_axis=0, concat_axis=0, tiled=True)  14.8 us
    all_to_all x2, starting transfers between devices, gathered(): return lax.all_to_all(copies, axis, split_axis=0, concat_axis=0, tiled=True)  12.7 us
    all_to_all x2, waiting for transfers between devices, gathered(): return lax.all_to_all(copies, axis, split_axis=0, concat_axis=0, tiled=True)  11.4 us
    pallas_call x5, Pallas kernels, single_step(): pl.pallas_call(kernel, in_specs=in_specs, out_specs=[pl.BlockSpec(memory_...  6.4 us
    ppermute x3, starting transfers between devices, body(): lax.ppermute(chip_kv, 'row', [(i, partner(i, hop, 0)) for i in range(row_...  4.17 us
    ppermute x2, starting transfers between devices, body(): lax.ppermute(atoms, both, pair + [(j, i) for i, j in pair])  2.73 us
    pallas_call x1, Pallas kernels, body(): pl.pallas_call(atom_kernel, in_specs=[vmem, smem] + [vmem] * 10, out_spec...  2.66 us
  transfers between devices with their start and end apart: 8, of which 3 were waited for; matrix products, arithmetic and copies ran while one was open for 0% of the time, Pallas kernels for 31%

profile of v7, /device:TPU:0, one launch (start us, length us, event | category | flops | bytes accessed | tf_op | source)
XLA Modules:
  0.0 78.0 jit_solution(8290828881119137962)
XLA Ops:
  0.6 2.1 %collective-permute-start = (bf16[128,128]{1,0:T(8,128)(2,1)}, bf16[128,128]{1,0:T(8,128)(2,1)S(1)}, u32[]{:S(2)}, u32[]{:S(2)}) collective-permute-start(bf16[128,128]{1,0:T(8,128)(2,1)} %own_ref.1), channel_id=1, source_target_pairs={{0,1},{2,3},{4,5},{6,7},{8,9},{10,11},{12,13},{14,15},{16,17},{18,... | collective-permute-start | bytes 98312 | tf_op jit(solution)/shard_map/ppermute | solution.py:388
  2.7 0.7 collective-permute-start.1
  3.4 0.0 copy-start
  3.4 0.0 copy-start.4
  3.4 0.0 copy-start.5
  3.4 0.0 copy-start.6
  3.4 0.0 copy-start.7
  3.4 0.0 copy-start.8
  3.4 0.0 copy-start.9
  3.4 0.0 copy-start.10
  3.5 5.9 %pair_bias.2 = (bf16[16,64,128]{2,1,0:T(8,128)(2,1)S(1)}, bf16[512,128]{1,0:T(8,128)(2,1)S(1)}, bf16[128,256]{1,0:T(8,128)(2,1)S(1)}) custom-call(bf16[256,128,128]{2,1,0:T(8,128)(2,1)} %refs_0_.3, bf16[512,128]{1,0:T(8,128)(2,1)} %bitcast.22, bf16[256,128]{1,0:T(8,128)(2,1)} %refs_2_.1, bf16[16,128]{1,0:T(8,128)(2,1)} %bitcast.23), custom_call_target="tpu_custom_call" | custom-call | flops 5079040000 | bytes 2359296 | tf_op jit(solution)/shard_map/pair_bias/pallas_call | solution.py:220
  9.3 0.1 stack.19.place_ref
  9.4 0.0 collective-permute-done.even_ref
  9.4 0.0 collective-permute-done.1.odd_ref
  9.4 0.0 copy-done
  9.4 0.0 copy-done.4
  9.5 0.0 copy-done.5
  9.5 0.0 copy-done.6
  9.5 0.0 copy-done.7
  9.5 0.0 copy-done.8
  9.5 0.0 copy-done.9
  9.5 0.0 copy-done.10
  9.5 2.7 %atom_stage.1 = (bf16[16,240,128]{2,1,0:T(8,128)(2,1)}, bf16[128,128]{1,0:T(8,128)(2,1)S(1)}, f32[8,128]{1,0:T(8,128)S(1)}) custom-call(bf16[16,64,128]{2,1,0:T(8,128)(2,1)S(1)} %get-tuple-element.20.first_ref.early_ref, s32[5]{0:T(128)S(1)} %stack.19.place_ref, bf16[128,128]{1,0:T(8,128)(2,1)S(1)} %collective-permute-done.even_ref, ...), custom_call_target="tpu_custom_call" | custom-call | flops 4000000000 | bytes 2000000 | tf_op jit(solution)/shard_map/atom_stage/pallas_call | solution.py:418
  12.2 9.0 %all-to-all-start = ((bf16[16,240,128]{2,1,0:T(8,128)(2,1)}), bf16[16,240,128]{2,1,0:T(8,128)(2,1)S(1)}, u32[]{:S(2)}, u32[]{:S(2)}) async-start(bf16[16,240,128]{2,1,0:T(8,128)(2,1)} %get-tuple-element.25), calls=%async_computation | async-start | bytes 1966080 | tf_op jit(solution)/shard_map/all_to_all | solution.py:361
  21.2 0.0 copy-start.1
  21.2 0.0 copy-start.2
  21.2 0.0 copy-start.3
  21.2 14.9 %pair_bias.3 = (bf16[16,224,128]{2,1,0:T(8,128)(2,1)}, f32[8,128]{1,0:T(8,128)S(1)}) custom-call(f32[8,128]{1,0:T(8,128)S(1)} %get-tuple-element.21._, bf16[16,64,128]{2,1,0:T(8,128)(2,1)S(1)} %get-tuple-element.20.first_ref.early_ref, bf16[256,128,128]{2,1,0:T(8,128)(2,1)} %refs_0_.3, bf16[512,128]{1,0:T(8,128)(2,1)S(1)} %get-tuple-element.22.refs_1_, ...), custom_call_target="tpu_custom_call" | custom-call | flops 17776640000 | bytes 8257536 | tf_op jit(solution)/shard_map/pair_bias/pallas_call | solution.py:220
  36.1 3.5 %all-to-all-done.got_ref = bf16[16,240,128]{2,1,0:T(8,128)(2,1)S(1)} async-done(((bf16[16,240,128]{2,1,0:T(8,128)(2,1)}), bf16[16,240,128]{2,1,0:T(8,128)(2,1)S(1)}, u32[]{:S(2)}, u32[]{:S(2)}) %all-to-all-start) | async-done | bytes 983072 | tf_op jit(solution)/shard_map/all_to_all | solution.py:361
  39.6 3.7 %all-to-all-start.1 = ((bf16[16,224,128]{2,1,0:T(8,128)(2,1)}), bf16[16,224,128]{2,1,0:T(8,128)(2,1)S(1)}, u32[]{:S(2)}, u32[]{:S(2)}) async-start(bf16[16,224,128]{2,1,0:T(8,128)(2,1)} %get-tuple-element.29), calls=%async_computation.1 | async-start | bytes 1835008 | tf_op jit(solution)/shard_map/all_to_all | solution.py:361
  43.4 0.0 copy-done.1
  43.4 0.0 copy-done.2
  43.4 0.0 copy-done.3
  43.4 2.4 %token_stage.1 = (bf16[256,768]{1,0:T(8,128)(2,1)S(1)}, bf16[48,512]{1,0:T(8,128)(2,1)S(1)}, bf16[96,256]{1,0:T(8,128)(2,1)S(1)}) custom-call(f32[8,128]{1,0:T(8,128)S(1)} %get-tuple-element.24._, bf16[16,240,128]{2,1,0:T(8,128)(2,1)S(1)} %all-to-all-done.got_ref, bf16[256,768]{1,0:T(8,128)(2,1)S(1)} %copy-done.1, bf16[128,768]{1,0:T(8,128)(2,1)S(1)} %copy-done.3, ...), custom_call_target="tpu_custom_call" | custom-call | flops 4000000000 | bytes 2000000 | tf_op jit(solution)/shard_map/token_stage/pallas_call | solution.py:349
  45.9 0.2 collective-permute-start.2
  46.1 1.1 %collective-permute-done.2.other_ref = bf16[96,256]{1,0:T(8,128)(2,1)S(1)} collective-permute-done((bf16[96,256]{1,0:T(8,128)(2,1)S(1)}, bf16[96,256]{1,0:T(8,128)(2,1)S(1)}, u32[]{:S(2)}, u32[]{:S(2)}) %collective-permute-start.2) | collective-permute-done | bytes 49184 | tf_op jit(solution)/shard_map/ppermute | solution.py:466
  47.2 3.1 %collective-permute-start.5 = (bf16[192,256]{1,0:T(8,128)(2,1)S(1)}, bf16[192,256]{1,0:T(8,128)(2,1)S(1)}, u32[]{:S(2)}, u32[]{:S(2)}) collective-permute-start(bf16[192,256]{1,0:T(8,128)(2,1)S(1)} %chip_keys.1.refs_0_), channel_id=1, source_target_pairs={{0,96},{16,112},{32,64},{48,80},{64,32},{80,48},{96,0},{112,16},{1... | collective-permute-start | bytes 294920 | tf_op jit(solution)/shard_map/ppermute | solution.py:477
  50.3 0.6 collective-permute-start.4
  50.9 0.4 collective-permute-start.3
  51.4 0.9 %out_ready.1 = (bf16[48,768]{1,0:T(8,128)(2,1)S(1)}, f32[48,256]{1,0:T(8,128)S(1)}, f32[128,256]{1,0:T(8,128)S(1)}, bf16[128,256]{1,0:T(8,128)(2,1)S(1)}, bf16[48,128]{1,0:T(8,128)(2,1)S(1)}) custom-call(s32[5]{0:T(128)S(1)} %stack.19.place_ref, bf16[16,240,128]{2,1,0:T(8,128)(2,1)S(1)} %all-to-all-done.got_ref, ...), custom_call_target="tpu_custom_call" | custom-call | flops 2000000000 | bytes 2000000 | tf_op jit(solution)/shard_map/out_ready/pallas_call | solution.py:349
  52.3 7.9 %all-to-all-done.1.bias_ref = bf16[16,224,128]{2,1,0:T(8,128)(2,1)S(1)} async-done(((bf16[16,224,128]{2,1,0:T(8,128)(2,1)}), bf16[16,224,128]{2,1,0:T(8,128)(2,1)S(1)}, u32[]{:S(2)}, u32[]{:S(2)}) %all-to-all-start.1) | async-done | bytes 917536 | tf_op jit(solution)/shard_map/all_to_all | solution.py:361
  60.2 0.0 collective-permute-done.5.refs_3_
  60.2 0.0 collective-permute-done.4.refs_2_
  60.2 0.0 collective-permute-done.3.refs_1_
  60.2 2.0 %token_attention.1 = bf16[16,48,384]{2,1,0:T(8,128)(2,1)S(1)} custom-call(s32[5]{0:T(128)S(1)} %stack.19.place_ref, bf16[48,512]{1,0:T(8,128)(2,1)S(1)} %get-tuple-element.26.held_ref, bf16[48,128]{1,0:T(8,128)(2,1)S(1)} %get-tuple-element.28.mixed_ref, bf16[16,240,128]{2,1,0:T(8,128)(2,1)S(1)} %all-to-all-done.got_ref, ...), custom_call_target="tpu_custom_call" | custom-call | flops 3000000000 | bytes 2000000 | tf_op jit(solution)/shard_map/token_attention/pallas_call | solution.py:349
  62.2 14.8 %all_to_all.15.got_ref = bf16[16,48,384]{2,1,0:T(8,128)(2,1)S(1)} all-to-all(bf16[16,48,384]{2,1,0:T(8,128)(2,1)S(1)} %token_attention.1), channel_id=1, replica_groups=mesh['row'=8,'col'=16] {'col'}, dimensions={0} | all-to-all | bytes 1179648 | tf_op jit(solution)/shard_map/all_to_all | solution.py:361
  77.0 1.0 %token_out.1 = (bf16[48,256]{1,0:T(8,128)(2,1)}, bf16[128,128]{1,0:T(8,128)(2,1)}) custom-call(bf16[16,48,384]{2,1,0:T(8,128)(2,1)S(1)} %all_to_all.15.got_ref, bf16[48,768]{1,0:T(8,128)(2,1)S(1)} %get-tuple-element.31.out_w_ref, f32[48,256]{1,0:T(8,128)S(1)} %get-tuple-element.32.own_ref, f32[128,256]{1,0:T(8,128)S(1)} %get-tuple-element.33.back_ref, ...), custom_call_target="tpu_custom_call" | custom-call | flops 2000000000 | bytes 2000000 | tf_op jit(solution)/shard_map/token_out/pallas_call | solution.py:349
  (1 shorter events, 0.0 us)
Async XLA Ops:
  0.6 8.8 %collective-permute-start = (bf16[128,128]{1,0:T(8,128)(2,1)}, bf16[128,128]{1,0:T(8,128)(2,1)S(1)}, u32[]{:S(2)}, u32[]{:S(2)}) collective-permute-start(bf16[128,128]{1,0:T(8,128)(2,1)} %own_ref.1), channel_id=1, source_target_pairs={{0,1},{2,3},{4,5},{6,7},{8,9},{10,11},{12,13},{14,15},{16,17},{18,... | collective-permute-start | bytes 98312 | tf_op jit(solution)/shard_map/ppermute | solution.py:388
  2.7 6.7 %collective-permute-start.1 = (bf16[128,128]{1,0:T(8,128)(2,1)}, bf16[128,128]{1,0:T(8,128)(2,1)S(1)}, u32[]{:S(2)}, u32[]{:S(2)}) collective-permute-start(bf16[128,128]{1,0:T(8,128)(2,1)} %own_ref.1), channel_id=1, source_target_pairs={{1,2},{3,4},{5,6},{7,8},{9,10},{11,12},{13,14},{15,16},{17,18},{19... | collective-permute-start | bytes 98312 | tf_op jit(solution)/shard_map/ppermute | solution.py:388
  3.4 6.1 %copy-start = (bf16[4,16,32,128]{3,2,1,0:T(8,128)(2,1)S(1)}, bf16[4,16,32,128]{3,2,1,0:T(8,128)(2,1)}, u32[]{:S(2)}) copy-start(bf16[4,16,32,128]{3,2,1,0:T(8,128)(2,1)} %atom_pair_ref.1) | copy-start | bytes 1572868
  3.4 6.1 %copy-start.4 = (bf16[128,4,128]{2,1,0:T(4,128)(2,1)S(1)}, bf16[128,4,128]{2,1,0:T(4,128)(2,1)}, u32[]{:S(2)}) copy-start(bf16[128,4,128]{2,1,0:T(4,128)(2,1)} %param.20) | copy-start | bytes 393220
  3.4 6.1 %copy-start.5 = (bf16[48,768]{1,0:T(8,128)(2,1)S(1)}, bf16[48,768]{1,0:T(8,128)(2,1)}, u32[]{:S(2)}) copy-start(bf16[48,768]{1,0:T(8,128)(2,1)} %mine_ref.1) | copy-start | bytes 221188
  3.4 6.1 %copy-start.6 = (bf16[128,128]{1,0:T(8,128)(2,1)S(1)}, bf16[128,128]{1,0:T(8,128)(2,1)}, u32[]{:S(2)}) copy-start(bf16[128,128]{1,0:T(8,128)(2,1)} %own_ref.1) | copy-start | bytes 98308
  3.4 6.1 %copy-start.7 = (bf16[128,128]{1,0:T(8,128)(2,1)S(1)}, bf16[128,128]{1,0:T(8,128)(2,1)}, u32[]{:S(2)}) copy-start(bf16[128,128]{1,0:T(8,128)(2,1)} %wo_ref.1) | copy-start | bytes 98308
  3.4 6.1 %copy-start.8 = (bf16[48,128]{1,0:T(8,128)(2,1)S(1)}, bf16[48,128]{1,0:T(8,128)(2,1)}, u32[]{:S(2)}) copy-start(bf16[48,128]{1,0:T(8,128)(2,1)} %back_w_ref.1) | copy-start | bytes 36868
  3.4 6.1 %copy-start.9 = (bf16[16,4]{0,1:T(4,128)(2,1)S(1)}, bf16[16,4]{0,1:T(4,128)(2,1)}, u32[]{:S(2)}) copy-start(bf16[16,4]{0,1:T(4,128)(2,1)} %param.21) | copy-start | bytes 388
  3.4 6.1 %copy-start.10 = (s32[128]{0:T(128)S(1)}, s32[128]{0:T(128)}, u32[]{:S(2)}) copy-start(s32[128]{0:T(128)} %param.17) | copy-start | bytes 1540
  12.2 27.5 %all-to-all-start = ((bf16[16,240,128]{2,1,0:T(8,128)(2,1)}), bf16[16,240,128]{2,1,0:T(8,128)(2,1)S(1)}, u32[]{:S(2)}, u32[]{:S(2)}) async-start(bf16[16,240,128]{2,1,0:T(8,128)(2,1)} %get-tuple-element.25), calls=%async_computation | async-start | bytes 1966080 | tf_op jit(solution)/shard_map/all_to_all | solution.py:361
  21.2 22.2 %copy-start.1 = (bf16[256,768]{1,0:T(8,128)(2,1)S(1)}, bf16[256,768]{1,0:T(8,128)(2,1)}, u32[]{:S(2)}) copy-start(bf16[256,768]{1,0:T(8,128)(2,1)} %single_ref.1) | copy-start | bytes 1179652
  21.2 22.2 %copy-start.2 = (bf16[768,4,48]{0,2,1:T(8,128)(2,1)S(1)}, bf16[768,4,48]{0,2,1:T(8,128)(2,1)}, u32[]{:S(2)}) copy-start(bf16[768,4,48]{0,2,1:T(8,128)(2,1)} %param.27) | copy-start | bytes 884740
  21.2 22.2 %copy-start.3 = (bf16[128,768]{1,0:T(8,128)(2,1)S(1)}, bf16[128,768]{1,0:T(8,128)(2,1)}, u32[]{:S(2)}) copy-start(bf16[128,768]{1,0:T(8,128)(2,1)} %agg_ref.1) | copy-start | bytes 589828
  39.6 20.5 %all-to-all-start.1 = ((bf16[16,224,128]{2,1,0:T(8,128)(2,1)}), bf16[16,224,128]{2,1,0:T(8,128)(2,1)S(1)}, u32[]{:S(2)}, u32[]{:S(2)}) async-start(bf16[16,224,128]{2,1,0:T(8,128)(2,1)} %get-tuple-element.29), calls=%async_computation.1 | async-start | bytes 1835008 | tf_op jit(solution)/shard_map/all_to_all | solution.py:361
  45.9 1.3 %collective-permute-start.2 = (bf16[96,256]{1,0:T(8,128)(2,1)S(1)}, bf16[96,256]{1,0:T(8,128)(2,1)S(1)}, u32[]{:S(2)}, u32[]{:S(2)}) collective-permute-start(bf16[96,256]{1,0:T(8,128)(2,1)S(1)} %get-tuple-element.30.own_ref), channel_id=1, source_target_pairs={{0,16},{16,0},{32,48},{48,32},{64,80},{80,64},{96,112},{112,96},{1... | collective-permute-start | bytes 147464 | tf_op jit(solution)/shard_map/ppermute | solution.py:466
  47.2 13.0 %collective-permute-start.5 = (bf16[192,256]{1,0:T(8,128)(2,1)S(1)}, bf16[192,256]{1,0:T(8,128)(2,1)S(1)}, u32[]{:S(2)}, u32[]{:S(2)}) collective-permute-start(bf16[192,256]{1,0:T(8,128)(2,1)S(1)} %chip_keys.1.refs_0_), channel_id=1, source_target_pairs={{0,96},{16,112},{32,64},{48,80},{64,32},{80,48},{96,0},{112,16},{1... | collective-permute-start | bytes 294920 | tf_op jit(solution)/shard_map/ppermute | solution.py:477
  50.3 9.9 %collective-permute-start.4 = (bf16[192,256]{1,0:T(8,128)(2,1)S(1)}, bf16[192,256]{1,0:T(8,128)(2,1)S(1)}, u32[]{:S(2)}, u32[]{:S(2)}) collective-permute-start(bf16[192,256]{1,0:T(8,128)(2,1)S(1)} %chip_keys.1.refs_0_), channel_id=1, source_target_pairs={{0,64},{16,80},{32,96},{48,112},{64,0},{80,16},{96,32},{112,48},{1... | collective-permute-start | bytes 294920 | tf_op jit(solution)/shard_map/ppermute | solution.py:477
  50.9 9.3 %collective-permute-start.3 = (bf16[192,256]{1,0:T(8,128)(2,1)S(1)}, bf16[192,256]{1,0:T(8,128)(2,1)S(1)}, u32[]{:S(2)}, u32[]{:S(2)}) collective-permute-start(bf16[192,256]{1,0:T(8,128)(2,1)S(1)} %chip_keys.1.refs_0_), channel_id=1, source_target_pairs={{0,32},{16,48},{32,0},{48,16},{64,96},{80,112},{96,64},{112,80},{1... | collective-permute-start | bytes 294920 | tf_op jit(solution)/shard_map/ppermute | solution.py:477
